TPU v7x, 512 devices: a whole 4x8x8 slice. The times are simulated.
512 devices in a mesh: pix: 32 (over y, x), chan: 16 (over z, core).
Axes of the slice: x: 4, y: 8, z: 8, core: 2. Of those that a mesh axis runs over, the one named last changes fastest.
Arguments:
- counts: float32 [131072, 2048], P('pix', 'chan'), may hold values from 0.1 to 200, as said below
- offset: float32 [2048], P('chan'), may hold values from -0.5 to 0.5
- loading: float32 [2048, 128], P('chan'), may hold values from -0.125 to 0.125
Outputs:
- grad_loading: float32 [2048, 128], P('chan')
- grad_offset: float32 [2048], P('chan')
Inputs may be any that keep to these rules, and one draw needn't show every extreme that they name: counts are positive intensities.
All inputs are finite; a program needn't handle non-finite values.
Results may differ from a plain program's by a relative error of at most 0.00024.
Values sent between devices are 32-bit elements; how exact they have to be, the bound alone decides.
No kernel may reach another device: no remote copies, remote signals or barrier semaphores. Data moves between devices by JAX's collectives and lax.ppermute only.
A program may use at most 64 MiB of HBM per device.

v0:
```python
import jax
import jax.numpy as jnp
from jax import lax
from jax.sharding import PartitionSpec as P

CHANNELS = 2048


def mult(left, right):
    return jnp.dot(left, right, preferred_element_type=jnp.float32, precision=lax.Precision.HIGHEST)


def on_device(counts, offset, loading):
    logs = jnp.log(counts)
    geo = lax.psum(jnp.sum(logs, axis=1), "chan") / CHANNELS
    centred = logs - geo[:, None] - offset[None, :]
    scores = lax.psum(mult(centred, loading), "chan")
    err = mult(scores, loading.T) - centred
    back = lax.psum(mult(err, loading), "chan")
    load_term = mult(centred.T, back) + mult(err.T, scores)
    offset_term = -jnp.sum(mult(back, loading.T) - err, axis=0)
    load_sum, offset_sum = lax.psum((load_term, offset_term), "pix")
    total = counts.shape[0] * lax.axis_size("pix")
    return (load_sum / total, offset_sum / total)


def solution(mesh):
    in_specs = (P("pix", "chan"), P("chan"), P("chan", None))
    out_specs = (P("chan", None), P("chan"))
    return jax.shard_map(
        on_device, mesh=mesh, in_specs=in_specs, out_specs=out_specs, check_vma=False
    )
```

profile of v0, /device:TPU:8, one launch (start us, length us, event | category | flops | bytes accessed | tf_op | source)
XLA Modules:
  0.0 551.5 jit_solution(16730761471782123763)
XLA Ops:
  7.2 0.0 copy-start
  7.2 0.0 copy-start.1
  7.2 0.0 copy-start.3
  7.2 0.0 all-reduce.4.cloned.1.call-start
  7.2 2.4 log_reduce_fusion
  9.6 54.0 %psum.35 = f32[4096]{0:T(1024)S(1)} all-reduce(f32[4096]{0:T(1024)S(1)} %log_reduce_fusion), channel_id=1, replica_groups=mesh['pix'=32,'chan'=16] {'chan'}, use_global_device_ids=true, to_apply=%region_1.0 | all-reduce | flops 4096 | bytes 32768 | tf_op jit(solution)/shard_map/psum | solution.py:15
  63.7 3.3 fusion.2
  66.9 0.0 all-reduce.4.cloned.1.call-update
  67.0 0.0 all-reduce.6.cloned.1.call-start
  67.0 117.6 %all-reduce.4.cloned.1.call-done = f32[4096,128]{1,0:T(8,128)} async-done(((f32[4096,128]{1,0:T(8,128)}), f32[4096,128]{1,0:T(8,128)}) %all-reduce.4.cloned.1.call-update) | async-done | bytes 2097168 | tf_op jit(solution)/shard_map/psum | solution.py:17
  184.6 3.6 convolution_subtract_fusion.1
  188.2 1.3 copy-done.2
  189.5 3.1 fusion.8
  192.6 0.0 all-reduce.6.cloned.1.call-update
  192.6 0.2 all-reduce.8.cloned.1.call-start
  192.9 5.7 %fusion.9 = f32[128,128]{1,0:T(8,128)S(1)} fusion(f32[4096,128]{1,0:T(8,128)} %copy-done.2, f32[4096,128]{1,0:T(8,128)} %all-reduce.4.cloned.1.call-done), kind=kOutput, calls=%fused_computation.16 | convolution fusion | flops 805306368 | bytes 4259840 | tf_op jit(solution)/shard_map/dot_general | solution.py:10
  198.5 115.0 %all-reduce.6.cloned.1.call-done = f32[4096,128]{1,0:T(8,128)} async-done(((f32[4096,128]{1,0:T(8,128)}), f32[4096,128]{1,0:T(8,128)}) %all-reduce.6.cloned.1.call-update) | async-done | bytes 2097168 | tf_op jit(solution)/shard_map/psum | solution.py:19
  313.5 4.0 fusion
  317.6 68.5 %psum.39 = f32[128]{0:T(128)S(1)} all-reduce(f32[128]{0:T(128)S(1)} %neg.3), channel_id=1, replica_groups=mesh['pix'=32,'chan'=16] {'pix'}, use_global_device_ids=true, to_apply=%region_6.0 | all-reduce | flops 128 | bytes 1024 | tf_op jit(solution)/shard_map/psum | solution.py:22
  386.1 6.4 %fusion.3 = f32[128,128]{1,0:T(8,128)} fusion(f32[128,128]{1,0:T(8,128)S(1)} %fusion.9, f32[4096,128]{1,0:T(8,128)} %all-reduce.6.cloned.1.call-done, f32[4096,128]{1,0:T(8,128)S(1)} %copy-done.1, f32[128]{0:T(128)S(1)} %copy-done.3, f32[4096]{0:T(1024)S(1)} %broadcast_multiply_fusion.1), kind=kOutput, calls=%fused_computation.7 | convolution fusion | flops 806371328 | bytes 4342272 | tf_op jit(solution)/shard_map/dot_general | solution.py:10
  392.5 0.0 all-reduce.8.cloned.1.call-update
  392.5 0.5 broadcast_multiply_fusion.2
  393.1 150.4 %all-reduce.8.cloned.1.call-done = f32[128,128]{1,0:T(8,128)} async-done(((f32[128,128]{1,0:T(8,128)}), f32[128,128]{1,0:T(8,128)}) %all-reduce.8.cloned.1.call-update) | async-done | bytes 65552 | tf_op jit(solution)/shard_map/psum | solution.py:22
  543.5 1.5 broadcast_multiply_fusion
  (6 shorter events, 0.0 us)
Async XLA Ops:
  7.2 56.5 %copy-start = (f32[128,128]{1,0:T(8,128)S(1)}, f32[128,128]{1,0:T(8,128)}, u32[]{:S(2)}) copy-start(f32[128,128]{1,0:T(8,128)} %param.5) | copy-start | bytes 196612
  7.2 56.5 %copy-start.1 = (f32[4096,128]{1,0:T(8,128)S(1)}, f32[4096,128]{1,0:T(8,128)}, u32[]{:S(2)}) copy-start(f32[4096,128]{1,0:T(8,128)} %param.3) | copy-start | bytes 6291460
  7.2 56.5 %copy-start.3 = (f32[128]{0:T(128)S(1)}, f32[128]{0:T(128)}, u32[]{:S(2)}) copy-start(f32[128]{0:T(128)} %param.4) | copy-start | bytes 1540
  7.2 177.4 %all-reduce.4.cloned.1.call-start = ((), (), s32[]{:S(2)}) async-start(), calls=%async_computation | async-start | bytes 4194304 | tf_op jit(solution)/shard_map/psum | solution.py:17
  67.0 246.6 %all-reduce.6.cloned.1.call-start = ((), (), s32[]{:S(2)}) async-start(), calls=%async_computation.1 | async-start | bytes 4194304 | tf_op jit(solution)/shard_map/psum | solution.py:19
  188.2 1.3 copy-start.2
  192.6 350.9 %all-reduce.8.cloned.1.call-start = ((), (), s32[]{:S(2)}) async-start(), calls=%async_computation.2 | async-start | bytes 131072 | tf_op jit(solution)/shard_map/psum | solution.py:22
Sparse Core Ops, SparseCore 0:
  67.1 117.4 all-reduce.3
  192.8 120.7 all-reduce.5
  392.7 150.7 all-reduce.7
where the time goes:
time: 552 us
  waiting for transfers between devices  383 us (69%)
  blocking collectives  123 us (22%)
  matrix products  26.1 us (5%)
  between operations  13.8 us (2%)
    psum x1, waiting for transfers between devices, on_device(): load_sum, offset_sum = lax.psum((load_term, offset_term), 'pix')  150 us
    psum x1, waiting for transfers between devices, on_device(): scores = lax.psum(mult(centred, loading), 'chan')  118 us
    psum x1, waiting for transfers between devices, on_device(): back = lax.psum(mult(err, loading), 'chan')  115 us
    psum x1, blocking collectives, on_device(): load_sum, offset_sum = lax.psum((load_term, offset_term), 'pix')  68.5 us
    psum x1, blocking collectives, on_device(): geo = lax.psum(jnp.sum(logs, axis=1), 'chan') / CHANNELS  54 us
    dot_general x6, matrix products, mult(): jnp.dot(left, right, preferred_element_type=jnp.float32, precision=lax.Pr...  26.1 us
  transfers between devices with their start and end apart: 3, of which 3 were waited for; matrix products, arithmetic and copies ran while one was open for 1% of the time, Pallas kernels for 0%

commit v1 on v0

v1 whole, which is shorter than its diff:
```python
import functools

import jax
import jax.numpy as jnp
from jax import lax
from jax.experimental import pallas as pl
from jax.experimental.pallas import tpu as pltpu
from jax.sharding import Mesh
from jax.sharding import PartitionSpec as P

F32 = jnp.float32
WIDE = ("y", "x")
DEEP = ("z", "c")
LIMIT = 48 * 1024 * 1024


def mult(left, right, contract=((1,), (0,))):
    return lax.dot_general(
        left, right, (contract, ((), ())),
        preferred_element_type=F32, precision=lax.Precision.HIGHEST,
    )


def whole(shape):
    return jax.ShapeDtypeStruct(shape, F32)


def call(body, out_shape, *args):
    return pl.pallas_call(
        body,
        out_shape=out_shape,
        compiler_params=pltpu.CompilerParams(vmem_limit_bytes=LIMIT),
    )(*args)


def send_body(which_ref, counts_ref, loading_ref, offset_ref, out_ref):
    half, comps = counts_ref.shape[0], loading_ref.shape[0]
    out_ref[0:half, :] = jnp.log(counts_ref[...])
    out_ref[half : half + comps, :] = loading_ref[...]
    out_ref[half + comps : half + comps + 8, :] = jnp.broadcast_to(offset_ref[...], (8, comps))


def keep_body(which_ref, counts_ref, out_ref):
    out_ref[...] = jnp.log(counts_ref[...])


def half_spec(half, width):
    return pl.BlockSpec((half, width), lambda i, which: (which[0], 0))


def on_half(body, which, counts, others, rows):
    half, width = counts.shape[0] // 2, counts.shape[1]
    specs = [half_spec(half, width)]
    specs += [pl.BlockSpec(a.shape, lambda i, which: (0, 0)) for a in others]
    return pl.pallas_call(
        body,
        out_shape=whole((rows, width)),
        grid_spec=pltpu.PrefetchScalarGridSpec(
            num_scalar_prefetch=1,
            grid=(1,),
            in_specs=specs,
            out_specs=pl.BlockSpec((rows, width), lambda i, which: (0, 0)),
        ),
        compiler_params=pltpu.CompilerParams(vmem_limit_bytes=LIMIT),
    )(which, counts, *others)


def encode_body(parts, mine_ref, other_ref, loading_ref, offset_ref, out_ref):
    half, comps = mine_ref.shape
    rows, share = half // parts, comps // parts
    mine = loading_ref[...]
    other = other_ref[half : half + comps, :]
    bar_mine = jnp.sum(mine, axis=0, keepdims=True) / comps
    bar_other = jnp.sum(other, axis=0, keepdims=True) / comps
    mine_c, other_c = mine - bar_mine, other - bar_other
    shift = mult(jnp.broadcast_to(offset_ref[...], (8, comps)), mine)
    shift += mult(other_ref[half + comps : half + comps + 8, :], other)
    gram = mult(mine, mine, ((0,), (0,))) + mult(other, other, ((0,), (0,)))
    ones = jnp.ones((8, comps), F32)
    for j in range(parts):
        a = mine_ref[j * rows : (j + 1) * rows, :]
        b = other_ref[j * rows : (j + 1) * rows, :]
        out_ref[j, 0:rows, :] = mult(a, mine_c) + mult(b, other_c)
        for h in range(rows // comps):
            sums = mult(ones, a[h * comps : (h + 1) * comps, :], ((1,), (1,)))
            out_ref[j, rows + h : rows + h + 1, :] = sums[0:1, :]
            sums = mult(ones, b[h * comps : (h + 1) * comps, :], ((1,), (1,)))
            out_ref[j, rows + 2 + h : rows + 3 + h, :] = sums[0:1, :]
        out_ref[j, rows + 4 : rows + 5, :] = bar_mine
        out_ref[j, rows + 5 : rows + 6, :] = bar_other
        out_ref[j, rows + 6 : rows + 7, :] = shift[0:1, :]
        out_ref[j, rows + 7 : rows + 8, :] = jnp.zeros((1, comps), F32)
        out_ref[j, rows + 8 : rows + 8 + share, :] = gram[j * share : (j + 1) * share, :]


def finish_body(channels, in_ref, out_ref):
    parts, height, comps = in_ref.shape
    share = comps // parts
    rows = height - 8 - share
    bars = jnp.concatenate([in_ref[j, rows + 4 : rows + 6, :] for j in range(parts)], axis=0)
    shift = in_ref[0, rows + 6 : rows + 7, :]
    for j in range(1, parts):
        shift += in_ref[j, rows + 6 : rows + 7, :]
    for h in range(rows // comps):
        sums = jnp.concatenate(
            [
                in_ref[j, rows + 2 * k + h : rows + 2 * k + h + 1, :]
                for j in range(parts)
                for k in range(2)
            ],
            axis=0,
        )
        geo = jnp.sum(sums, axis=0, keepdims=True) / channels
        apart = sums - comps * geo
        at = h * comps
        total = mult(apart, bars, ((0,), (0,))) - shift
        for j in range(parts):
            total += in_ref[j, at : at + comps, :]
        for j in range(parts):
            out_ref[j, at : at + comps, :] = total
            out_ref[j, rows + h : rows + h + 1, :] = geo
    gram = in_ref[0, rows + 8 : rows + 8 + share, :]
    for j in range(1, parts):
        gram += in_ref[j, rows + 8 : rows + 8 + share, :]
    for j in range(parts):
        out_ref[j, rows + 2 : rows + 8, :] = jnp.zeros((6, comps), F32)
        out_ref[j, rows + 8 : rows + 8 + share, :] = gram


def grad_body(in_ref, mine_ref, other_ref, loading_ref, offset_ref, mine_out, other_out):
    parts, height, comps = in_ref.shape
    share = comps // parts
    rows = height - 8 - share
    half = parts * rows
    gram = jnp.concatenate([in_ref[j, rows + 8 : rows + 8 + share, :] for j in range(parts)], axis=0)
    row = lax.broadcasted_iota(jnp.int32, (comps, comps), 0)
    col = lax.broadcasted_iota(jnp.int32, (comps, comps), 1)
    hat = gram - jnp.where(row == col, 2.0, 0.0).astype(F32)
    mine_l = loading_ref[...]
    other_l = other_ref[half : half + comps, :]
    mine_off = offset_ref[...]
    other_off = other_ref[half + comps : half + comps + 1, :]
    pick = lax.broadcasted_iota(jnp.int32, (8, comps), 0)
    zero = jnp.zeros((comps, comps), F32)
    w_mine, w_other, square = zero, zero, zero
    s_sum = jnp.zeros((1, comps), F32)
    c_mine, c_other = s_sum, s_sum
    for j in range(parts):
        geos = in_ref[j, rows : rows + 8, :]
        for h in range(rows // comps):
            at = j * rows + h * comps
            s = in_ref[j, h * comps : (h + 1) * comps, :]
            geo = mult(geos, jnp.where(pick == h, 1.0, 0.0).astype(F32), ((0,), (0,)))
            a = mine_ref[at : at + comps, :] - geo - mine_off
            b = other_ref[at : at + comps, :] - geo - other_off
            turned = s.T
            w_mine += mult(turned, a)
            w_other += mult(turned, b)
            square += mult(turned, s)
            s_sum += jnp.sum(s, axis=0, keepdims=True)
            c_mine += jnp.sum(a, axis=0, keepdims=True)
            c_other += jnp.sum(b, axis=0, keepdims=True)
    s_hat = mult(jnp.broadcast_to(s_sum, (8, comps)), hat)
    for w, load, c, out in ((w_mine, mine_l, c_mine, mine_out), (w_other, other_l, c_other, other_out)):
        out[0:comps, :] = mult(w.T, hat) + mult(load, square)
        out[comps : comps + 8, :] = -(mult(s_hat, load, ((1,), (1,))) + c)


def add_body(a_ref, b_ref, out_ref):
    total = a_ref[...] + b_ref[...]
    for j in range(out_ref.shape[0]):
        out_ref[j] = total


def gather_body(in_ref, out_ref):
    total = jnp.sum(in_ref[...], axis=0)
    for j in range(out_ref.shape[0]):
        out_ref[j] = total


def last_body(pixels, in_ref, load_ref, off_ref):
    comps = load_ref.shape[0]
    total = jnp.sum(in_ref[...], axis=0) / pixels
    load_ref[...] = total[0:comps, :]
    off_ref[...] = total[comps : comps + 1, :]


def on_device(counts, offset, loading):
    pixels = counts.shape[0] * lax.axis_size(WIDE)
    comps = loading.shape[1]
    parts = lax.axis_size("z")
    channels = counts.shape[1] * parts * 2
    half = counts.shape[0] // 2
    rows = half // parts
    height = rows + 8 + comps // parts
    core = lax.axis_index("c").astype(jnp.int32)
    offset = offset.reshape(1, comps)

    sent = on_half(send_body, (1 - core).reshape(1), counts, (loading, offset), half + comps + 8)
    other = lax.ppermute(sent, "c", [(0, 1), (1, 0)])
    mine = on_half(keep_body, core.reshape(1), counts, (), half)
    partial = call(
        functools.partial(encode_body, parts), whole((parts, height, comps)), mine, other, loading, offset
    )
    gathered = lax.all_to_all(partial, "z", 0, 0)
    copies = call(functools.partial(finish_body, channels), whole((parts, height, comps)), gathered)
    scores = lax.all_to_all(copies, "z", 0, 0)
    shape = whole((comps + 8, comps))
    grad_mine, grad_other = call(grad_body, (shape, shape), scores, mine, other, loading, offset)
    arrived = lax.ppermute(grad_other, "c", [(0, 1), (1, 0)])
    nx, ny = lax.axis_size("x"), lax.axis_size("y")
    total = call(add_body, whole((nx, comps + 8, comps)), grad_mine, arrived)
    total = lax.all_to_all(total, "x", 0, 0)
    total = call(gather_body, whole((ny, comps + 8, comps)), total)
    total = lax.all_to_all(total, "y", 0, 0)
    grad, grad_offset = call(
        functools.partial(last_body, pixels), (whole((comps, comps)), whole((1, comps))), total
    )
    return grad, grad_offset.reshape(comps)


def solution(mesh):
    wide, deep = mesh.devices.shape
    split = Mesh(mesh.devices.reshape(wide // 4, 4, deep // 2, 2), WIDE + DEEP)
    return jax.shard_map(
        on_device,
        mesh=split,
        in_specs=(P(WIDE, DEEP), P(DEEP), P(DEEP, None)),
        out_specs=(P(DEEP, None), P(DEEP)),
        check_vma=False,
    )
```

time: 552 us -> 133 us (0.24)
  the two profiles are of different devices: /device:TPU:8 before, /device:TPU:2 now
where the time goes in v1:
time: 133 us
  blocking collectives  108 us (81%)
  Pallas kernels  12.9 us (10%)
  starting transfers between devices  3.97 us (3%)
  waiting for transfers between devices  3.78 us (3%)
  local copies, waits for them, and re-layouts  3.09 us (2%)
    all_to_all x1, blocking collectives, on_device(): gathered = lax.all_to_all(partial, 'z', 0, 0)  41.3 us
    all_to_all x1, blocking collectives, on_device(): scores = lax.all_to_all(copies, 'z', 0, 0)  32.5 us
    all_to_all x1, blocking collectives, on_device(): total = lax.all_to_all(total, 'y', 0, 0)  24.3 us
    pallas_call x6, Pallas kernels, call(): pl.pallas_call(body, out_shape=out_shape, compiler_params=pltpu.CompilerP...  12.6 us
    all_to_all x1, blocking collectives, on_device(): total = lax.all_to_all(total, 'x', 0, 0)  10.3 us
    unnamed x12, local copies, waits for them, and re-layouts  3.09 us
  transfers between devices with their start and end apart: 2, of which 2 were waited for; matrix products, arithmetic and copies ran while one was open for 0% of the time, Pallas kernels for 0%

profile of v1, /device:TPU:2, one launch (start us, length us, event | category | flops | bytes accessed | tf_op | source)
XLA Modules:
  0.0 132.9 jit_solution(5118604759452399381)
XLA Ops:
  0.6 0.0 copy-start
  0.6 1.6 %copy-done = f32[4096,128]{1,0:T(8,128)S(1)} copy-done((f32[4096,128]{1,0:T(8,128)S(1)}, f32[4096,128]{1,0:T(8,128)}, u32[]{:S(2)}) %copy-start) | copy-done | bytes 2097176
  2.2 0.0 copy-start.2
  2.2 0.8 copy-done.2
  3.1 0.7 copy-done.4
  3.7 0.1 shard_map.51
  3.9 2.1 %collective-permute-start = (f32[2184,128]{1,0:T(8,128)S(1)}, f32[2184,128]{1,0:T(8,128)S(1)}, u32[]{:S(2)}, u32[]{:S(2)}) collective-permute-start(f32[2184,128]{1,0:T(8,128)S(1)} %shard_map.51), channel_id=1, source_target_pairs={{0,1},{1,0},{2,3},{3,2},{4,5},{5,4},{6,7},{7,6},{8,9},{9,8},{10,11... | collective-permute-start | bytes 3354632 | tf_op jit(solution)/shard_map/ppermute | solution.py:200
  5.9 0.0 copy-done.1
  5.9 0.1 shard_map.50.mine_ref
  6.1 2.6 %collective-permute-done.other_ref = f32[2184,128]{1,0:T(8,128)S(1)} collective-permute-done((f32[2184,128]{1,0:T(8,128)S(1)}, f32[2184,128]{1,0:T(8,128)S(1)}, u32[]{:S(2)}, u32[]{:S(2)}) %collective-permute-start) | collective-permute-done | bytes 1118240 | tf_op jit(solution)/shard_map/ppermute | solution.py:200
  8.7 5.2 %shard_map.52 = f32[8,280,128]{2,1,0:T(8,128)S(1)} custom-call(f32[2048,128]{1,0:T(8,128)S(1)} %shard_map.50.mine_ref, f32[2184,128]{1,0:T(8,128)S(1)} %collective-permute-done.other_ref, f32[128,128]{1,0:T(8,128)S(1)} %copy-done.2, f32[1,128]{1,0:T(1,128)S(1)} %bitcast.5), custom_call_target="tpu_custom_call" | custom-call | tf_op jit(solution)/shard_map/pallas_call | solution.py:29
  13.8 41.3 %all_to_all.20.in_ref = f32[8,280,128]{2,1,0:T(8,128)S(1)} all-to-all(f32[8,280,128]{2,1,0:T(8,128)S(1)} %shard_map.52), channel_id=1, replica_groups=mesh['y'=8,'x'=4,'z'=8,'c'=2] {'z'}, dimensions={0} | all-to-all | bytes 2293760 | tf_op jit(solution)/shard_map/all_to_all | solution.py:205
  55.1 0.4 shard_map.53
  55.5 0.0 copy-start.3
  55.5 0.0 copy-start.5
  55.5 32.5 %all_to_all.21.in_ref = f32[8,280,128]{2,1,0:T(8,128)S(1)} all-to-all(f32[8,280,128]{2,1,0:T(8,128)S(1)} %shard_map.53), channel_id=1, replica_groups=mesh['y'=8,'x'=4,'z'=8,'c'=2] {'z'}, dimensions={0} | all-to-all | bytes 2293760 | tf_op jit(solution)/shard_map/all_to_all | solution.py:207
  88.0 0.0 copy-done.3
  88.0 0.0 copy-done.5
  88.0 6.4 %shard_map.54 = (f32[136,128]{1,0:T(8,128)S(1)}, f32[136,128]{1,0:T(8,128)S(1)}) custom-call(f32[8,280,128]{2,1,0:T(8,128)S(1)} %all_to_all.21.in_ref, f32[2048,128]{1,0:T(8,128)S(1)} %shard_map.50.mine_ref, f32[2184,128]{1,0:T(8,128)S(1)} %collective-permute-done.other_ref, f32[128,128]{1,0:T(8,128)S(1)} %copy-done.3, f32[1,128]{1,0:T(1,128)S(1)} %bitcast.6), custom_call_target="tpu_custom_call" | custom-call | tf_op jit(solution)/shard_map/pallas_call | solution.py:29
  94.4 1.9 %collective-permute-start.1 = (f32[136,128]{1,0:T(8,128)S(1)}, f32[136,128]{1,0:T(8,128)S(1)}, u32[]{:S(2)}, u32[]{:S(2)}) collective-permute-start(f32[136,128]{1,0:T(8,128)S(1)} %get-tuple-element.7), channel_id=1, source_target_pairs={{0,1},{1,0},{2,3},{3,2},{4,5},{5,4},{6,7},{7,6},{8,9},{9,8},{10,11... | collective-permute-start | bytes 208904 | tf_op jit(solution)/shard_map/ppermute | solution.py:210
  96.3 1.2 collective-permute-done.1.b_ref
  97.5 10.3 %all_to_all.22.in_ref = f32[4,136,128]{2,1,0:T(8,128)S(1)} all-to-all(f32[4,136,128]{2,1,0:T(8,128)S(1)} %shard_map.55), channel_id=1, replica_groups=mesh['y'=8,'x'=4,'z'=8,'c'=2] {'x'}, dimensions={0} | all-to-all | bytes 557056 | tf_op jit(solution)/shard_map/all_to_all | solution.py:213
  107.9 24.3 %all_to_all.23.in_ref = f32[8,136,128]{2,1,0:T(8,128)S(1)} all-to-all(f32[8,136,128]{2,1,0:T(8,128)S(1)} %shard_map.56), channel_id=1, replica_groups=mesh['y'=8,'x'=4,'z'=8,'c'=2] {'y'}, dimensions={0} | all-to-all | bytes 1114112 | tf_op jit(solution)/shard_map/all_to_all | solution.py:215
  132.2 0.7 shard_map.57
  (4 shorter events, 0.1 us)
Async XLA Ops:
  0.6 1.6 %copy-start = (f32[4096,128]{1,0:T(8,128)S(1)}, f32[4096,128]{1,0:T(8,128)}, u32[]{:S(2)}) copy-start(f32[4096,128]{1,0:T(8,128)} %counts_ref.3) | copy-start | bytes 6291460
  2.2 0.8 copy-start.2
  3.1 0.7 copy-start.4
  3.7 2.2 %copy-start.1 = (f32[4096,128]{1,0:T(8,128)S(1)}, f32[4096,128]{1,0:T(8,128)}, u32[]{:S(2)}) copy-start(f32[4096,128]{1,0:T(8,128)} %counts_ref.3) | copy-start | bytes 6291460
  3.9 4.8 %collective-permute-start = (f32[2184,128]{1,0:T(8,128)S(1)}, f32[2184,128]{1,0:T(8,128)S(1)}, u32[]{:S(2)}, u32[]{:S(2)}) collective-permute-start(f32[2184,128]{1,0:T(8,128)S(1)} %shard_map.51), channel_id=1, source_target_pairs={{0,1},{1,0},{2,3},{3,2},{4,5},{5,4},{6,7},{7,6},{8,9},{9,8},{10,11... | collective-permute-start | bytes 3354632 | tf_op jit(solution)/shard_map/ppermute | solution.py:200
  55.5 32.5 %copy-start.3 = (f32[128,128]{1,0:T(8,128)S(1)}, f32[128,128]{1,0:T(8,128)}, u32[]{:S(2)}) copy-start(f32[128,128]{1,0:T(8,128)} %loading_ref.5) | copy-start | bytes 196612
  55.5 32.5 %copy-start.5 = (f32[128]{0:T(128)S(1)}, f32[128]{0:T(128)}, u32[]{:S(2)}) copy-start(f32[128]{0:T(128)} %param.4) | copy-start | bytes 1540
  94.4 3.2 %collective-permute-start.1 = (f32[136,128]{1,0:T(8,128)S(1)}, f32[136,128]{1,0:T(8,128)S(1)}, u32[]{:S(2)}, u32[]{:S(2)}) collective-permute-start(f32[136,128]{1,0:T(8,128)S(1)} %get-tuple-element.7), channel_id=1, source_target_pairs={{0,1},{1,0},{2,3},{3,2},{4,5},{5,4},{6,7},{7,6},{8,9},{9,8},{10,11... | collective-permute-start | bytes 208904 | tf_op jit(solution)/shard_map/ppermute | solution.py:210

commit v2 on v0

v2 whole, which is shorter than its diff:
```python
import functools

import jax
import jax.numpy as jnp
from jax import lax
from jax.experimental import pallas as pl
from jax.experimental.pallas import tpu as pltpu
from jax.sharding import Mesh
from jax.sharding import PartitionSpec as P

F32 = jnp.float32
AXES = ("y", "x", "zh", "zl", "c")
WIDE = ("y", "x")
DEEP = ("zh", "zl", "c")
LIMIT = 48 * 1024 * 1024


def mult(left, right, contract=((1,), (0,))):
    return lax.dot_general(
        left, right, (contract, ((), ())),
        preferred_element_type=F32, precision=lax.Precision.HIGHEST,
    )


def whole(*shape):
    return jax.ShapeDtypeStruct(shape, F32)


def call(body, out_shape, *args):
    return pl.pallas_call(
        body,
        out_shape=out_shape,
        compiler_params=pltpu.CompilerParams(vmem_limit_bytes=LIMIT),
    )(*args)


def tail(loading_ref, offset_ref, out_ref):
    comps = loading_ref.shape[0]
    rows = out_ref.shape[0] - comps - 8
    out_ref[rows : rows + comps, :] = loading_ref[...]
    out_ref[rows + comps : rows + comps + 8, :] = jnp.broadcast_to(offset_ref[...], (8, comps))
    return rows


def split_body(which, keep_in, core_in, near_in, far_in, loading_ref, offset_ref, keep, core, near, far):
    rows = tail(loading_ref, offset_ref, near)
    near[0:rows, :] = jnp.log(near_in[...])
    tail(loading_ref, offset_ref, far)
    far[0:rows, :] = jnp.log(far_in[...])
    core[...] = jnp.log(core_in[...])
    keep[...] = jnp.log(keep_in[...])


def split(which, counts, loading, offset):
    rows, width = counts.shape[0] // 4, counts.shape[1]

    def block(k):
        return pl.BlockSpec((rows, width), lambda i, which: (which[k], 0))

    def full(shape):
        return pl.BlockSpec(shape, lambda i, which: (0, 0))

    more = rows + loading.shape[0] + 8
    heights = (rows, rows, more, more)
    return pl.pallas_call(
        split_body,
        out_shape=tuple(whole(h, width) for h in heights),
        grid_spec=pltpu.PrefetchScalarGridSpec(
            num_scalar_prefetch=1,
            grid=(1,),
            in_specs=[block(k) for k in range(4)] + [full(loading.shape), full(offset.shape)],
            out_specs=tuple(full((h, width)) for h in heights),
        ),
        compiler_params=pltpu.CompilerParams(vmem_limit_bytes=LIMIT),
    )(which, counts, counts, counts, counts, loading, offset)


def log_sums(logs, ones, comps):
    return [
        mult(ones, logs[h * comps : (h + 1) * comps, :], ((1,), (1,)))[0:1, :]
        for h in range(logs.shape[0] // comps)
    ]


def encode_body(parts, keep, core, near, far, loading_ref, out_ref):
    total, comps = keep.shape
    rows, share = total // parts, comps // parts
    loads = [loading_ref[...], far[total : total + comps, :], near[total : total + comps, :]]
    bars = [jnp.sum(load, axis=0, keepdims=True) / comps for load in loads]
    bare = [load - bar for load, bar in zip(loads, bars)]
    pair = jnp.concatenate(bare[0:2], axis=0)
    gram = mult(loads[0], loads[0], ((0,), (0,)))
    for load in loads[1:]:
        gram += mult(load, load, ((0,), (0,)))
    shift = mult(far[total + comps : total + comps + 8, :], loads[1])
    shift += mult(near[total + comps : total + comps + 8, :], loads[2])
    ones = jnp.ones((8, comps), F32)
    for j in range(parts):
        logs = [source[j * rows : (j + 1) * rows, :] for source in (keep, core, near)]
        both = jnp.concatenate(logs[0:2], axis=1)
        out_ref[j, 0:rows, :] = mult(both, pair) + mult(logs[2], bare[2])
        for k, part in enumerate(logs):
            for h, sums in enumerate(log_sums(part, ones, comps)):
                at = rows + 4 * h + k
                out_ref[j, at : at + 1, :] = sums
            out_ref[j, rows + 8 + k : rows + 9 + k, :] = bars[k]
        out_ref[j, rows + 12 : rows + 13, :] = shift[0:1, :]
        out_ref[j, rows + 16 : rows + 16 + share, :] = gram[j * share : (j + 1) * share, :]


def encode_last_body(in_ref, more, loading_ref, offset_ref, out_ref):
    parts, height, comps = in_ref.shape
    share = comps // parts
    rows = height - 16 - share
    total = parts * rows
    load = more[total : total + comps, :]
    bar = jnp.sum(load, axis=0, keepdims=True) / comps
    bare = load - bar
    gram = mult(load, load, ((0,), (0,)))
    shift = mult(more[total + comps : total + comps + 8, :], load)
    shift += mult(jnp.broadcast_to(offset_ref[...], (8, comps)), loading_ref[...])
    ones = jnp.ones((8, comps), F32)
    blank = jnp.zeros((3, comps), F32)
    for j in range(parts):
        logs = more[j * rows : (j + 1) * rows, :]
        out_ref[j, 0:rows, :] = in_ref[j, 0:rows, :] + mult(logs, bare)
        for h, sums in enumerate(log_sums(logs, ones, comps)):
            at = rows + 4 * h
            out_ref[j, at : at + 3, :] = in_ref[j, at : at + 3, :]
            out_ref[j, at + 3 : at + 4, :] = sums
        out_ref[j, rows + 8 : rows + 11, :] = in_ref[j, rows + 8 : rows + 11, :]
        out_ref[j, rows + 11 : rows + 12, :] = bar
        out_ref[j, rows + 12 : rows + 13, :] = in_ref[j, rows + 12 : rows + 13, :] + shift[0:1, :]
        out_ref[j, rows + 13 : rows + 16, :] = blank
        at = rows + 16
        out_ref[j, at : at + share, :] = in_ref[j, at : at + share, :] + gram[j * share : (j + 1) * share, :]


def finish_body(channels, in_ref, out_ref):
    parts, height, comps = in_ref.shape
    share = comps // parts
    rows = height - 16 - share
    bars = jnp.concatenate([in_ref[j, rows + 8 : rows + 12, :] for j in range(parts)], axis=0)
    shift = in_ref[0, rows + 12 : rows + 13, :]
    for j in range(1, parts):
        shift += in_ref[j, rows + 12 : rows + 13, :]
    for h in range(rows // comps):
        sums = jnp.concatenate(
            [in_ref[j, rows + 4 * h : rows + 4 * h + 4, :] for j in range(parts)], axis=0
        )
        geo = jnp.sum(sums, axis=0, keepdims=True) / channels
        at = h * comps
        total = mult(sums - comps * geo, bars, ((0,), (0,))) - shift
        for j in range(parts):
            total += in_ref[j, at : at + comps, :]
        for j in range(parts):
            out_ref[j, at : at + comps, :] = total
            out_ref[j, rows + h : rows + h + 1, :] = geo
    gram = in_ref[0, rows + 16 : rows + 16 + share, :]
    for j in range(1, parts):
        gram += in_ref[j, rows + 16 : rows + 16 + share, :]
    for j in range(parts):
        out_ref[j, rows + 2 : rows + 8, :] = jnp.zeros((6, comps), F32)
        out_ref[j, rows + 8 : rows + 8 + share, :] = gram


def grad_body(in_ref, keep, core, near, far, more, loading_ref, offset_ref, mine_out, near_out):
    parts, height, comps = in_ref.shape
    share = comps // parts
    rows = height - 8 - share
    total = parts * rows
    gram = jnp.concatenate([in_ref[j, rows + 8 : rows + 8 + share, :] for j in range(parts)], axis=0)
    row = lax.broadcasted_iota(jnp.int32, (comps, comps), 0)
    col = lax.broadcasted_iota(jnp.int32, (comps, comps), 1)
    hat = gram - jnp.where(row == col, 2.0, 0.0).astype(F32)
    logs = (keep, core, near, more)
    loads = (loading_ref[...],) + tuple(a[total : total + comps, :] for a in (far, near, more))
    offs = (offset_ref[...],) + tuple(a[total + comps : total + comps + 1, :] for a in (far, near, more))
    pick = lax.broadcasted_iota(jnp.int32, (8, comps), 0)
    wide = jnp.zeros((comps, 5 * comps), F32)
    s_sum = jnp.zeros((1, comps), F32)
    c_sum = [s_sum] * 4
    for j in range(parts):
        geos = in_ref[j, rows : rows + 8, :]
        s = in_ref[j, 0:rows, :]
        s_sum += jnp.sum(s, axis=0, keepdims=True)
        geo = jnp.concatenate(
            [
                mult(geos, jnp.where(pick == h, 1.0, 0.0).astype(F32), ((0,), (0,)))
                for h in range(rows // comps)
            ],
            axis=0,
        )
        centred = [a[j * rows : (j + 1) * rows, :] - geo - off for a, off in zip(logs, offs)]
        c_sum = [c + jnp.sum(a, axis=0, keepdims=True) for c, a in zip(c_sum, centred)]
        wide += mult(s.T, jnp.concatenate(centred + [s], axis=1))
    square = wide[:, 4 * comps : 5 * comps]
    s_hat = mult(jnp.broadcast_to(s_sum, (8, comps)), hat)
    for k in range(4):
        out = (mine_out, near_out)[k // 2]
        w = wide[:, k * comps : (k + 1) * comps]
        out[k % 2, 0:comps, :] = mult(w.T, hat) + mult(loads[k], square)
        out[k % 2, comps : comps + 8, :] = -(mult(s_hat, loads[k], ((1,), (1,))) + c_sum[k])


def deal_body(which, a_ref, b_ref, out_ref):
    core = which[0]
    _, height, comps = a_ref.shape
    pieces = out_ref.shape[0] // 2
    share = comps // pieces
    sums = [a_ref[k] + b_ref[k] for k in range(2)]
    for p in range(pieces):
        for k in range(2):
            first, other = sums[k], sums[1 - k]
            for rows, at in ((slice(p * share, (p + 1) * share), 0), (slice(comps, comps + 8 - share), share)):
                piece = jnp.where(core == 0, first[rows, :], other[rows, :])
                out_ref[2 * p + k, at : at + piece.shape[0], :] = piece


def deal(which, a, b, devices):
    comps = a.shape[2]
    return pl.pallas_call(
        deal_body,
        out_shape=whole(devices, 8, comps),
        in_specs=[
            pl.BlockSpec(memory_space=pltpu.SMEM),
            pl.BlockSpec(memory_space=pltpu.VMEM),
            pl.BlockSpec(memory_space=pltpu.VMEM),
        ],
        compiler_params=pltpu.CompilerParams(vmem_limit_bytes=LIMIT),
    )(which, a, b)


def gather_body(pixels, in_ref, out_ref):
    total = jnp.sum(in_ref[...], axis=0) / pixels
    for j in range(out_ref.shape[0]):
        out_ref[j] = total


def last_body(in_ref, load_ref, off_ref):
    pieces = in_ref.shape[0]
    share = load_ref.shape[0] // pieces
    for p in range(pieces):
        load_ref[p * share : (p + 1) * share, :] = in_ref[p, 0:share, :]
    off_ref[...] = in_ref[0, share : share + 1, :]


def on_device(counts, offset, loading):
    pixels = counts.shape[0] * lax.axis_size(WIDE)
    comps = loading.shape[1]
    parts = lax.axis_size("zh")
    channels = counts.shape[1] * parts * 4
    rows = counts.shape[0] // 4 // parts
    share = comps // parts
    core = lax.axis_index("c").astype(jnp.int32)
    side = lax.axis_index("zl").astype(jnp.int32)
    which = jnp.stack(
        [2 * core + side, 2 * (1 - core) + side, 2 * core + 1 - side, 2 * (1 - core) + 1 - side]
    )
    offset = offset.reshape(1, comps)

    swap = [(0, 1), (1, 0)]
    z_size = 2 * parts
    near_pairs = []
    for z in range(z_size):
        for c in range(2):
            partner = (((z - c) % z_size ^ 1) + c) % z_size
            near_pairs.append((2 * z + c, 2 * partner + c))

    keep, core_out, near_out, far_out = split(which, counts, loading, offset)
    near = lax.ppermute(near_out, DEEP, near_pairs)
    far = lax.ppermute(far_out, "c", swap)
    more = lax.ppermute(far, DEEP, near_pairs)
    other = lax.ppermute(core_out, "c", swap)
    height = rows + 16 + share
    partial = call(
        functools.partial(encode_body, parts), whole(parts, height, comps), keep, other, near, far, loading
    )
    partial = call(encode_last_body, whole(parts, height, comps), partial, more, loading, offset)
    gathered = lax.all_to_all(partial, "zh", 0, 0)
    copies = call(functools.partial(finish_body, channels), whole(parts, height - 8, comps), gathered)
    scores = lax.all_to_all(copies, "zh", 0, 0)
    shape = whole(2, comps + 8, comps)
    grad_mine, grad_near = call(
        grad_body, (shape, shape), scores, keep, other, near, far, more, loading, offset
    )
    arrived = lax.ppermute(grad_near, DEEP, near_pairs)
    plane = lax.axis_size(WIDE)
    pieces = deal(core.reshape(1), grad_mine, arrived, 2 * plane)
    pieces = lax.all_to_all(pieces, WIDE + ("c",), 0, 0)
    pieces = call(functools.partial(gather_body, pixels), whole(plane, 8, comps), pieces)
    pieces = lax.all_to_all(pieces, WIDE, 0, 0)
    grad, grad_offset = call(last_body, (whole(comps, comps), whole(1, comps)), pieces)
    return grad, grad_offset.reshape(comps)


def solution(mesh):
    wide, deep = mesh.devices.shape
    split_mesh = Mesh(mesh.devices.reshape(wide // 4, 4, deep // 4, 2, 2), AXES)
    return jax.shard_map(
        on_device,
        mesh=split_mesh,
        in_specs=(P(WIDE, DEEP), P(DEEP), P(DEEP, None)),
        out_specs=(P(DEEP, None), P(DEEP)),
        check_vma=False,
    )
```

time: 552 us -> 126 us (0.23)
  the two profiles are of different devices: /device:TPU:8 before, /device:TPU:1 now
where the time goes in v2:
time: 126 us; the launch traced here: 125 us
  blocking collectives  75.6 us (60%)
  starting transfers between devices  26.6 us (21%)
  Pallas kernels  11.1 us (9%)
  waiting for transfers between devices  8.17 us (6%)
  local copies, waits for them, and re-layouts  3.09 us (2%)
    all_to_all x1, blocking collectives, on_device(): pieces = lax.all_to_all(pieces, WIDE + ('c',), 0, 0)  25.9 us
    all_to_all x1, blocking collectives, on_device(): gathered = lax.all_to_all(partial, 'zh', 0, 0)  19.8 us
    all_to_all x1, blocking collectives, on_device(): scores = lax.all_to_all(copies, 'zh', 0, 0)  17 us
    all_to_all x1, blocking collectives, on_device(): pieces = lax.all_to_all(pieces, WIDE, 0, 0)  12.9 us
    pallas_call x6, Pallas kernels, call(): pl.pallas_call(body, out_shape=out_shape, compiler_params=pltpu.CompilerP...  10.3 us
    ppermute x1, starting transfers between devices, on_device(): far = lax.ppermute(far_out, 'c', swap)  8.79 us
    ppermute x1, starting transfers between devices, on_device(): arrived = lax.ppermute(grad_near, DEEP, near_pairs)  8.71 us
    ppermute x1, starting transfers between devices, on_device(): near = lax.ppermute(near_out, DEEP, near_pairs)  5.29 us
  transfers between devices with their start and end apart: 5, of which 4 were waited for; matrix products, arithmetic and copies ran while one was open for 0% of the time, Pallas kernels for 3%

profile of v2, /device:TPU:1, one launch (start us, length us, event | category | flops | bytes accessed | tf_op | source)
XLA Modules:
  0.0 125.4 jit_solution(14455710417122955879)
XLA Ops:
  0.6 0.1 pad_add_fusion.which
  0.7 1.6 %copy-done = f32[4096,128]{1,0:T(8,128)S(1)} copy-done((f32[4096,128]{1,0:T(8,128)S(1)}, f32[4096,128]{1,0:T(8,128)}, u32[]{:S(2)}) %copy-start) | copy-done | bytes 2097176
  2.3 0.8 copy-done.1
  3.2 0.7 copy-done.2
  3.8 0.8 shard_map.50
  4.6 8.8 %collective-permute-start.2 = (f32[1160,128]{1,0:T(8,128)S(1)}, f32[1160,128]{1,0:T(8,128)S(1)}, u32[]{:S(2)}, u32[]{:S(2)}) collective-permute-start(f32[1160,128]{1,0:T(8,128)S(1)} %get-tuple-element.13), channel_id=1, source_target_pairs={{0,1},{1,0},{2,3},{3,2},{4,5},{5,4},{6,7},{7,6},{8,9},{9,8},{10,11... | collective-permute-start | bytes 1781768 | tf_op jit(solution)/shard_map/ppermute | solution.py:272
  13.4 5.3 %collective-permute-start.1 = (f32[1160,128]{1,0:T(8,128)S(1)}, f32[1160,128]{1,0:T(8,128)S(1)}, u32[]{:S(2)}, u32[]{:S(2)}) collective-permute-start(f32[1160,128]{1,0:T(8,128)S(1)} %get-tuple-element.12), channel_id=1, source_target_pairs={{0,2},{1,15},{2,0},{3,5},{4,6},{5,3},{6,4},{7,9},{8,10},{9,7},{10,... | collective-permute-start | bytes 1781768 | tf_op jit(solution)/shard_map/ppermute | solution.py:271
  18.7 1.9 %collective-permute-start.3 = (f32[1160,128]{1,0:T(8,128)S(1)}, f32[1160,128]{1,0:T(8,128)S(1)}, u32[]{:S(2)}, u32[]{:S(2)}) collective-permute-start(f32[1160,128]{1,0:T(8,128)S(1)} %collective-permute-done.2.far), channel_id=1, source_target_pairs={{0,2},{1,15},{2,0},{3,5},{4,6},{5,3},{6,4},{7,9},{8,10},{9,7},{10,... | collective-permute-start | bytes 1781768 | tf_op jit(solution)/shard_map/ppermute | solution.py:273
  20.7 1.9 %collective-permute-start = (f32[1024,128]{1,0:T(8,128)S(1)}, f32[1024,128]{1,0:T(8,128)S(1)}, u32[]{:S(2)}, u32[]{:S(2)}) collective-permute-start(f32[1024,128]{1,0:T(8,128)S(1)} %get-tuple-element.11), channel_id=1, source_target_pairs={{0,1},{1,0},{2,3},{3,2},{4,5},{5,4},{6,7},{7,6},{8,9},{9,8},{10,11... | collective-permute-start | bytes 1572872 | tf_op jit(solution)/shard_map/ppermute | solution.py:274
  22.6 1.9 %collective-permute-done.core = f32[1024,128]{1,0:T(8,128)S(1)} collective-permute-done((f32[1024,128]{1,0:T(8,128)S(1)}, f32[1024,128]{1,0:T(8,128)S(1)}, u32[]{:S(2)}, u32[]{:S(2)}) %collective-permute-start) | collective-permute-done | bytes 524320 | tf_op jit(solution)/shard_map/ppermute | solution.py:274
  24.5 1.6 %collective-permute-done.1.near = f32[1160,128]{1,0:T(8,128)S(1)} collective-permute-done((f32[1160,128]{1,0:T(8,128)S(1)}, f32[1160,128]{1,0:T(8,128)S(1)}, u32[]{:S(2)}, u32[]{:S(2)}) %collective-permute-start.1) | collective-permute-done | bytes 593952 | tf_op jit(solution)/shard_map/ppermute | solution.py:271
  26.0 4.1 %shard_map.51.in_ref = f32[4,304,128]{2,1,0:T(8,128)S(1)} custom-call(f32[1024,128]{1,0:T(8,128)S(1)} %get-tuple-element.10.keep, f32[1024,128]{1,0:T(8,128)S(1)} %collective-permute-done.core, f32[1160,128]{1,0:T(8,128)S(1)} %collective-permute-done.1.near, f32[1160,128]{1,0:T(8,128)S(1)} %collective-permute-done.2.far, f32[128,128]{1,0:T(8,128)S(1)} %copy-done.1), custom_call_target="tpu_custom_call" | custom-call | tf_op jit(solution)/shard_map/pallas_call | solution.py:30
  30.1 2.3 %collective-permute-done.3.more = f32[1160,128]{1,0:T(8,128)S(1)} collective-permute-done((f32[1160,128]{1,0:T(8,128)S(1)}, f32[1160,128]{1,0:T(8,128)S(1)}, u32[]{:S(2)}, u32[]{:S(2)}) %collective-permute-start.3) | collective-permute-done | bytes 593952 | tf_op jit(solution)/shard_map/ppermute | solution.py:273
  32.4 1.5 %shard_map.52 = f32[4,304,128]{2,1,0:T(8,128)S(1)} custom-call(f32[4,304,128]{2,1,0:T(8,128)S(1)} %shard_map.51.in_ref, f32[1160,128]{1,0:T(8,128)S(1)} %collective-permute-done.3.more, f32[128,128]{1,0:T(8,128)S(1)} %copy-done.1, f32[1,128]{1,0:T(1,128)S(1)} %bitcast.8), custom_call_target="tpu_custom_call" | custom-call | tf_op jit(solution)/shard_map/pallas_call | solution.py:30
  33.9 19.8 %all_to_all.20.in_ref = f32[4,304,128]{2,1,0:T(8,128)S(1)} all-to-all(f32[4,304,128]{2,1,0:T(8,128)S(1)} %shard_map.52), channel_id=1, replica_groups=mesh['y'=8,'x'=4,'zh'=4,'zl'=2,'c'=2] {'zh'}, dimensions={0} | all-to-all | bytes 1245184 | tf_op jit(solution)/shard_map/all_to_all | solution.py:280
  53.7 0.3 shard_map.53
  54.1 17.0 %all_to_all.21.in_ref = f32[4,296,128]{2,1,0:T(8,128)S(1)} all-to-all(f32[4,296,128]{2,1,0:T(8,128)S(1)} %shard_map.53), channel_id=1, replica_groups=mesh['y'=8,'x'=4,'zh'=4,'zl'=2,'c'=2] {'zh'}, dimensions={0} | all-to-all | bytes 1212416 | tf_op jit(solution)/shard_map/all_to_all | solution.py:282
  71.1 3.6 %shard_map.54 = (f32[2,136,128]{2,1,0:T(8,128)S(1)}, f32[2,136,128]{2,1,0:T(8,128)S(1)}) custom-call(f32[4,296,128]{2,1,0:T(8,128)S(1)} %all_to_all.21.in_ref, f32[1024,128]{1,0:T(8,128)S(1)} %get-tuple-element.10.keep, f32[1024,128]{1,0:T(8,128)S(1)} %collective-permute-done.core, f32[1160,128]{1,0:T(8,128)S(1)} %collective-permute-done.1.near, ...), custom_call_target="tpu_custom_call" | custom-call | tf_op jit(solution)/shard_map/pallas_call | solution.py:30
  74.7 8.7 %collective-permute-start.4 = (f32[2,136,128]{2,1,0:T(8,128)S(1)}, f32[2,136,128]{2,1,0:T(8,128)S(1)}, u32[]{:S(2)}, u32[]{:S(2)}) collective-permute-start(f32[2,136,128]{2,1,0:T(8,128)S(1)} %get-tuple-element.15), channel_id=1, source_target_pairs={{0,2},{1,15},{2,0},{3,5},{4,6},{5,3},{6,4},{7,9},{8,10},{9,7},{10,... | collective-permute-start | bytes 417800 | tf_op jit(solution)/shard_map/ppermute | solution.py:287
  83.4 2.4 %collective-permute-done.4.b_ref = f32[2,136,128]{2,1,0:T(8,128)S(1)} collective-permute-done((f32[2,136,128]{2,1,0:T(8,128)S(1)}, f32[2,136,128]{2,1,0:T(8,128)S(1)}, u32[]{:S(2)}, u32[]{:S(2)}) %collective-permute-start.4) | collective-permute-done | bytes 139296 | tf_op jit(solution)/shard_map/ppermute | solution.py:287
  85.9 25.9 %all_to_all.22.in_ref = f32[64,8,128]{2,1,0:T(8,128)S(1)} all-to-all(f32[64,8,128]{2,1,0:T(8,128)S(1)} %shard_map.55), channel_id=1, replica_groups=mesh['y'=8,'x'=4,'zh'=4,'zl'=2,'c'=2] {'y','x','c'}, dimensions={0} | all-to-all | bytes 524288 | tf_op jit(solution)/shard_map/all_to_all | solution.py:290
  111.8 0.1 shard_map.56
  111.9 12.9 %all_to_all.23.in_ref = f32[32,8,128]{2,1,0:T(8,128)S(1)} all-to-all(f32[32,8,128]{2,1,0:T(8,128)S(1)} %shard_map.56), channel_id=1, replica_groups=mesh['y'=8,'x'=4,'zh'=4,'zl'=2,'c'=2] {'y','x'}, dimensions={0} | all-to-all | bytes 262144 | tf_op jit(solution)/shard_map/all_to_all | solution.py:292
  124.8 0.6 shard_map.57
  (5 shorter events, 0.0 us)
Async XLA Ops:
  0.7 1.6 %copy-start = (f32[4096,128]{1,0:T(8,128)S(1)}, f32[4096,128]{1,0:T(8,128)}, u32[]{:S(2)}) copy-start(f32[4096,128]{1,0:T(8,128)} %far_in.1) | copy-start | bytes 6291460
  2.3 0.8 copy-start.1
  3.2 0.7 copy-start.2
  4.6 14.1 %collective-permute-start.2 = (f32[1160,128]{1,0:T(8,128)S(1)}, f32[1160,128]{1,0:T(8,128)S(1)}, u32[]{:S(2)}, u32[]{:S(2)}) collective-permute-start(f32[1160,128]{1,0:T(8,128)S(1)} %get-tuple-element.13), channel_id=1, source_target_pairs={{0,1},{1,0},{2,3},{3,2},{4,5},{5,4},{6,7},{7,6},{8,9},{9,8},{10,11... | collective-permute-start | bytes 1781768 | tf_op jit(solution)/shard_map/ppermute | solution.py:272
  13.4 12.6 %collective-permute-start.1 = (f32[1160,128]{1,0:T(8,128)S(1)}, f32[1160,128]{1,0:T(8,128)S(1)}, u32[]{:S(2)}, u32[]{:S(2)}) collective-permute-start(f32[1160,128]{1,0:T(8,128)S(1)} %get-tuple-element.12), channel_id=1, source_target_pairs={{0,2},{1,15},{2,0},{3,5},{4,6},{5,3},{6,4},{7,9},{8,10},{9,7},{10,... | collective-permute-start | bytes 1781768 | tf_op jit(solution)/shard_map/ppermute | solution.py:271
  18.7 13.7 %collective-permute-start.3 = (f32[1160,128]{1,0:T(8,128)S(1)}, f32[1160,128]{1,0:T(8,128)S(1)}, u32[]{:S(2)}, u32[]{:S(2)}) collective-permute-start(f32[1160,128]{1,0:T(8,128)S(1)} %collective-permute-done.2.far), channel_id=1, source_target_pairs={{0,2},{1,15},{2,0},{3,5},{4,6},{5,3},{6,4},{7,9},{8,10},{9,7},{10,... | collective-permute-start | bytes 1781768 | tf_op jit(solution)/shard_map/ppermute | solution.py:273
  20.7 3.8 %collective-permute-start = (f32[1024,128]{1,0:T(8,128)S(1)}, f32[1024,128]{1,0:T(8,128)S(1)}, u32[]{:S(2)}, u32[]{:S(2)}) collective-permute-start(f32[1024,128]{1,0:T(8,128)S(1)} %get-tuple-element.11), channel_id=1, source_target_pairs={{0,1},{1,0},{2,3},{3,2},{4,5},{5,4},{6,7},{7,6},{8,9},{9,8},{10,11... | collective-permute-start | bytes 1572872 | tf_op jit(solution)/shard_map/ppermute | solution.py:274
  74.7 11.2 %collective-permute-start.4 = (f32[2,136,128]{2,1,0:T(8,128)S(1)}, f32[2,136,128]{2,1,0:T(8,128)S(1)}, u32[]{:S(2)}, u32[]{:S(2)}) collective-permute-start(f32[2,136,128]{2,1,0:T(8,128)S(1)} %get-tuple-element.15), channel_id=1, source_target_pairs={{0,2},{1,15},{2,0},{3,5},{4,6},{5,3},{6,4},{7,9},{8,10},{9,7},{10,... | collective-permute-start | bytes 417800 | tf_op jit(solution)/shard_map/ppermute | solution.py:287

commit v3 on v2

v3 whole, which is shorter than its diff:
```python
import functools

import jax
import jax.numpy as jnp
from jax import lax
from jax.experimental import pallas as pl
from jax.experimental.pallas import tpu as pltpu
from jax.sharding import Mesh
from jax.sharding import PartitionSpec as P

F32 = jnp.float32
AXES = ("y", "x", "zh", "zl", "c")
WIDE = ("y", "x")
DEEP = ("zh", "zl", "c")
PARTS = 4
LIMIT = 48 * 1024 * 1024
EDGE = 48 * 1024 * 1024


def mult(left, right, contract=((1,), (0,))):
    return lax.dot_general(
        left, right, (contract, ((), ())),
        preferred_element_type=F32, precision=lax.Precision.HIGHEST,
    )


def whole(*shape):
    return jax.ShapeDtypeStruct(shape, F32)


def call(body, out_shape, *args, scalars=0):
    spaces = [pltpu.SMEM] * scalars + [pltpu.VMEM] * (len(args) - scalars)
    return pl.pallas_call(
        body,
        out_shape=out_shape,
        in_specs=[pl.BlockSpec(memory_space=space) for space in spaces],
        compiler_params=pltpu.CompilerParams(vmem_limit_bytes=LIMIT),
    )(*args)


def cut_body(which, counts_ref, out_ref):
    out_ref[...] = jnp.log(counts_ref[...])


def cut_more_body(which, counts_ref, loading_ref, offset_ref, out_ref):
    rows, comps = counts_ref.shape
    out_ref[0:rows, :] = jnp.log(counts_ref[...])
    out_ref[rows : rows + comps, :] = loading_ref[...]
    out_ref[rows + comps : rows + comps + 8, :] = jnp.broadcast_to(offset_ref[...], (8, comps))


def cut(which, counts, *others):
    rows, width = counts.shape[0] // 4, counts.shape[1]

    def full(shape):
        return pl.BlockSpec(shape, lambda i, which: (0, 0))

    height = rows + (others[0].shape[0] + 8 if others else 0)
    return pl.pallas_call(
        cut_more_body if others else cut_body,
        out_shape=whole(height, width),
        grid_spec=pltpu.PrefetchScalarGridSpec(
            num_scalar_prefetch=1,
            grid=(1,),
            in_specs=[pl.BlockSpec((rows, width), lambda i, which: (which[0], 0))]
            + [full(a.shape) for a in others],
            out_specs=full((height, width)),
        ),
        compiler_params=pltpu.CompilerParams(vmem_limit_bytes=EDGE),
    )(which.reshape(1), counts, *others)


def log_sums(logs, ones, comps):
    return [
        mult(ones, logs[h * comps : (h + 1) * comps, :], ((1,), (1,)))[0:1, :]
        for h in range(logs.shape[0] // comps)
    ]


def encode_body(keep, core, near, far, loading_ref, out_ref):
    total, comps = keep.shape
    parts = PARTS
    rows, share = total // parts, comps // parts
    loads = [loading_ref[...], far[total : total + comps, :], near[total : total + comps, :]]
    bars = [jnp.sum(load, axis=0, keepdims=True) / comps for load in loads]
    bare = [load - bar for load, bar in zip(loads, bars)]
    pair = jnp.concatenate(bare[0:2], axis=0)
    gram = mult(loads[0], loads[0], ((0,), (0,)))
    for load in loads[1:]:
        gram += mult(load, load, ((0,), (0,)))
    shift = mult(far[total + comps : total + comps + 8, :], loads[1])
    shift += mult(near[total + comps : total + comps + 8, :], loads[2])
    ones = jnp.ones((8, comps), F32)
    for j in range(parts):
        logs = [source[j * rows : (j + 1) * rows, :] for source in (keep, core, near)]
        both = jnp.concatenate(logs[0:2], axis=1)
        out_ref[j, 0:rows, :] = mult(both, pair) + mult(logs[2], bare[2])
        for k, part in enumerate(logs):
            for h, sums in enumerate(log_sums(part, ones, comps)):
                at = rows + 4 * h + k
                out_ref[j, at : at + 1, :] = sums
            out_ref[j, rows + 8 + k : rows + 9 + k, :] = bars[k]
        out_ref[j, rows + 12 : rows + 13, :] = shift[0:1, :]
        out_ref[j, rows + 16 : rows + 16 + share, :] = gram[j * share : (j + 1) * share, :]


def encode_last_body(steps, place, in_ref, more, loading_ref, offset_ref, *outs):
    parts, height, comps = in_ref.shape
    share = comps // parts
    rows = height - 16 - share
    total = parts * rows
    load = more[total : total + comps, :]
    bar = jnp.sum(load, axis=0, keepdims=True) / comps
    bare = load - bar
    gram = mult(load, load, ((0,), (0,)))
    shift = mult(more[total + comps : total + comps + 8, :], load)
    shift += mult(jnp.broadcast_to(offset_ref[...], (8, comps)), loading_ref[...])
    ones = jnp.ones((8, comps), F32)
    blank = jnp.zeros((3, comps), F32)
    for step, out_ref in zip(steps, outs):
        j = lax.rem(place[0] + step, parts)
        logs = more[pl.ds(pl.multiple_of(j * rows, rows), rows), :]
        out_ref[0:rows, :] = in_ref[j, 0:rows, :] + mult(logs, bare)
        for h, sums in enumerate(log_sums(logs, ones, comps)):
            at = rows + 4 * h
            out_ref[at : at + 3, :] = in_ref[j, at : at + 3, :]
            out_ref[at + 3 : at + 4, :] = sums
        out_ref[rows + 8 : rows + 11, :] = in_ref[j, rows + 8 : rows + 11, :]
        out_ref[rows + 11 : rows + 12, :] = bar
        out_ref[rows + 12 : rows + 13, :] = in_ref[j, rows + 12 : rows + 13, :] + shift[0:1, :]
        out_ref[rows + 13 : rows + 16, :] = blank
        at = rows + 16
        mine = in_ref[j, at : at + share, :]
        for q in range(parts):
            mine += jnp.where(j == q, gram[q * share : (q + 1) * share, :], 0.0)
        out_ref[at : at + share, :] = mine


def finish_body(channels, *refs):
    ins, out_ref = refs[:-1], refs[-1]
    parts = len(ins)
    height, comps = ins[0].shape
    share = comps // parts
    rows = height - 16 - share
    bars = jnp.concatenate([a[rows + 8 : rows + 12, :] for a in ins], axis=0)
    shift = sum(a[rows + 12 : rows + 13, :] for a in ins)
    for h in range(rows // comps):
        sums = jnp.concatenate([a[rows + 4 * h : rows + 4 * h + 4, :] for a in ins], axis=0)
        geo = jnp.sum(sums, axis=0, keepdims=True) / channels
        at = h * comps
        total = mult(sums - comps * geo, bars, ((0,), (0,))) - shift
        for a in ins:
            total += a[at : at + comps, :]
        out_ref[at : at + comps, :] = total
        out_ref[rows + h : rows + h + 1, :] = geo
    out_ref[rows + 2 : rows + 8, :] = jnp.zeros((6, comps), F32)
    out_ref[rows + 8 : rows + 8 + share, :] = sum(a[rows + 16 : rows + 16 + share, :] for a in ins)


def block_terms(j, s_ref, logs, offs, rows):
    comps = s_ref.shape[1]
    pick = lax.broadcasted_iota(jnp.int32, (8, comps), 0)
    geos = s_ref[rows : rows + 8, :]
    s = s_ref[0:rows, :]
    geo = jnp.concatenate(
        [
            mult(geos, jnp.where(pick == h, 1.0, 0.0).astype(F32), ((0,), (0,)))
            for h in range(rows // comps)
        ],
        axis=0,
    )
    here = pl.ds(pl.multiple_of(j * rows, rows), rows)
    both = jnp.concatenate([a[here, :] - geo - off for a, off in zip(logs, offs)] + [s], axis=1)
    return mult(s.T, both), jnp.sum(both, axis=0, keepdims=True)


def grad_body(steps, place, keep, core, near, far, more, offset_ref, *refs):
    total, comps = keep.shape
    out_ref = refs[-1]
    blocks, before = refs[: len(steps)], refs[len(steps) : -1]
    parts = PARTS
    rows = total // parts
    logs = (keep, core, near, more)
    offs = (offset_ref[...],) + tuple(a[total + comps : total + comps + 1, :] for a in (far, near, more))
    wide, sums = 0.0, 0.0
    if before:
        wide, sums = before[0][0:comps, :], before[0][comps : comps + 1, :]
    for step, block in zip(steps, blocks):
        j = lax.rem(place[0] + parts - step, parts)
        more_wide, more_sums = block_terms(j, block, logs, offs, rows)
        wide, sums = wide + more_wide, sums + more_sums
    out_ref[0:comps, :] = wide
    out_ref[comps : comps + 8, :] = jnp.broadcast_to(sums, (8, sums.shape[1]))


def last_grad_body(place, in_ref, near, far, more, loading_ref, own, one, two, three, *outs):
    comps = loading_ref.shape[0]
    total = near.shape[0] - comps - 8
    share = comps // PARTS
    rows = own.shape[0] - 8 - share
    row = lax.broadcasted_iota(jnp.int32, (comps, comps), 0)
    col = lax.broadcasted_iota(jnp.int32, (comps, comps), 1)
    hat = jnp.where(row == col, -2.0, 0.0).astype(F32)
    for step, a in enumerate((own, one, two, three)):
        j = lax.rem(place[0] + PARTS - step, PARTS)
        part = a[rows + 8 : rows + 8 + share, :]
        hat += jnp.where(lax.div(row, share) == j, jnp.concatenate([part] * PARTS, axis=0), 0.0)
    wide = in_ref[0:comps, :]
    sums = in_ref[comps : comps + 8, :]
    loads = (loading_ref[...],) + tuple(a[total : total + comps, :] for a in (far, near, more))
    square = wide[:, 4 * comps : 5 * comps]
    s_hat = mult(sums[:, 4 * comps : 5 * comps], hat)
    for k, out in enumerate(outs):
        here = slice(k * comps, (k + 1) * comps)
        out[0:comps, :] = mult(wide[:, here], hat, ((0,), (0,))) + mult(loads[k], square)
        out[comps : comps + 8, :] = -(mult(s_hat, loads[k], ((1,), (1,))) + sums[:, here])


def deal_body(a_ref, b_ref, c_ref, d_ref, out_ref):
    pieces, _, comps = out_ref.shape
    share = comps // pieces
    total = a_ref[...] + b_ref[...] + c_ref[...] + d_ref[...]
    for p in range(pieces):
        out_ref[p, 0:share, :] = total[p * share : (p + 1) * share, :]
        out_ref[p, share:8, :] = total[comps : comps + 8 - share, :]


def gather_body(pixels, in_ref, out_ref):
    total = jnp.sum(in_ref[...], axis=0) / pixels
    for j in range(out_ref.shape[0]):
        out_ref[j] = total


def last_body(in_ref, load_ref, off_ref):
    pieces = in_ref.shape[0]
    share = load_ref.shape[0] // pieces
    for p in range(pieces):
        load_ref[p * share : (p + 1) * share, :] = in_ref[p, 0:share, :]
    off_ref[...] = in_ref[0, share : share + 1, :]


def on_device(counts, offset, loading):
    pixels = counts.shape[0] * lax.axis_size(WIDE)
    comps = loading.shape[1]
    channels = counts.shape[1] * PARTS * 4
    rows = counts.shape[0] // 4 // PARTS
    share = comps // PARTS
    core = lax.axis_index("c").astype(jnp.int32)
    side = lax.axis_index("zl").astype(jnp.int32)
    place = lax.axis_index("zh").astype(jnp.int32).reshape(1)
    offset = offset.reshape(1, comps)

    swap = [(0, 1), (1, 0)]
    ring = [[(h, (h + k) % PARTS) for h in range(PARTS)] for k in range(PARTS)]
    near_pairs, cross_pairs = [], []
    for z in range(2 * PARTS):
        for c in range(2):
            partner = (((z - c) % (2 * PARTS) ^ 1) + c) % (2 * PARTS)
            near_pairs.append((2 * z + c, 2 * partner + c))
            cross_pairs.append((2 * z + c, 2 * partner + 1 - c))

    near_out = cut(2 * core + 1 - side, counts, loading, offset)
    near = lax.ppermute(near_out, DEEP, near_pairs)
    far_out = cut(2 * (1 - core) + 1 - side, counts, loading, offset)
    far = lax.ppermute(far_out, "c", swap)
    more = lax.ppermute(far, DEEP, near_pairs)
    other = lax.ppermute(cut(2 * (1 - core) + side, counts), "c", swap)
    keep = cut(2 * core + side, counts)
    height = rows + 16 + share
    partial = call(
        encode_body, whole(PARTS, height, comps), keep, other, near, far, loading
    )
    late = (partial, more, loading, offset)
    block = whole(height, comps)
    (two,) = call(functools.partial(encode_last_body, (2,)), (block,), place, *late, scalars=1)
    two = lax.ppermute(two, "zh", ring[2])
    one, three, own = call(
        functools.partial(encode_last_body, (1, 3, 0)), (block,) * 3, place, *late, scalars=1
    )
    one = lax.ppermute(one, "zh", ring[1])
    three = lax.ppermute(three, "zh", ring[3])
    own = call(functools.partial(finish_body, channels), whole(height - 8, comps), own, one, two, three)
    two, one, three = [lax.ppermute(own, "zh", ring[k]) for k in (2, 1, 3)]
    total = whole(comps + 8, 5 * comps)
    common = (place, keep, other, near, far, more, offset)
    grads = call(functools.partial(grad_body, (0,)), total, *common, own, scalars=1)
    grads = call(functools.partial(grad_body, (1, 3)), total, *common, one, three, grads, scalars=1)
    grads = call(functools.partial(grad_body, (2,)), total, *common, two, grads, scalars=1)
    shape = whole(comps + 8, comps)
    mine, to_core, to_near, to_cross = call(
        last_grad_body, (shape,) * 4, place, grads, near, far, more, loading, own, one, two, three, scalars=1
    )
    cross = lax.ppermute(to_cross, DEEP, cross_pairs)
    neared = lax.ppermute(to_near, DEEP, near_pairs)
    cored = lax.ppermute(to_core, "c", swap)
    plane = lax.axis_size(WIDE)
    pieces = call(deal_body, whole(plane, 8, comps), mine, cored, neared, cross)
    pieces = lax.all_to_all(pieces, WIDE, 0, 0)
    pieces = call(functools.partial(gather_body, pixels), whole(plane, 8, comps), pieces)
    pieces = lax.all_to_all(pieces, WIDE, 0, 0)
    grad, grad_offset = call(last_body, (whole(comps, comps), whole(1, comps)), pieces)
    return grad, grad_offset.reshape(comps)


def solution(mesh):
    wide, deep = mesh.devices.shape
    split_mesh = Mesh(mesh.devices.reshape(wide // 4, 4, deep // 4, 2, 2), AXES)
    return jax.shard_map(
        on_device,
        mesh=split_mesh,
        in_specs=(P(WIDE, DEEP), P(DEEP), P(DEEP, None)),
        out_specs=(P(DEEP, None), P(DEEP)),
        check_vma=False,
    )
```

time: 126 us -> 130 us (1.032)
  the two profiles are of different devices: /device:TPU:1 before, /device:TPU:8 now
where the time goes in v3:
time: 130 us; the launch traced here: 129 us
  starting transfers between devices  48.8 us (38%)
  blocking collectives  33.3 us (26%)
  waiting for transfers between devices  24 us (18%)
  Pallas kernels  19.3 us (15%)
  local copies, waits for them, and re-layouts  3.09 us (2%)
    all_to_all x2, blocking collectives, on_device(): pieces = lax.all_to_all(pieces, WIDE, 0, 0)  33.3 us
    pallas_call x11, Pallas kernels, call(): pl.pallas_call(body, out_shape=out_shape, in_specs=[pl.BlockSpec(memory_s...  17.4 us
    ppermute x3, starting transfers between devices, on_device(): two, one, three = [lax.ppermute(own, 'zh', ring[k]) for k in (2, 1, 3)]  11.7 us
    ppermute x1, starting transfers between devices, on_device(): other = lax.ppermute(cut(2 * (1 - core) + side, counts), 'c', swap)  8.78 us
    ppermute x1, waiting for transfers between devices, on_device(): two = lax.ppermute(two, 'zh', ring[2])  8.03 us
    ppermute x3, waiting for transfers between devices, on_device(): two, one, three = [lax.ppermute(own, 'zh', ring[k]) for k in (2, 1, 3)]  7.47 us
    ppermute x1, starting transfers between devices, on_device(): three = lax.ppermute(three, 'zh', ring[3])  6.25 us
    ppermute x1, starting transfers between devices, on_device(): two = lax.ppermute(two, 'zh', ring[2])  6.03 us
  transfers between devices with their start and end apart: 13, of which 6 were waited for; matrix products, arithmetic and copies ran while one was open for 0% of the time, Pallas kernels for 10%

profile of v3, /device:TPU:8, one launch (start us, length us, event | category | flops | bytes accessed | tf_op | source)
XLA Modules:
  0.0 129.4 jit_solution(8202230850883892617)
XLA Ops:
  3.8 2.1 %collective-permute-start.2 = (f32[1160,128]{1,0:T(8,128)S(1)}, f32[1160,128]{1,0:T(8,128)S(1)}, u32[]{:S(2)}, u32[]{:S(2)}) collective-permute-start(f32[1160,128]{1,0:T(8,128)S(1)} %shard_map.53), channel_id=1, source_target_pairs={{0,1},{1,0},{2,3},{3,2},{4,5},{5,4},{6,7},{7,6},{8,9},{9,8},{10,11... | collective-permute-start | bytes 1781768 | tf_op jit(solution)/shard_map/ppermute | solution.py:265
  6.8 4.3 %collective-permute-start.1 = (f32[1160,128]{1,0:T(8,128)}, f32[1160,128]{1,0:T(8,128)}, u32[]{:S(2)}, u32[]{:S(2)}) collective-permute-start(f32[1160,128]{1,0:T(8,128)} %shard_map.52), channel_id=1, source_target_pairs={{0,2},{1,15},{2,0},{3,5},{4,6},{5,3},{6,4},{7,9},{8,10},{9,7},{10,... | collective-permute-start | bytes 1781768 | tf_op jit(solution)/shard_map/ppermute | solution.py:263
  11.1 1.9 %collective-permute-start.3 = (f32[1160,128]{1,0:T(8,128)S(1)}, f32[1160,128]{1,0:T(8,128)S(1)}, u32[]{:S(2)}, u32[]{:S(2)}) collective-permute-start(f32[1160,128]{1,0:T(8,128)S(1)} %collective-permute-done.2.far), channel_id=1, source_target_pairs={{0,2},{1,15},{2,0},{3,5},{4,6},{5,3},{6,4},{7,9},{8,10},{9,7},{10,... | collective-permute-start | bytes 1781768 | tf_op jit(solution)/shard_map/ppermute | solution.py:266
  13.9 8.8 %collective-permute-start = (f32[1024,128]{1,0:T(8,128)}, f32[1024,128]{1,0:T(8,128)}, u32[]{:S(2)}, u32[]{:S(2)}) collective-permute-start(f32[1024,128]{1,0:T(8,128)} %shard_map.51), channel_id=1, source_target_pairs={{0,1},{1,0},{2,3},{3,2},{4,5},{5,4},{6,7},{7,6},{8,9},{9,8},{10,11... | collective-permute-start | bytes 1572872 | tf_op jit(solution)/shard_map/ppermute | solution.py:267
  24.6 5.3 %shard_map.54.in_ref = f32[4,304,128]{2,1,0:T(8,128)S(1)} custom-call(f32[1024,128]{1,0:T(8,128)S(1)} %shard_map.50.keep, f32[1024,128]{1,0:T(8,128)} %collective-permute-done.core, f32[1160,128]{1,0:T(8,128)} %collective-permute-done.1.near, f32[1160,128]{1,0:T(8,128)S(1)} %collective-permute-done.2.far, f32[128,128]{1,0:T(8,128)S(1)} %copy-done.3), custom_call_target="tpu_custom_call" | custom-call | tf_op jit(solution)/shard_map/pallas_call | solution.py:33
  31.1 1.9 %collective-permute-start.4 = (f32[304,128]{1,0:T(8,128)S(1)}, f32[304,128]{1,0:T(8,128)S(1)}, u32[]{:S(2)}, u32[]{:S(2)}) collective-permute-start(f32[304,128]{1,0:T(8,128)S(1)} %get-tuple-element.12), channel_id=1, source_target_pairs={{0,4},{4,8},{8,12},{12,0},{1,5},{5,9},{9,13},{13,1},{2,6},{6,10},{... | collective-permute-start | bytes 466952 | tf_op jit(solution)/shard_map/ppermute | solution.py:280
  33.1 6.2 %collective-permute-start.6 = (f32[304,128]{1,0:T(8,128)S(1)}, f32[304,128]{1,0:T(8,128)S(1)}, u32[]{:S(2)}, u32[]{:S(2)}) collective-permute-start(f32[304,128]{1,0:T(8,128)S(1)} %get-tuple-element.13), channel_id=1, source_target_pairs={{0,12},{4,0},{8,4},{12,8},{1,13},{5,1},{9,5},{13,9},{2,14},{6,2},{... | collective-permute-start | bytes 466952 | tf_op jit(solution)/shard_map/ppermute | solution.py:281
  39.9 6.0 %collective-permute-start.5 = (f32[304,128]{1,0:T(8,128)S(1)}, f32[304,128]{1,0:T(8,128)S(1)}, u32[]{:S(2)}, u32[]{:S(2)}) collective-permute-start(f32[304,128]{1,0:T(8,128)S(1)} %shard_map.56), channel_id=1, source_target_pairs={{0,8},{4,12},{8,0},{12,4},{1,9},{5,13},{9,1},{13,5},{2,10},{6,14},... | collective-permute-start | bytes 466952 | tf_op jit(solution)/shard_map/ppermute | solution.py:276
  47.7 8.0 %collective-permute-done.5.refs_2_ = f32[304,128]{1,0:T(8,128)S(1)} collective-permute-done((f32[304,128]{1,0:T(8,128)S(1)}, f32[304,128]{1,0:T(8,128)S(1)}, u32[]{:S(2)}, u32[]{:S(2)}) %collective-permute-start.5) | collective-permute-done | bytes 155680 | tf_op jit(solution)/shard_map/ppermute | solution.py:276
  56.1 1.9 %collective-permute-start.9 = (f32[296,128]{1,0:T(8,128)S(1)}, f32[296,128]{1,0:T(8,128)S(1)}, u32[]{:S(2)}, u32[]{:S(2)}) collective-permute-start(f32[296,128]{1,0:T(8,128)S(1)} %shard_map.57.refs_0_.own), channel_id=1, source_target_pairs={{0,12},{4,0},{8,4},{12,8},{1,13},{5,1},{9,5},{13,9},{2,14},{6,2},{... | collective-permute-start | bytes 454664 | tf_op jit(solution)/shard_map/ppermute | solution.py:283
  58.0 4.8 %collective-permute-start.8 = (f32[296,128]{1,0:T(8,128)S(1)}, f32[296,128]{1,0:T(8,128)S(1)}, u32[]{:S(2)}, u32[]{:S(2)}) collective-permute-start(f32[296,128]{1,0:T(8,128)S(1)} %shard_map.57.refs_0_.own), channel_id=1, source_target_pairs={{0,4},{4,8},{8,12},{12,0},{1,5},{5,9},{9,13},{13,1},{2,6},{6,10},{... | collective-permute-start | bytes 454664 | tf_op jit(solution)/shard_map/ppermute | solution.py:283
  62.9 5.0 %collective-permute-start.7 = (f32[296,128]{1,0:T(8,128)S(1)}, f32[296,128]{1,0:T(8,128)S(1)}, u32[]{:S(2)}, u32[]{:S(2)}) collective-permute-start(f32[296,128]{1,0:T(8,128)S(1)} %shard_map.57.refs_0_.own), channel_id=1, source_target_pairs={{0,8},{4,12},{8,0},{12,4},{1,9},{5,13},{9,1},{13,5},{2,10},{6,14},... | collective-permute-start | bytes 454664 | tf_op jit(solution)/shard_map/ppermute | solution.py:283
  67.9 2.1 %shard_map.58.refs_2_ = f32[136,640]{1,0:T(8,128)S(1)} custom-call(s32[1]{0:T(128)} %bitcast.place, f32[1024,128]{1,0:T(8,128)S(1)} %shard_map.50.keep, f32[1024,128]{1,0:T(8,128)} %collective-permute-done.core, f32[1160,128]{1,0:T(8,128)} %collective-permute-done.1.near, f32[1160,128]{1,0:T(8,128)S(1)} %collective-permute-done.2.far, ...), custom_call_target="tpu_custom_call" | custom-call | tf_op jit(solution)/shard_map/pallas_call | solution.py:33
  70.0 2.8 %shard_map.59.refs_1_ = f32[136,640]{1,0:T(8,128)S(1)} custom-call(s32[1]{0:T(128)} %bitcast.place, f32[1024,128]{1,0:T(8,128)S(1)} %shard_map.50.keep, f32[1024,128]{1,0:T(8,128)} %collective-permute-done.core, f32[1160,128]{1,0:T(8,128)} %collective-permute-done.1.near, f32[1160,128]{1,0:T(8,128)S(1)} %collective-permute-done.2.far, ...), custom_call_target="tpu_custom_call" | custom-call | tf_op jit(solution)/shard_map/pallas_call | solution.py:33
  72.8 7.5 %collective-permute-done.7.refs_0_.two = f32[296,128]{1,0:T(8,128)S(1)} collective-permute-done((f32[296,128]{1,0:T(8,128)S(1)}, f32[296,128]{1,0:T(8,128)S(1)}, u32[]{:S(2)}, u32[]{:S(2)}) %collective-permute-start.7) | collective-permute-done | bytes 151584 | tf_op jit(solution)/shard_map/ppermute | solution.py:283
  80.3 2.1 %shard_map.60.in_ref = f32[136,640]{1,0:T(8,128)S(1)} custom-call(s32[1]{0:T(128)} %bitcast.place, f32[1024,128]{1,0:T(8,128)S(1)} %shard_map.50.keep, f32[1024,128]{1,0:T(8,128)} %collective-permute-done.core, f32[1160,128]{1,0:T(8,128)} %collective-permute-done.1.near, f32[1160,128]{1,0:T(8,128)S(1)} %collective-permute-done.2.far, ...), custom_call_target="tpu_custom_call" | custom-call | tf_op jit(solution)/shard_map/pallas_call | solution.py:33
  82.4 2.2 %shard_map.61 = (f32[136,128]{1,0:T(8,128)S(1)}, f32[136,128]{1,0:T(8,128)S(1)}, f32[136,128]{1,0:T(8,128)S(1)}, f32[136,128]{1,0:T(8,128)S(1)}) custom-call(s32[1]{0:T(128)} %bitcast.place, f32[136,640]{1,0:T(8,128)S(1)} %shard_map.60.in_ref, f32[1160,128]{1,0:T(8,128)} %collective-permute-done.1.near, f32[1160,128]{1,0:T(8,128)S(1)} %collective-permute-done.2.far, ...), custom_call_target="tpu_custom_call" | custom-call | tf_op jit(solution)/shard_map/pallas_call | solution.py:33
  84.6 1.9 %collective-permute-start.10 = (f32[136,128]{1,0:T(8,128)S(1)}, f32[136,128]{1,0:T(8,128)S(1)}, u32[]{:S(2)}, u32[]{:S(2)}) collective-permute-start(f32[136,128]{1,0:T(8,128)S(1)} %get-tuple-element.15), channel_id=1, source_target_pairs={{0,1},{1,0},{2,3},{3,2},{4,5},{5,4},{6,7},{7,6},{8,9},{9,8},{10,11... | collective-permute-start | bytes 208904 | tf_op jit(solution)/shard_map/ppermute | solution.py:295
  86.5 1.9 %collective-permute-start.11 = (f32[136,128]{1,0:T(8,128)S(1)}, f32[136,128]{1,0:T(8,128)S(1)}, u32[]{:S(2)}, u32[]{:S(2)}) collective-permute-start(f32[136,128]{1,0:T(8,128)S(1)} %get-tuple-element.16), channel_id=1, source_target_pairs={{0,2},{1,15},{2,0},{3,5},{4,6},{5,3},{6,4},{7,9},{8,10},{9,7},{10,... | collective-permute-start | bytes 208904 | tf_op jit(solution)/shard_map/ppermute | solution.py:294
  88.4 2.0 %collective-permute-start.12 = (f32[136,128]{1,0:T(8,128)S(1)}, f32[136,128]{1,0:T(8,128)S(1)}, u32[]{:S(2)}, u32[]{:S(2)}) collective-permute-start(f32[136,128]{1,0:T(8,128)S(1)} %get-tuple-element.17), channel_id=1, source_target_pairs={{0,3},{1,14},{2,1},{3,4},{4,7},{5,2},{6,5},{7,8},{8,11},{9,6},{10,... | collective-permute-start | bytes 208904 | tf_op jit(solution)/shard_map/ppermute | solution.py:293
  90.4 2.3 %collective-permute-done.11.c_ref = f32[136,128]{1,0:T(8,128)S(1)} collective-permute-done((f32[136,128]{1,0:T(8,128)S(1)}, f32[136,128]{1,0:T(8,128)S(1)}, u32[]{:S(2)}, u32[]{:S(2)}) %collective-permute-start.11) | collective-permute-done | bytes 69664 | tf_op jit(solution)/shard_map/ppermute | solution.py:294
  92.7 2.7 %collective-permute-done.12.d_ref = f32[136,128]{1,0:T(8,128)S(1)} collective-permute-done((f32[136,128]{1,0:T(8,128)S(1)}, f32[136,128]{1,0:T(8,128)S(1)}, u32[]{:S(2)}, u32[]{:S(2)}) %collective-permute-start.12) | collective-permute-done | bytes 69664 | tf_op jit(solution)/shard_map/ppermute | solution.py:293
  95.4 19.5 %all_to_all.10.in_ref = f32[32,8,128]{2,1,0:T(8,128)S(1)} all-to-all(f32[32,8,128]{2,1,0:T(8,128)S(1)} %shard_map.62), channel_id=1, replica_groups=mesh['y'=8,'x'=4,'zh'=4,'zl'=2,'c'=2] {'y','x'}, dimensions={0} | all-to-all | bytes 262144 | tf_op jit(solution)/shard_map/all_to_all | solution.py:298
  114.9 13.8 %all_to_all.11.in_ref = f32[32,8,128]{2,1,0:T(8,128)S(1)} all-to-all(f32[32,8,128]{2,1,0:T(8,128)S(1)} %shard_map.63), channel_id=1, replica_groups=mesh['y'=8,'x'=4,'zh'=4,'zl'=2,'c'=2] {'y','x'}, dimensions={0} | all-to-all | bytes 262144 | tf_op jit(solution)/shard_map/all_to_all | solution.py:300
  (31 shorter events, 11.5 us)
Async XLA Ops:
  0.6 5.3 %copy-start.5 = (f32[128]{0:T(128)S(1)}, f32[128]{0:T(128)}, u32[]{:S(2)}) copy-start(f32[128]{0:T(128)} %param.4) | copy-start | bytes 1540
  0.7 1.6 %copy-start = (f32[4096,128]{1,0:T(8,128)S(1)}, f32[4096,128]{1,0:T(8,128)}, u32[]{:S(2)}) copy-start(f32[4096,128]{1,0:T(8,128)} %counts_ref.7) | copy-start | bytes 6291460
  2.2 0.8 copy-start.2
  3.1 0.7 copy-start.4
  3.7 2.2 %copy-start.1 = (f32[4096,128]{1,0:T(8,128)S(1)}, f32[4096,128]{1,0:T(8,128)}, u32[]{:S(2)}) copy-start(f32[4096,128]{1,0:T(8,128)} %counts_ref.7) | copy-start | bytes 6291460
  3.7 2.2 %copy-start.3 = (f32[128,128]{1,0:T(8,128)S(1)}, f32[128,128]{1,0:T(8,128)}, u32[]{:S(2)}) copy-start(f32[128,128]{1,0:T(8,128)} %loading_ref.11) | copy-start | bytes 196612
  3.8 7.3 %collective-permute-start.2 = (f32[1160,128]{1,0:T(8,128)S(1)}, f32[1160,128]{1,0:T(8,128)S(1)}, u32[]{:S(2)}, u32[]{:S(2)}) collective-permute-start(f32[1160,128]{1,0:T(8,128)S(1)} %shard_map.53), channel_id=1, source_target_pairs={{0,1},{1,0},{2,3},{3,2},{4,5},{5,4},{6,7},{7,6},{8,9},{9,8},{10,11... | collective-permute-start | bytes 1781768 | tf_op jit(solution)/shard_map/ppermute | solution.py:265
  6.8 17.7 %collective-permute-start.1 = (f32[1160,128]{1,0:T(8,128)}, f32[1160,128]{1,0:T(8,128)}, u32[]{:S(2)}, u32[]{:S(2)}) collective-permute-start(f32[1160,128]{1,0:T(8,128)} %shard_map.52), channel_id=1, source_target_pairs={{0,2},{1,15},{2,0},{3,5},{4,6},{5,3},{6,4},{7,9},{8,10},{9,7},{10,... | collective-permute-start | bytes 1781768 | tf_op jit(solution)/shard_map/ppermute | solution.py:263
  11.1 18.8 %collective-permute-start.3 = (f32[1160,128]{1,0:T(8,128)S(1)}, f32[1160,128]{1,0:T(8,128)S(1)}, u32[]{:S(2)}, u32[]{:S(2)}) collective-permute-start(f32[1160,128]{1,0:T(8,128)S(1)} %collective-permute-done.2.far), channel_id=1, source_target_pairs={{0,2},{1,15},{2,0},{3,5},{4,6},{5,3},{6,4},{7,9},{8,10},{9,7},{10,... | collective-permute-start | bytes 1781768 | tf_op jit(solution)/shard_map/ppermute | solution.py:266
  13.9 10.6 %collective-permute-start = (f32[1024,128]{1,0:T(8,128)}, f32[1024,128]{1,0:T(8,128)}, u32[]{:S(2)}, u32[]{:S(2)}) collective-permute-start(f32[1024,128]{1,0:T(8,128)} %shard_map.51), channel_id=1, source_target_pairs={{0,1},{1,0},{2,3},{3,2},{4,5},{5,4},{6,7},{7,6},{8,9},{9,8},{10,11... | collective-permute-start | bytes 1572872 | tf_op jit(solution)/shard_map/ppermute | solution.py:267
  31.1 14.8 %collective-permute-start.4 = (f32[304,128]{1,0:T(8,128)S(1)}, f32[304,128]{1,0:T(8,128)S(1)}, u32[]{:S(2)}, u32[]{:S(2)}) collective-permute-start(f32[304,128]{1,0:T(8,128)S(1)} %get-tuple-element.12), channel_id=1, source_target_pairs={{0,4},{4,8},{8,12},{12,0},{1,5},{5,9},{9,13},{13,1},{2,6},{6,10},{... | collective-permute-start | bytes 466952 | tf_op jit(solution)/shard_map/ppermute | solution.py:280
  33.1 14.7 %collective-permute-start.6 = (f32[304,128]{1,0:T(8,128)S(1)}, f32[304,128]{1,0:T(8,128)S(1)}, u32[]{:S(2)}, u32[]{:S(2)}) collective-permute-start(f32[304,128]{1,0:T(8,128)S(1)} %get-tuple-element.13), channel_id=1, source_target_pairs={{0,12},{4,0},{8,4},{12,8},{1,13},{5,1},{9,5},{13,9},{2,14},{6,2},{... | collective-permute-start | bytes 466952 | tf_op jit(solution)/shard_map/ppermute | solution.py:281
  39.9 15.8 %collective-permute-start.5 = (f32[304,128]{1,0:T(8,128)S(1)}, f32[304,128]{1,0:T(8,128)S(1)}, u32[]{:S(2)}, u32[]{:S(2)}) collective-permute-start(f32[304,128]{1,0:T(8,128)S(1)} %shard_map.56), channel_id=1, source_target_pairs={{0,8},{4,12},{8,0},{12,4},{1,9},{5,13},{9,1},{13,5},{2,10},{6,14},... | collective-permute-start | bytes 466952 | tf_op jit(solution)/shard_map/ppermute | solution.py:276
  56.1 13.9 %collective-permute-start.9 = (f32[296,128]{1,0:T(8,128)S(1)}, f32[296,128]{1,0:T(8,128)S(1)}, u32[]{:S(2)}, u32[]{:S(2)}) collective-permute-start(f32[296,128]{1,0:T(8,128)S(1)} %shard_map.57.refs_0_.own), channel_id=1, source_target_pairs={{0,12},{4,0},{8,4},{12,8},{1,13},{5,1},{9,5},{13,9},{2,14},{6,2},{... | collective-permute-start | bytes 454664 | tf_op jit(solution)/shard_map/ppermute | solution.py:283
  58.0 12.0 %collective-permute-start.8 = (f32[296,128]{1,0:T(8,128)S(1)}, f32[296,128]{1,0:T(8,128)S(1)}, u32[]{:S(2)}, u32[]{:S(2)}) collective-permute-start(f32[296,128]{1,0:T(8,128)S(1)} %shard_map.57.refs_0_.own), channel_id=1, source_target_pairs={{0,4},{4,8},{8,12},{12,0},{1,5},{5,9},{9,13},{13,1},{2,6},{6,10},{... | collective-permute-start | bytes 454664 | tf_op jit(solution)/shard_map/ppermute | solution.py:283
  62.9 17.4 %collective-permute-start.7 = (f32[296,128]{1,0:T(8,128)S(1)}, f32[296,128]{1,0:T(8,128)S(1)}, u32[]{:S(2)}, u32[]{:S(2)}) collective-permute-start(f32[296,128]{1,0:T(8,128)S(1)} %shard_map.57.refs_0_.own), channel_id=1, source_target_pairs={{0,8},{4,12},{8,0},{12,4},{1,9},{5,13},{9,1},{13,5},{2,10},{6,14},... | collective-permute-start | bytes 454664 | tf_op jit(solution)/shard_map/ppermute | solution.py:283
  84.6 5.8 %collective-permute-start.10 = (f32[136,128]{1,0:T(8,128)S(1)}, f32[136,128]{1,0:T(8,128)S(1)}, u32[]{:S(2)}, u32[]{:S(2)}) collective-permute-start(f32[136,128]{1,0:T(8,128)S(1)} %get-tuple-element.15), channel_id=1, source_target_pairs={{0,1},{1,0},{2,3},{3,2},{4,5},{5,4},{6,7},{7,6},{8,9},{9,8},{10,11... | collective-permute-start | bytes 208904 | tf_op jit(solution)/shard_map/ppermute | solution.py:295
  86.5 6.2 %collective-permute-start.11 = (f32[136,128]{1,0:T(8,128)S(1)}, f32[136,128]{1,0:T(8,128)S(1)}, u32[]{:S(2)}, u32[]{:S(2)}) collective-permute-start(f32[136,128]{1,0:T(8,128)S(1)} %get-tuple-element.16), channel_id=1, source_target_pairs={{0,2},{1,15},{2,0},{3,5},{4,6},{5,3},{6,4},{7,9},{8,10},{9,7},{10,... | collective-permute-start | bytes 208904 | tf_op jit(solution)/shard_map/ppermute | solution.py:294
  88.4 6.9 %collective-permute-start.12 = (f32[136,128]{1,0:T(8,128)S(1)}, f32[136,128]{1,0:T(8,128)S(1)}, u32[]{:S(2)}, u32[]{:S(2)}) collective-permute-start(f32[136,128]{1,0:T(8,128)S(1)} %get-tuple-element.17), channel_id=1, source_target_pairs={{0,3},{1,14},{2,1},{3,4},{4,7},{5,2},{6,5},{7,8},{8,11},{9,6},{10,... | collective-permute-start | bytes 208904 | tf_op jit(solution)/shard_map/ppermute | solution.py:293

commit v4 on v0

v4 whole, which is shorter than its diff:
```python
import functools

import jax
import jax.numpy as jnp
from jax import lax
from jax.experimental import pallas as pl
from jax.experimental.pallas import tpu as pltpu
from jax.sharding import Mesh
from jax.sharding import PartitionSpec as P

F32 = jnp.float32
AXES = ("y", "x", "zh", "zl", "c")
WIDE = ("y", "x")
DEEP = ("zh", "zl", "c")
PARTS = 4
LIMIT = 48 * 1024 * 1024
EDGE = 65500000


def mult(left, right, contract=((1,), (0,))):
    return lax.dot_general(
        left, right, (contract, ((), ())),
        preferred_element_type=F32, precision=lax.Precision.HIGHEST,
    )


def whole(*shape):
    return jax.ShapeDtypeStruct(shape, F32)


def call(body, out_shape, *args, scalars=0):
    spaces = [pltpu.SMEM] * scalars + [pltpu.VMEM] * (len(args) - scalars)
    return pl.pallas_call(
        body,
        out_shape=out_shape,
        in_specs=[pl.BlockSpec(memory_space=space) for space in spaces],
        compiler_params=pltpu.CompilerParams(vmem_limit_bytes=LIMIT),
    )(*args)


def cut_body(tail, which, counts_ref, *refs):
    out_ref, held, sem = refs[-3:]
    rows, comps = held.shape
    copy = pltpu.make_async_copy(
        counts_ref.at[pl.ds(pl.multiple_of(which[0] * rows, rows), rows), :], held, sem
    )
    copy.start()
    if tail:
        loading_ref, offset_ref = refs[0:2]
        out_ref[rows : rows + comps, :] = loading_ref[...]
        out_ref[rows + comps : rows + comps + 8, :] = jnp.broadcast_to(offset_ref[...], (8, comps))
    copy.wait()
    out_ref[0:rows, :] = jnp.log(held[...])


def cut(which, counts, tail=()):
    rows, width = counts.shape[0] // 4, counts.shape[1]
    height = rows + (tail[0].shape[0] + 8 if tail else 0)
    return pl.pallas_call(
        functools.partial(cut_body, bool(tail)),
        out_shape=whole(height, width),
        in_specs=[pl.BlockSpec(memory_space=pltpu.SMEM), pl.BlockSpec(memory_space=pl.ANY)]
        + [pl.BlockSpec(memory_space=pltpu.VMEM)] * len(tail),
        scratch_shapes=[pltpu.VMEM((rows, width), F32), pltpu.SemaphoreType.DMA],
        compiler_params=pltpu.CompilerParams(vmem_limit_bytes=EDGE),
    )(which.reshape(1), counts, *tail)


def group_terms(sources, loads, offs):
    both = jnp.concatenate(loads, axis=0)
    bar = jnp.sum(both, axis=0, keepdims=True) / both.shape[0]
    gram = mult(both, both, ((0,), (0,)))
    shift = mult(jnp.concatenate(offs, axis=1), both)
    return bar, both - bar, shift[0:1, :], gram


def log_sums(a, b, at, comps):
    return jnp.sum((a[at : at + comps, :] + b[at : at + comps, :]).T, axis=0, keepdims=True)


def encode_body(keep, near, loading_ref, offset_ref, out_ref):
    total, comps = keep.shape
    rows, share = total // PARTS, comps // PARTS
    bar, bare, shift, gram = group_terms(
        (keep, near),
        (loading_ref[...], near[total : total + comps, :]),
        (jnp.broadcast_to(offset_ref[...], (8, comps)), near[total + comps : total + comps + 8, :]),
    )
    blank = jnp.zeros((1, comps), F32)
    for j in range(PARTS):
        a, b = keep[j * rows : (j + 1) * rows, :], near[j * rows : (j + 1) * rows, :]
        out_ref[j, 0:rows, :] = mult(jnp.concatenate([a, b], axis=1), bare)
        sums = [log_sums(a, b, h * comps, comps) for h in range(2)]
        out_ref[j, rows : rows + 8, :] = jnp.concatenate(
            [sums[0], blank, sums[1], blank, bar, blank, shift, blank], axis=0
        )
        out_ref[j, rows + 8 : rows + 8 + share, :] = gram[j * share : (j + 1) * share, :]


def encode_last_body(in_ref, cross, core, out_ref):
    height, comps = in_ref.shape[1:]
    share = comps // PARTS
    rows = height - 8 - share
    total = PARTS * rows
    bar, bare, shift, gram = group_terms(
        (core, cross),
        [a[total : total + comps, :] for a in (core, cross)],
        [a[total + comps : total + comps + 8, :] for a in (core, cross)],
    )
    blank = jnp.zeros((1, comps), F32)
    for j in range(PARTS):
        a, b = core[j * rows : (j + 1) * rows, :], cross[j * rows : (j + 1) * rows, :]
        out_ref[j, 0:rows, :] = in_ref[j, 0:rows, :] + mult(jnp.concatenate([a, b], axis=1), bare)
        sums = [log_sums(a, b, h * comps, comps) for h in range(2)]
        out_ref[j, rows : rows + 8, :] = in_ref[j, rows : rows + 8, :] + jnp.concatenate(
            [blank, sums[0], blank, sums[1], blank, bar, shift, blank], axis=0
        )
        at = rows + 8
        out_ref[j, at : at + share, :] = in_ref[j, at : at + share, :] + gram[j * share : (j + 1) * share, :]


def finish_body(channels, in_ref, out_ref):
    height, comps = in_ref.shape[1:]
    share = comps // PARTS
    rows = height - 8 - share
    group = channels // (2 * PARTS)
    bars = jnp.concatenate([in_ref[j, rows + 4 : rows + 6, :] for j in range(PARTS)], axis=0)
    shift = sum(in_ref[j, rows + 6 : rows + 7, :] for j in range(PARTS))
    geos = []
    for h in range(2):
        sums = jnp.concatenate(
            [in_ref[j, rows + 2 * h : rows + 2 * h + 2, :] for j in range(PARTS)], axis=0
        )
        geo = jnp.sum(sums, axis=0, keepdims=True) / channels
        at = h * comps
        total = mult(sums - group * geo, bars, ((0,), (0,))) - shift
        for j in range(PARTS):
            total += in_ref[j, at : at + comps, :]
        for j in range(PARTS):
            out_ref[j, at : at + comps, :] = total
        geos.append(geo)
    geos = jnp.concatenate(geos + [jnp.zeros((6, comps), F32)], axis=0)
    gram = sum(in_ref[j, rows + 8 : rows + 8 + share, :] for j in range(PARTS))
    for j in range(PARTS):
        out_ref[j, rows : rows + 8, :] = geos
        out_ref[j, rows + 8 : rows + 8 + share, :] = gram


def grad_body(in_ref, keep, core, near, cross, loading_ref, offset_ref, *outs):
    height, comps = in_ref.shape[1:]
    share = comps // PARTS
    rows = height - 8 - share
    total = PARTS * rows
    gram = jnp.concatenate([in_ref[j, rows + 8 : rows + 8 + share, :] for j in range(PARTS)], axis=0)
    row = lax.broadcasted_iota(jnp.int32, (comps, comps), 0)
    col = lax.broadcasted_iota(jnp.int32, (comps, comps), 1)
    hat = gram - jnp.where(row == col, 2.0, 0.0).astype(F32)
    logs = (keep, core, near, cross)
    loads = (loading_ref[...],) + tuple(a[total : total + comps, :] for a in logs[1:])
    offs = (offset_ref[...],) + tuple(a[total + comps : total + comps + 1, :] for a in logs[1:])
    wide = jnp.zeros((comps, 5 * comps), F32)
    sums = jnp.zeros((1, 5 * comps), F32)
    for j in range(PARTS):
        s = in_ref[j, 0:rows, :]
        geo = jnp.concatenate(
            [
                jnp.broadcast_to(in_ref[j, rows + h : rows + h + 1, :], (comps, comps)).T
                for h in range(2)
            ],
            axis=0,
        )
        both = [a[j * rows : (j + 1) * rows, :] - geo - off for a, off in zip(logs, offs)]
        both = jnp.concatenate(both + [s], axis=1)
        sums += jnp.sum(both, axis=0, keepdims=True)
        wide += mult(s.T, both)
    square = wide[:, 4 * comps : 5 * comps]
    s_hat = mult(jnp.broadcast_to(sums[:, 4 * comps : 5 * comps], (8, comps)), hat)
    for k, out in enumerate(outs):
        here = slice(k * comps, (k + 1) * comps)
        out[0:comps, :] = mult(wide[:, here], hat, ((0,), (0,))) + mult(loads[k], square)
        out[comps : comps + 8, :] = -(mult(s_hat, loads[k], ((1,), (1,))) + sums[:, here])


def deal_body(a_ref, b_ref, c_ref, d_ref, out_ref):
    pieces, _, comps = out_ref.shape
    share = comps // pieces
    total = a_ref[...] + b_ref[...] + c_ref[...] + d_ref[...]
    for p in range(pieces):
        out_ref[p, 0:share, :] = total[p * share : (p + 1) * share, :]
        out_ref[p, share:8, :] = total[comps : comps + 8 - share, :]


def gather_body(pixels, in_ref, out_ref):
    total = jnp.sum(in_ref[...], axis=0) / pixels
    for j in range(out_ref.shape[0]):
        out_ref[j] = total


def last_body(in_ref, load_ref, off_ref):
    pieces = in_ref.shape[0]
    share = load_ref.shape[0] // pieces
    for p in range(pieces):
        load_ref[p * share : (p + 1) * share, :] = in_ref[p, 0:share, :]
    off_ref[...] = in_ref[0, share : share + 1, :]


def on_device(counts, offset, loading):
    pixels = counts.shape[0] * lax.axis_size(WIDE)
    comps = loading.shape[1]
    channels = counts.shape[1] * PARTS * 4
    height = counts.shape[0] // 4 // PARTS + 8 + comps // PARTS
    core = lax.axis_index("c").astype(jnp.int32)
    side = lax.axis_index("zl").astype(jnp.int32)
    offset = offset.reshape(1, comps)

    swap = [(0, 1), (1, 0)]
    near_pairs, cross_pairs = [], []
    for z in range(2 * PARTS):
        for c in range(2):
            partner = (((z - c) % (2 * PARTS) ^ 1) + c) % (2 * PARTS)
            near_pairs.append((2 * z + c, 2 * partner + c))
            cross_pairs.append((2 * z + c, 2 * partner + 1 - c))
    back_pairs = [(b, a) for a, b in cross_pairs]

    tail = (loading, offset)
    near_out = cut(2 * core + 1 - side, counts, tail)
    cross_out = cut(2 * (1 - core) + 1 - side, counts, tail)
    core_out = cut(2 * (1 - core) + side, counts, tail)
    keep = cut(2 * core + side, counts)
    near = lax.ppermute(near_out, DEEP, near_pairs)
    cross = lax.ppermute(cross_out, DEEP, back_pairs)
    other = lax.ppermute(core_out, "c", swap)
    block = whole(PARTS, height, comps)
    partial = call(encode_body, block, keep, near, loading, offset)
    partial = call(encode_last_body, block, partial, cross, other)
    gathered = lax.all_to_all(partial, "zh", 0, 0)
    copies = call(functools.partial(finish_body, channels), block, gathered)
    scores = lax.all_to_all(copies, "zh", 0, 0)
    shape = whole(comps + 8, comps)
    mine, to_core, to_near, to_cross = call(
        grad_body, (shape,) * 4, scores, keep, other, near, cross, loading, offset
    )
    crossed = lax.ppermute(to_cross, DEEP, cross_pairs)
    neared = lax.ppermute(to_near, DEEP, near_pairs)
    cored = lax.ppermute(to_core, "c", swap)
    plane = lax.axis_size(WIDE)
    pieces = call(deal_body, whole(plane, 8, comps), mine, cored, neared, crossed)
    pieces = lax.all_to_all(pieces, WIDE, 0, 0)
    pieces = call(functools.partial(gather_body, pixels), whole(plane, 8, comps), pieces)
    pieces = lax.all_to_all(pieces, WIDE, 0, 0)
    grad, grad_offset = call(last_body, (whole(comps, comps), whole(1, comps)), pieces)
    return grad, grad_offset.reshape(comps)


def solution(mesh):
    wide, deep = mesh.devices.shape
    split_mesh = Mesh(mesh.devices.reshape(wide // 4, 4, deep // 4, 2, 2), AXES)
    return jax.shard_map(
        on_device,
        mesh=split_mesh,
        in_specs=(P(WIDE, DEEP), P(DEEP), P(DEEP, None)),
        out_specs=(P(DEEP, None), P(DEEP)),
        check_vma=False,
    )
```

time: 552 us -> 124 us (0.22)
  waiting for transfers between devices: 383 us -> 3.9 us
  blocking collectives: 123 us -> 76.1 us
  matrix products: 26.1 us -> 0 us
  starting transfers between devices: 0.3 us -> 22.2 us
  Pallas kernels: 0 us -> 18.9 us
  between operations: 13.8 us -> 0.85 us
    psum x3 -> x0, waiting for transfers between devices: 383 us -> none  [the longest x1 150 us: on_device(): load_sum, offset_sum = lax.psum((load_term, offset_term), 'pix')]
    psum x2 -> x0, blocking collectives: 123 us -> none  [the longest x1 68.5 us: on_device(): load_sum, offset_sum = lax.psum((load_term, offset_term), 'pix')]
    all_to_all x0 -> x4, blocking collectives: none -> 76.1 us  [the longest x2 33.3 us: on_device(): pieces = lax.all_to_all(pieces, WIDE, 0, 0)]
    dot_general x6 -> x0, matrix products: 26.1 us -> none  [mult(): jnp.dot(left, right, preferred_element_type=jnp.float32, precision=lax.Pr...]
    ppermute x0 -> x6, starting transfers between devices: none -> 22.2 us  [the longest x1 8.03 us: on_device(): cross = lax.ppermute(cross_out, DEEP, back_pairs)]
    pallas_call x0 -> x11, Pallas kernels: none -> 18.9 us  [the longest x4 10.4 us: cut(): pl.pallas_call(functools.partial(cut_body, bool(tail)), out_shape=whole(h...]
  transfers between devices with their start and end apart: 3 -> 6, of which waited for: 3 -> 2; matrix products, arithmetic and copies ran while one was open for 1% -> 0% of each run, Pallas kernels for 0% -> 7%
where the time goes in v4:
time: 124 us; the launch traced here: 123 us
  blocking collectives  76.1 us (61%)
  starting transfers between devices  22.2 us (18%)
  Pallas kernels  18.9 us (15%)
  waiting for transfers between devices  3.9 us (3%)
    all_to_all x2, blocking collectives, on_device(): pieces = lax.all_to_all(pieces, WIDE, 0, 0)  33.3 us
    all_to_all x1, blocking collectives, on_device(): gathered = lax.all_to_all(partial, 'zh', 0, 0)  23.7 us
    all_to_all x1, blocking collectives, on_device(): scores = lax.all_to_all(copies, 'zh', 0, 0)  19.1 us
    pallas_call x4, Pallas kernels, cut(): pl.pallas_call(functools.partial(cut_body, bool(tail)), out_shape=whole(h...  10.4 us
    pallas_call x7, Pallas kernels, call(): pl.pallas_call(body, out_shape=out_shape, in_specs=[pl.BlockSpec(memory_s...  8.54 us
    ppermute x1, starting transfers between devices, on_device(): cross = lax.ppermute(cross_out, DEEP, back_pairs)  8.03 us
    ppermute x1, starting transfers between devices, on_device(): near = lax.ppermute(near_out, DEEP, near_pairs)  4.28 us
    ppermute x1, waiting for transfers between devices, on_device(): crossed = lax.ppermute(to_cross, DEEP, cross_pairs)  3.66 us
  transfers between devices with their start and end apart: 6, of which 2 were waited for; matrix products, arithmetic and copies ran while one was open for 0% of the time, Pallas kernels for 7%

profile of v4, /device:TPU:8, one launch (start us, length us, event | category | flops | bytes accessed | tf_op | source)
XLA Modules:
  0.0 123.0 jit_solution(439034933783178009)
XLA Ops:
  0.6 2.8 %shard_map.51 = f32[1160,128]{1,0:T(8,128)} custom-call(s32[1]{0:T(128)} %bitcast.1.which, f32[4096,128]{1,0:T(8,128)} %counts_ref.7, f32[128,128]{1,0:T(8,128)} %loading_ref.3, f32[1,128]{1,0:T(1,128)} %bitcast.6), custom_call_target="tpu_custom_call" | custom-call | tf_op jit(solution)/shard_map/pallas_call | solution.py:59
  3.4 4.3 %collective-permute-start = (f32[1160,128]{1,0:T(8,128)}, f32[1160,128]{1,0:T(8,128)S(1)}, u32[]{:S(2)}, u32[]{:S(2)}) collective-permute-start(f32[1160,128]{1,0:T(8,128)} %shard_map.51), channel_id=1, source_target_pairs={{0,2},{1,15},{2,0},{3,5},{4,6},{5,3},{6,4},{7,9},{8,10},{9,7},{10,... | collective-permute-start | bytes 1781768 | tf_op jit(solution)/shard_map/ppermute | solution.py:230
  7.7 2.8 %shard_map.53 = f32[1160,128]{1,0:T(8,128)} custom-call(s32[1]{0:T(128)} %bitcast.3.which, f32[4096,128]{1,0:T(8,128)} %counts_ref.7, f32[128,128]{1,0:T(8,128)} %loading_ref.3, f32[1,128]{1,0:T(1,128)} %bitcast.7), custom_call_target="tpu_custom_call" | custom-call | tf_op jit(solution)/shard_map/pallas_call | solution.py:59
  10.5 8.0 %collective-permute-start.1 = (f32[1160,128]{1,0:T(8,128)}, f32[1160,128]{1,0:T(8,128)S(1)}, u32[]{:S(2)}, u32[]{:S(2)}) collective-permute-start(f32[1160,128]{1,0:T(8,128)} %shard_map.53), channel_id=1, source_target_pairs={{3,0},{14,1},{1,2},{4,3},{7,4},{2,5},{5,6},{8,7},{11,8},{6,9},{9,1... | collective-permute-start | bytes 1781768 | tf_op jit(solution)/shard_map/ppermute | solution.py:231
  18.6 0.0 copy-start.2
  18.6 0.0 copy-start.3
  18.6 2.8 %shard_map.54 = f32[1160,128]{1,0:T(8,128)} custom-call(s32[1]{0:T(128)} %bitcast.4.which, f32[4096,128]{1,0:T(8,128)} %counts_ref.7, f32[128,128]{1,0:T(8,128)} %loading_ref.3, f32[1,128]{1,0:T(1,128)} %bitcast.8), custom_call_target="tpu_custom_call" | custom-call | tf_op jit(solution)/shard_map/pallas_call | solution.py:59
  21.4 2.0 %collective-permute-start.2 = (f32[1160,128]{1,0:T(8,128)}, f32[1160,128]{1,0:T(8,128)}, u32[]{:S(2)}, u32[]{:S(2)}) collective-permute-start(f32[1160,128]{1,0:T(8,128)} %shard_map.54), channel_id=1, source_target_pairs={{0,1},{1,0},{2,3},{3,2},{4,5},{5,4},{6,7},{7,6},{8,9},{9,8},{10,11... | collective-permute-start | bytes 1781768 | tf_op jit(solution)/shard_map/ppermute | solution.py:232
  23.5 1.9 %shard_map.50.keep = f32[1024,128]{1,0:T(8,128)} custom-call(s32[1]{0:T(128)} %bitcast.which, f32[4096,128]{1,0:T(8,128)} %counts_ref.7), custom_call_target="tpu_custom_call" | custom-call | tf_op jit(solution)/shard_map/pallas_call | solution.py:59
  25.5 1.0 copy-done
  26.5 1.2 %shard_map.52.in_ref = f32[4,296,128]{2,1,0:T(8,128)S(1)} custom-call(f32[1024,128]{1,0:T(8,128)S(1)} %copy-done, f32[1160,128]{1,0:T(8,128)S(1)} %collective-permute-done.near, f32[128,128]{1,0:T(8,128)S(1)} %copy-done.2, f32[1,128]{1,0:T(1,128)S(1)} %bitcast.9), custom_call_target="tpu_custom_call" | custom-call | tf_op jit(solution)/shard_map/pallas_call | solution.py:33
  27.8 2.3 %shard_map.55 = f32[4,296,128]{2,1,0:T(8,128)S(1)} custom-call(f32[4,296,128]{2,1,0:T(8,128)S(1)} %shard_map.52.in_ref, f32[1160,128]{1,0:T(8,128)S(1)} %collective-permute-done.1.cross, f32[1160,128]{1,0:T(8,128)} %collective-permute-done.2.core), custom_call_target="tpu_custom_call" | custom-call | tf_op jit(solution)/shard_map/pallas_call | solution.py:33
  30.1 23.7 %all_to_all.20.in_ref = f32[4,296,128]{2,1,0:T(8,128)S(1)} all-to-all(f32[4,296,128]{2,1,0:T(8,128)S(1)} %shard_map.55), channel_id=1, replica_groups=mesh['y'=8,'x'=4,'zh'=4,'zl'=2,'c'=2] {'zh'}, dimensions={0} | all-to-all | bytes 1212416 | tf_op jit(solution)/shard_map/all_to_all | solution.py:236
  53.8 0.4 shard_map.56
  54.2 19.1 %all_to_all.21.in_ref = f32[4,296,128]{2,1,0:T(8,128)S(1)} all-to-all(f32[4,296,128]{2,1,0:T(8,128)S(1)} %shard_map.56), channel_id=1, replica_groups=mesh['y'=8,'x'=4,'zh'=4,'zl'=2,'c'=2] {'zh'}, dimensions={0} | all-to-all | bytes 1212416 | tf_op jit(solution)/shard_map/all_to_all | solution.py:238
  73.3 3.9 %shard_map.57 = (f32[136,128]{1,0:T(8,128)S(1)}, f32[136,128]{1,0:T(8,128)S(1)}, f32[136,128]{1,0:T(8,128)S(1)}, f32[136,128]{1,0:T(8,128)S(1)}) custom-call(f32[4,296,128]{2,1,0:T(8,128)S(1)} %all_to_all.21.in_ref, f32[1024,128]{1,0:T(8,128)S(1)} %copy-done.1, f32[1160,128]{1,0:T(8,128)} %collective-permute-done.2.core, ...), custom_call_target="tpu_custom_call" | custom-call | tf_op jit(solution)/shard_map/pallas_call | solution.py:33
  77.2 1.9 %collective-permute-start.3 = (f32[136,128]{1,0:T(8,128)S(1)}, f32[136,128]{1,0:T(8,128)S(1)}, u32[]{:S(2)}, u32[]{:S(2)}) collective-permute-start(f32[136,128]{1,0:T(8,128)S(1)} %get-tuple-element.9), channel_id=1, source_target_pairs={{0,1},{1,0},{2,3},{3,2},{4,5},{5,4},{6,7},{7,6},{8,9},{9,8},{10,11... | collective-permute-start | bytes 208904 | tf_op jit(solution)/shard_map/ppermute | solution.py:245
  79.2 3.0 %collective-permute-start.4 = (f32[136,128]{1,0:T(8,128)S(1)}, f32[136,128]{1,0:T(8,128)S(1)}, u32[]{:S(2)}, u32[]{:S(2)}) collective-permute-start(f32[136,128]{1,0:T(8,128)S(1)} %get-tuple-element.10), channel_id=1, source_target_pairs={{0,2},{1,15},{2,0},{3,5},{4,6},{5,3},{6,4},{7,9},{8,10},{9,7},{10,... | collective-permute-start | bytes 208904 | tf_op jit(solution)/shard_map/ppermute | solution.py:244
  82.2 2.9 %collective-permute-start.5 = (f32[136,128]{1,0:T(8,128)S(1)}, f32[136,128]{1,0:T(8,128)S(1)}, u32[]{:S(2)}, u32[]{:S(2)}) collective-permute-start(f32[136,128]{1,0:T(8,128)S(1)} %get-tuple-element.11), channel_id=1, source_target_pairs={{0,3},{1,14},{2,1},{3,4},{4,7},{5,2},{6,5},{7,8},{8,11},{9,6},{10,... | collective-permute-start | bytes 208904 | tf_op jit(solution)/shard_map/ppermute | solution.py:243
  85.1 0.2 collective-permute-done.4.c_ref
  85.4 3.7 %collective-permute-done.5.d_ref = f32[136,128]{1,0:T(8,128)S(1)} collective-permute-done((f32[136,128]{1,0:T(8,128)S(1)}, f32[136,128]{1,0:T(8,128)S(1)}, u32[]{:S(2)}, u32[]{:S(2)}) %collective-permute-start.5) | collective-permute-done | bytes 69664 | tf_op jit(solution)/shard_map/ppermute | solution.py:243
  89.0 19.5 %all_to_all.22.in_ref = f32[32,8,128]{2,1,0:T(8,128)S(1)} all-to-all(f32[32,8,128]{2,1,0:T(8,128)S(1)} %shard_map.58), channel_id=1, replica_groups=mesh['y'=8,'x'=4,'zh'=4,'zl'=2,'c'=2] {'y','x'}, dimensions={0} | all-to-all | bytes 262144 | tf_op jit(solution)/shard_map/all_to_all | solution.py:248
  108.6 13.8 %all_to_all.23.in_ref = f32[32,8,128]{2,1,0:T(8,128)S(1)} all-to-all(f32[32,8,128]{2,1,0:T(8,128)S(1)} %shard_map.59), channel_id=1, replica_groups=mesh['y'=8,'x'=4,'zh'=4,'zl'=2,'c'=2] {'y','x'}, dimensions={0} | all-to-all | bytes 262144 | tf_op jit(solution)/shard_map/all_to_all | solution.py:250
  122.4 0.6 shard_map.60
  (11 shorter events, 0.1 us)
Async XLA Ops:
  3.4 22.0 %collective-permute-start = (f32[1160,128]{1,0:T(8,128)}, f32[1160,128]{1,0:T(8,128)S(1)}, u32[]{:S(2)}, u32[]{:S(2)}) collective-permute-start(f32[1160,128]{1,0:T(8,128)} %shard_map.51), channel_id=1, source_target_pairs={{0,2},{1,15},{2,0},{3,5},{4,6},{5,3},{6,4},{7,9},{8,10},{9,7},{10,... | collective-permute-start | bytes 1781768 | tf_op jit(solution)/shard_map/ppermute | solution.py:230
  10.5 17.2 %collective-permute-start.1 = (f32[1160,128]{1,0:T(8,128)}, f32[1160,128]{1,0:T(8,128)S(1)}, u32[]{:S(2)}, u32[]{:S(2)}) collective-permute-start(f32[1160,128]{1,0:T(8,128)} %shard_map.53), channel_id=1, source_target_pairs={{3,0},{14,1},{1,2},{4,3},{7,4},{2,5},{5,6},{8,7},{11,8},{6,9},{9,1... | collective-permute-start | bytes 1781768 | tf_op jit(solution)/shard_map/ppermute | solution.py:231
  18.6 6.9 %copy-start.2 = (f32[128,128]{1,0:T(8,128)S(1)}, f32[128,128]{1,0:T(8,128)}, u32[]{:S(2)}) copy-start(f32[128,128]{1,0:T(8,128)} %loading_ref.3) | copy-start | bytes 196612
  18.6 6.9 %copy-start.3 = (f32[128]{0:T(128)S(1)}, f32[128]{0:T(128)}, u32[]{:S(2)}) copy-start(f32[128]{0:T(128)} %param.4) | copy-start | bytes 1540
  21.4 6.3 %collective-permute-start.2 = (f32[1160,128]{1,0:T(8,128)}, f32[1160,128]{1,0:T(8,128)}, u32[]{:S(2)}, u32[]{:S(2)}) collective-permute-start(f32[1160,128]{1,0:T(8,128)} %shard_map.54), channel_id=1, source_target_pairs={{0,1},{1,0},{2,3},{3,2},{4,5},{5,4},{6,7},{7,6},{8,9},{9,8},{10,11... | collective-permute-start | bytes 1781768 | tf_op jit(solution)/shard_map/ppermute | solution.py:232
  25.5 1.0 copy-start
  30.1 43.2 %copy-start.1 = (f32[1024,128]{1,0:T(8,128)S(1)}, f32[1024,128]{1,0:T(8,128)}, u32[]{:S(2)}) copy-start(f32[1024,128]{1,0:T(8,128)} %shard_map.50.keep) | copy-start | bytes 1572868
  77.2 7.9 %collective-permute-start.3 = (f32[136,128]{1,0:T(8,128)S(1)}, f32[136,128]{1,0:T(8,128)S(1)}, u32[]{:S(2)}, u32[]{:S(2)}) collective-permute-start(f32[136,128]{1,0:T(8,128)S(1)} %get-tuple-element.9), channel_id=1, source_target_pairs={{0,1},{1,0},{2,3},{3,2},{4,5},{5,4},{6,7},{7,6},{8,9},{9,8},{10,11... | collective-permute-start | bytes 208904 | tf_op jit(solution)/shard_map/ppermute | solution.py:245
  79.2 6.2 %collective-permute-start.4 = (f32[136,128]{1,0:T(8,128)S(1)}, f32[136,128]{1,0:T(8,128)S(1)}, u32[]{:S(2)}, u32[]{:S(2)}) collective-permute-start(f32[136,128]{1,0:T(8,128)S(1)} %get-tuple-element.10), channel_id=1, source_target_pairs={{0,2},{1,15},{2,0},{3,5},{4,6},{5,3},{6,4},{7,9},{8,10},{9,7},{10,... | collective-permute-start | bytes 208904 | tf_op jit(solution)/shard_map/ppermute | solution.py:244
  82.2 6.8 %collective-permute-start.5 = (f32[136,128]{1,0:T(8,128)S(1)}, f32[136,128]{1,0:T(8,128)S(1)}, u32[]{:S(2)}, u32[]{:S(2)}) collective-permute-start(f32[136,128]{1,0:T(8,128)S(1)} %get-tuple-element.11), channel_id=1, source_target_pairs={{0,3},{1,14},{2,1},{3,4},{4,7},{5,2},{6,5},{7,8},{8,11},{9,6},{10,... | collective-permute-start | bytes 208904 | tf_op jit(solution)/shard_map/ppermute | solution.py:243

commit v5 on v4

--- a/solution.py
+++ b/solution.py
@@ -14,7 +14,7 @@
 DEEP = ("zh", "zl", "c")
 PARTS = 4
 LIMIT = 48 * 1024 * 1024
-EDGE = 65500000
+EDGE = 53500000
 
 
 def mult(left, right, contract=((1,), (0,))):
@@ -38,32 +38,45 @@
     )(*args)
 
 
-def cut_body(tail, which, counts_ref, *refs):
-    out_ref, held, sem = refs[-3:]
-    rows, comps = held.shape
-    copy = pltpu.make_async_copy(
-        counts_ref.at[pl.ds(pl.multiple_of(which[0] * rows, rows), rows), :], held, sem
-    )
-    copy.start()
-    if tail:
-        loading_ref, offset_ref = refs[0:2]
-        out_ref[rows : rows + comps, :] = loading_ref[...]
-        out_ref[rows + comps : rows + comps + 8, :] = jnp.broadcast_to(offset_ref[...], (8, comps))
-    copy.wait()
-    out_ref[0:rows, :] = jnp.log(held[...])
-
-
-def cut(which, counts, tail=()):
+def split_body(which, counts_ref, loading_ref, offset_ref, keep, core, near, cross, held, row, sems):
+    rows, comps = keep.shape
+    outs = (near, cross, core, keep)
+    copies = [
+        pltpu.make_async_copy(
+            counts_ref.at[pl.ds(pl.multiple_of(which[k] * rows, rows), rows), :], held.at[k], sems.at[k]
+        )
+        for k in range(4)
+    ]
+    loads = [
+        pltpu.make_async_copy(loading_ref, outs[k].at[pl.ds(rows, comps), :], sems.at[4 + k])
+        for k in range(3)
+    ]
+    short = pltpu.make_async_copy(offset_ref, row, sems.at[7])
+    for copy in copies + loads + [short]:
+        copy.start()
+    for k in range(4):
+        copies[k].wait()
+        outs[k][0:rows, :] = jnp.log(held[k])
+    short.wait()
+    for k in range(3):
+        loads[k].wait()
+        outs[k][rows + comps : rows + comps + 8, :] = jnp.broadcast_to(row[...], (8, comps))
+
+
+def split(which, counts, loading, offset):
     rows, width = counts.shape[0] // 4, counts.shape[1]
-    height = rows + (tail[0].shape[0] + 8 if tail else 0)
+    more = rows + loading.shape[0] + 8
     return pl.pallas_call(
-        functools.partial(cut_body, bool(tail)),
-        out_shape=whole(height, width),
-        in_specs=[pl.BlockSpec(memory_space=pltpu.SMEM), pl.BlockSpec(memory_space=pl.ANY)]
-        + [pl.BlockSpec(memory_space=pltpu.VMEM)] * len(tail),
-        scratch_shapes=[pltpu.VMEM((rows, width), F32), pltpu.SemaphoreType.DMA],
+        split_body,
+        out_shape=(whole(rows, width),) + (whole(more, width),) * 3,
+        in_specs=[pl.BlockSpec(memory_space=pltpu.SMEM)] + [pl.BlockSpec(memory_space=pltpu.HBM)] * 3,
+        scratch_shapes=[
+            pltpu.VMEM((4, rows, width), F32),
+            pltpu.VMEM((1, width), F32),
+            pltpu.SemaphoreType.DMA((8,)),
+        ],
         compiler_params=pltpu.CompilerParams(vmem_limit_bytes=EDGE),
-    )(which.reshape(1), counts, *tail)
+    )(which, counts, loading, offset)
 
 
 def group_terms(sources, loads, offs):
@@ -103,13 +116,13 @@
     rows = height - 8 - share
     total = PARTS * rows
     bar, bare, shift, gram = group_terms(
-        (core, cross),
-        [a[total : total + comps, :] for a in (core, cross)],
-        [a[total + comps : total + comps + 8, :] for a in (core, cross)],
+        (cross, core),
+        [a[total : total + comps, :] for a in (cross, core)],
+        [a[total + comps : total + comps + 8, :] for a in (cross, core)],
     )
     blank = jnp.zeros((1, comps), F32)
     for j in range(PARTS):
-        a, b = core[j * rows : (j + 1) * rows, :], cross[j * rows : (j + 1) * rows, :]
+        a, b = cross[j * rows : (j + 1) * rows, :], core[j * rows : (j + 1) * rows, :]
         out_ref[j, 0:rows, :] = in_ref[j, 0:rows, :] + mult(jnp.concatenate([a, b], axis=1), bare)
         sums = [log_sums(a, b, h * comps, comps) for h in range(2)]
         out_ref[j, rows : rows + 8, :] = in_ref[j, rows : rows + 8, :] + jnp.concatenate(
@@ -146,7 +159,7 @@
         out_ref[j, rows + 8 : rows + 8 + share, :] = gram
 
 
-def grad_body(in_ref, keep, core, near, cross, loading_ref, offset_ref, *outs):
+def grad_body(in_ref, keep, core, near, cross, loading_ref, offset_ref, out_ref):
     height, comps = in_ref.shape[1:]
     share = comps // PARTS
     rows = height - 8 - share
@@ -175,23 +188,32 @@
         wide += mult(s.T, both)
     square = wide[:, 4 * comps : 5 * comps]
     s_hat = mult(jnp.broadcast_to(sums[:, 4 * comps : 5 * comps], (8, comps)), hat)
+    pieces = out_ref.shape[0]
+    cut = comps // pieces
+    lines = []
+    for k in range(4):
+        here = slice(k * comps, (k + 1) * comps)
+        grad = mult(wide[:, here], hat, ((0,), (0,))) + mult(loads[k], square)
+        for p in range(pieces):
+            out_ref[p, k * cut : (k + 1) * cut, :] = grad[p * cut : (p + 1) * cut, :]
+        lines.append(-(mult(s_hat, loads[k], ((1,), (1,)))[0:1, :] + sums[:, here]))
+    lines = jnp.concatenate(lines + lines, axis=0)
+    for p in range(pieces):
+        out_ref[p, 4 * cut : 4 * cut + 8, :] = lines
+
+
+def deal_body(in_ref, *outs):
+    total = jnp.sum(in_ref[...], axis=0)
+    cut = (total.shape[0] - 8) // 4
     for k, out in enumerate(outs):
-        here = slice(k * comps, (k + 1) * comps)
-        out[0:comps, :] = mult(wide[:, here], hat, ((0,), (0,))) + mult(loads[k], square)
-        out[comps : comps + 8, :] = -(mult(s_hat, loads[k], ((1,), (1,))) + sums[:, here])
-
-
-def deal_body(a_ref, b_ref, c_ref, d_ref, out_ref):
-    pieces, _, comps = out_ref.shape
-    share = comps // pieces
-    total = a_ref[...] + b_ref[...] + c_ref[...] + d_ref[...]
-    for p in range(pieces):
-        out_ref[p, 0:share, :] = total[p * share : (p + 1) * share, :]
-        out_ref[p, share:8, :] = total[comps : comps + 8 - share, :]
-
-
-def gather_body(pixels, in_ref, out_ref):
-    total = jnp.sum(in_ref[...], axis=0) / pixels
+        line = total[4 * cut + k : 4 * cut + k + 1, :]
+        out[...] = jnp.concatenate(
+            [total[k * cut : (k + 1) * cut, :], jnp.broadcast_to(line, (8 - cut, line.shape[1]))], axis=0
+        )
+
+
+def gather_body(pixels, a_ref, b_ref, c_ref, d_ref, out_ref):
+    total = (a_ref[...] + b_ref[...] + c_ref[...] + d_ref[...]) / pixels
     for j in range(out_ref.shape[0]):
         out_ref[j] = total
 
@@ -222,11 +244,10 @@
             cross_pairs.append((2 * z + c, 2 * partner + 1 - c))
     back_pairs = [(b, a) for a, b in cross_pairs]
 
-    tail = (loading, offset)
-    near_out = cut(2 * core + 1 - side, counts, tail)
-    cross_out = cut(2 * (1 - core) + 1 - side, counts, tail)
-    core_out = cut(2 * (1 - core) + side, counts, tail)
-    keep = cut(2 * core + side, counts)
+    which = jnp.stack(
+        [2 * core + 1 - side, 2 * (1 - core) + 1 - side, 2 * (1 - core) + side, 2 * core + side]
+    )
+    keep, core_out, near_out, cross_out = split(which, counts, loading, offset)
     near = lax.ppermute(near_out, DEEP, near_pairs)
     cross = lax.ppermute(cross_out, DEEP, back_pairs)
     other = lax.ppermute(core_out, "c", swap)
@@ -236,17 +257,17 @@
     gathered = lax.all_to_all(partial, "zh", 0, 0)
     copies = call(functools.partial(finish_body, channels), block, gathered)
     scores = lax.all_to_all(copies, "zh", 0, 0)
-    shape = whole(comps + 8, comps)
-    mine, to_core, to_near, to_cross = call(
-        grad_body, (shape,) * 4, scores, keep, other, near, cross, loading, offset
-    )
+    plane = lax.axis_size(WIDE)
+    pieces = whole(plane, 4 * comps // plane + 8, comps)
+    pieces = call(grad_body, pieces, scores, keep, other, near, cross, loading, offset)
+    pieces = lax.all_to_all(pieces, WIDE, 0, 0)
+    mine, to_core, to_near, to_cross = call(deal_body, (whole(8, comps),) * 4, pieces)
     crossed = lax.ppermute(to_cross, DEEP, cross_pairs)
     neared = lax.ppermute(to_near, DEEP, near_pairs)
     cored = lax.ppermute(to_core, "c", swap)
-    plane = lax.axis_size(WIDE)
-    pieces = call(deal_body, whole(plane, 8, comps), mine, cored, neared, crossed)
-    pieces = lax.all_to_all(pieces, WIDE, 0, 0)
-    pieces = call(functools.partial(gather_body, pixels), whole(plane, 8, comps), pieces)
+    pieces = call(
+        functools.partial(gather_body, pixels), whole(plane, 8, comps), mine, cored, neared, crossed
+    )
     pieces = lax.all_to_all(pieces, WIDE, 0, 0)
     grad, grad_offset = call(last_body, (whole(comps, comps), whole(1, comps)), pieces)
     return grad, grad_offset.reshape(comps)

time: 124 us -> 126 us (1.016)
  Pallas kernels: 18.9 us -> 8.6 us
  waiting for transfers between devices: 3.9 us -> 12.1 us
  blocking collectives: 76.1 us -> 79.3 us
    pallas_call x4 -> x1, Pallas kernels: 10.4 us -> 2.21 us  [split(): pl.pallas_call(split_body, out_shape=(whole(rows, width),) + (whole(more,...]
    ppermute x1, waiting for transfers between devices: 0.01 us -> 7.21 us  [on_device(): cross = lax.ppermute(cross_out, DEEP, back_pairs)]
    all_to_all x2, blocking collectives: 33.3 us -> 36.4 us  [on_device(): pieces = lax.all_to_all(pieces, WIDE, 0, 0)]
    pallas_call x7, Pallas kernels: 8.54 us -> 6.39 us  [call(): pl.pallas_call(body, out_shape=out_shape, in_specs=[pl.BlockSpec(memory_s...]
    ppermute x1, starting transfers between devices: 3.01 us -> 4.65 us  [on_device(): neared = lax.ppermute(to_near, DEEP, near_pairs)]
  transfers between devices with their start and end apart: 6 -> 6, of which waited for: 2 -> 3; matrix products, arithmetic and copies ran while one was open for 0% -> 0% of each run, Pallas kernels for 7% -> 1%
where the time goes in v5:
time: 126 us; the launch traced here: 125 us
  blocking collectives  79.3 us (63%)
  starting transfers between devices  22.9 us (18%)
  waiting for transfers between devices  12.1 us (10%)
  Pallas kernels  8.6 us (7%)
  local copies, waits for them, and re-layouts  1.51 us (1%)
    all_to_all x2, blocking collectives, on_device(): pieces = lax.all_to_all(pieces, WIDE, 0, 0)  36.4 us
    all_to_all x1, blocking collectives, on_device(): gathered = lax.all_to_all(partial, 'zh', 0, 0)  23.9 us
    all_to_all x1, blocking collectives, on_device(): scores = lax.all_to_all(copies, 'zh', 0, 0)  19.1 us
    ppermute x1, starting transfers between devices, on_device(): cross = lax.ppermute(cross_out, DEEP, back_pairs)  8.03 us
    ppermute x1, waiting for transfers between devices, on_device(): cross = lax.ppermute(cross_out, DEEP, back_pairs)  7.21 us
    pallas_call x7, Pallas kernels, call(): pl.pallas_call(body, out_shape=out_shape, in_specs=[pl.BlockSpec(memory_s...  6.39 us
    ppermute x1, starting transfers between devices, on_device(): neared = lax.ppermute(to_near, DEEP, near_pairs)  4.65 us
    ppermute x1, starting transfers between devices, on_device(): near = lax.ppermute(near_out, DEEP, near_pairs)  4.28 us
  transfers between devices with their start and end apart: 6, of which 3 were waited for; matrix products, arithmetic and copies ran while one was open for 0% of the time, Pallas kernels for 1%

profile of v5, /device:TPU:8, one launch (start us, length us, event | category | flops | bytes accessed | tf_op | source)
XLA Modules:
  0.0 125.3 jit_solution(15076805710504182114)
XLA Ops:
  0.6 0.1 pad_add_fusion.which
  0.7 0.8 copy-done
  1.6 0.7 copy-done.2
  2.2 2.2 %shard_map.50 = (f32[1024,128]{1,0:T(8,128)S(1)}, f32[1160,128]{1,0:T(8,128)S(1)}, f32[1160,128]{1,0:T(8,128)S(1)}, f32[1160,128]{1,0:T(8,128)S(1)}) custom-call(s32[4]{0:T(128)S(1)} %pad_add_fusion.which, f32[4096,128]{1,0:T(8,128)} %counts_ref.1, f32[128,128]{1,0:T(8,128)S(1)} %copy-done, f32[1,128]{1,0:T(1,128)S(1)} %bitcast.6), custom_call_target="tpu_custom_call" | custom-call | tf_op jit(solution)/shard_map/pallas_call | solution.py:69
  4.4 4.3 %collective-permute-start = (f32[1160,128]{1,0:T(8,128)S(1)}, f32[1160,128]{1,0:T(8,128)S(1)}, u32[]{:S(2)}, u32[]{:S(2)}) collective-permute-start(f32[1160,128]{1,0:T(8,128)S(1)} %get-tuple-element.13), channel_id=1, source_target_pairs={{0,2},{1,15},{2,0},{3,5},{4,6},{5,3},{6,4},{7,9},{8,10},{9,7},{10,... | collective-permute-start | bytes 1781768 | tf_op jit(solution)/shard_map/ppermute | solution.py:251
  8.7 8.0 %collective-permute-start.1 = (f32[1160,128]{1,0:T(8,128)S(1)}, f32[1160,128]{1,0:T(8,128)S(1)}, u32[]{:S(2)}, u32[]{:S(2)}) collective-permute-start(f32[1160,128]{1,0:T(8,128)S(1)} %get-tuple-element.14), channel_id=1, source_target_pairs={{3,0},{14,1},{1,2},{4,3},{7,4},{2,5},{5,6},{8,7},{11,8},{6,9},{9,1... | collective-permute-start | bytes 1781768 | tf_op jit(solution)/shard_map/ppermute | solution.py:252
  16.8 2.0 %collective-permute-start.2 = (f32[1160,128]{1,0:T(8,128)S(1)}, f32[1160,128]{1,0:T(8,128)S(1)}, u32[]{:S(2)}, u32[]{:S(2)}) collective-permute-start(f32[1160,128]{1,0:T(8,128)S(1)} %get-tuple-element.15), channel_id=1, source_target_pairs={{0,1},{1,0},{2,3},{3,2},{4,5},{5,4},{6,7},{7,6},{8,9},{9,8},{10,11... | collective-permute-start | bytes 1781768 | tf_op jit(solution)/shard_map/ppermute | solution.py:253
  18.8 0.8 collective-permute-done.near
  19.6 1.3 %shard_map.51.in_ref = f32[4,296,128]{2,1,0:T(8,128)S(1)} custom-call(f32[1024,128]{1,0:T(8,128)S(1)} %get-tuple-element.12.keep, f32[1160,128]{1,0:T(8,128)S(1)} %collective-permute-done.near, f32[128,128]{1,0:T(8,128)S(1)} %copy-done, f32[1,128]{1,0:T(1,128)S(1)} %bitcast.7), custom_call_target="tpu_custom_call" | custom-call | tf_op jit(solution)/shard_map/pallas_call | solution.py:33
  20.8 7.2 %collective-permute-done.1.cross = f32[1160,128]{1,0:T(8,128)S(1)} collective-permute-done((f32[1160,128]{1,0:T(8,128)S(1)}, f32[1160,128]{1,0:T(8,128)S(1)}, u32[]{:S(2)}, u32[]{:S(2)}) %collective-permute-start.1) | collective-permute-done | bytes 593952 | tf_op jit(solution)/shard_map/ppermute | solution.py:252
  28.0 1.3 %shard_map.52 = f32[4,296,128]{2,1,0:T(8,128)S(1)} custom-call(f32[4,296,128]{2,1,0:T(8,128)S(1)} %shard_map.51.in_ref, f32[1160,128]{1,0:T(8,128)S(1)} %collective-permute-done.1.cross, f32[1160,128]{1,0:T(8,128)S(1)} %collective-permute-done.2.core), custom_call_target="tpu_custom_call" | custom-call | tf_op jit(solution)/shard_map/pallas_call | solution.py:33
  29.3 0.0 copy-start.1
  29.3 0.0 copy-start.3
  29.3 23.9 %all_to_all.20.in_ref = f32[4,296,128]{2,1,0:T(8,128)S(1)} all-to-all(f32[4,296,128]{2,1,0:T(8,128)S(1)} %shard_map.52), channel_id=1, replica_groups=mesh['y'=8,'x'=4,'zh'=4,'zl'=2,'c'=2] {'zh'}, dimensions={0} | all-to-all | bytes 1212416 | tf_op jit(solution)/shard_map/all_to_all | solution.py:257
  53.2 0.4 shard_map.53
  53.6 19.1 %all_to_all.21.in_ref = f32[4,296,128]{2,1,0:T(8,128)S(1)} all-to-all(f32[4,296,128]{2,1,0:T(8,128)S(1)} %shard_map.53), channel_id=1, replica_groups=mesh['y'=8,'x'=4,'zh'=4,'zl'=2,'c'=2] {'zh'}, dimensions={0} | all-to-all | bytes 1212416 | tf_op jit(solution)/shard_map/all_to_all | solution.py:259
  72.7 2.8 %shard_map.54 = f32[32,24,128]{2,1,0:T(8,128)S(1)} custom-call(f32[4,296,128]{2,1,0:T(8,128)S(1)} %all_to_all.21.in_ref, f32[1024,128]{1,0:T(8,128)S(1)} %get-tuple-element.12.keep, f32[1160,128]{1,0:T(8,128)S(1)} %collective-permute-done.2.core, f32[1160,128]{1,0:T(8,128)S(1)} %collective-permute-done.near, f32[1160,128]{1,0:T(8,128)S(1)} %collective-permute-done.1.cross, ...), custom_call_target="tpu_custom_call" | custom-call | tf_op jit(solution)/shard_map/pallas_call | solution.py:33
  75.5 21.8 %all_to_all.22.in_ref = f32[32,24,128]{2,1,0:T(8,128)S(1)} all-to-all(f32[32,24,128]{2,1,0:T(8,128)S(1)} %shard_map.54), channel_id=1, replica_groups=mesh['y'=8,'x'=4,'zh'=4,'zl'=2,'c'=2] {'y','x'}, dimensions={0} | all-to-all | bytes 786432 | tf_op jit(solution)/shard_map/all_to_all | solution.py:263
  97.4 1.9 %collective-permute-start.3 = (f32[8,128]{1,0:T(8,128)S(1)}, f32[8,128]{1,0:T(8,128)S(1)}, u32[]{:S(2)}, u32[]{:S(2)}) collective-permute-start(f32[8,128]{1,0:T(8,128)S(1)} %get-tuple-element.17), channel_id=1, source_target_pairs={{0,1},{1,0},{2,3},{3,2},{4,5},{5,4},{6,7},{7,6},{8,9},{9,8},{10,11... | collective-permute-start | bytes 12296 | tf_op jit(solution)/shard_map/ppermute | solution.py:267
  99.3 4.7 %collective-permute-start.4 = (f32[8,128]{1,0:T(8,128)S(1)}, f32[8,128]{1,0:T(8,128)S(1)}, u32[]{:S(2)}, u32[]{:S(2)}) collective-permute-start(f32[8,128]{1,0:T(8,128)S(1)} %get-tuple-element.18), channel_id=1, source_target_pairs={{0,2},{1,15},{2,0},{3,5},{4,6},{5,3},{6,4},{7,9},{8,10},{9,7},{10,... | collective-permute-start | bytes 12296 | tf_op jit(solution)/shard_map/ppermute | solution.py:266
  103.9 2.0 %collective-permute-start.5 = (f32[8,128]{1,0:T(8,128)S(1)}, f32[8,128]{1,0:T(8,128)S(1)}, u32[]{:S(2)}, u32[]{:S(2)}) collective-permute-start(f32[8,128]{1,0:T(8,128)S(1)} %get-tuple-element.19), channel_id=1, source_target_pairs={{0,3},{1,14},{2,1},{3,4},{4,7},{5,2},{6,5},{7,8},{8,11},{9,6},{10,... | collective-permute-start | bytes 12296 | tf_op jit(solution)/shard_map/ppermute | solution.py:265
  106.0 4.1 %collective-permute-done.5.d_ref = f32[8,128]{1,0:T(8,128)S(1)} collective-permute-done((f32[8,128]{1,0:T(8,128)S(1)}, f32[8,128]{1,0:T(8,128)S(1)}, u32[]{:S(2)}, u32[]{:S(2)}) %collective-permute-start.5) | collective-permute-done | bytes 4128 | tf_op jit(solution)/shard_map/ppermute | solution.py:265
  110.1 14.5 %all_to_all.23.in_ref = f32[32,8,128]{2,1,0:T(8,128)S(1)} all-to-all(f32[32,8,128]{2,1,0:T(8,128)S(1)} %shard_map.56), channel_id=1, replica_groups=mesh['y'=8,'x'=4,'zh'=4,'zl'=2,'c'=2] {'y','x'}, dimensions={0} | all-to-all | bytes 262144 | tf_op jit(solution)/shard_map/all_to_all | solution.py:271
  124.6 0.6 shard_map.57
  (9 shorter events, 0.1 us)
Async XLA Ops:
  0.7 0.8 copy-start
  1.6 0.7 copy-start.2
  4.4 15.1 %collective-permute-start = (f32[1160,128]{1,0:T(8,128)S(1)}, f32[1160,128]{1,0:T(8,128)S(1)}, u32[]{:S(2)}, u32[]{:S(2)}) collective-permute-start(f32[1160,128]{1,0:T(8,128)S(1)} %get-tuple-element.13), channel_id=1, source_target_pairs={{0,2},{1,15},{2,0},{3,5},{4,6},{5,3},{6,4},{7,9},{8,10},{9,7},{10,... | collective-permute-start | bytes 1781768 | tf_op jit(solution)/shard_map/ppermute | solution.py:251
  8.7 19.3 %collective-permute-start.1 = (f32[1160,128]{1,0:T(8,128)S(1)}, f32[1160,128]{1,0:T(8,128)S(1)}, u32[]{:S(2)}, u32[]{:S(2)}) collective-permute-start(f32[1160,128]{1,0:T(8,128)S(1)} %get-tuple-element.14), channel_id=1, source_target_pairs={{3,0},{14,1},{1,2},{4,3},{7,4},{2,5},{5,6},{8,7},{11,8},{6,9},{9,1... | collective-permute-start | bytes 1781768 | tf_op jit(solution)/shard_map/ppermute | solution.py:252
  16.8 11.3 %collective-permute-start.2 = (f32[1160,128]{1,0:T(8,128)S(1)}, f32[1160,128]{1,0:T(8,128)S(1)}, u32[]{:S(2)}, u32[]{:S(2)}) collective-permute-start(f32[1160,128]{1,0:T(8,128)S(1)} %get-tuple-element.15), channel_id=1, source_target_pairs={{0,1},{1,0},{2,3},{3,2},{4,5},{5,4},{6,7},{7,6},{8,9},{9,8},{10,11... | collective-permute-start | bytes 1781768 | tf_op jit(solution)/shard_map/ppermute | solution.py:253
  29.3 43.3 %copy-start.1 = (f32[128,128]{1,0:T(8,128)S(1)}, f32[128,128]{1,0:T(8,128)}, u32[]{:S(2)}) copy-start(f32[128,128]{1,0:T(8,128)} %loading_ref.5) | copy-start | bytes 196612
  29.3 43.3 %copy-start.3 = (f32[128]{0:T(128)S(1)}, f32[128]{0:T(128)}, u32[]{:S(2)}) copy-start(f32[128]{0:T(128)} %param.4) | copy-start | bytes 1540
  97.4 8.6 %collective-permute-start.3 = (f32[8,128]{1,0:T(8,128)S(1)}, f32[8,128]{1,0:T(8,128)S(1)}, u32[]{:S(2)}, u32[]{:S(2)}) collective-permute-start(f32[8,128]{1,0:T(8,128)S(1)} %get-tuple-element.17), channel_id=1, source_target_pairs={{0,1},{1,0},{2,3},{3,2},{4,5},{5,4},{6,7},{7,6},{8,9},{9,8},{10,11... | collective-permute-start | bytes 12296 | tf_op jit(solution)/shard_map/ppermute | solution.py:267
  99.3 6.7 %collective-permute-start.4 = (f32[8,128]{1,0:T(8,128)S(1)}, f32[8,128]{1,0:T(8,128)S(1)}, u32[]{:S(2)}, u32[]{:S(2)}) collective-permute-start(f32[8,128]{1,0:T(8,128)S(1)} %get-tuple-element.18), channel_id=1, source_target_pairs={{0,2},{1,15},{2,0},{3,5},{4,6},{5,3},{6,4},{7,9},{8,10},{9,7},{10,... | collective-permute-start | bytes 12296 | tf_op jit(solution)/shard_map/ppermute | solution.py:266
  103.9 6.1 %collective-permute-start.5 = (f32[8,128]{1,0:T(8,128)S(1)}, f32[8,128]{1,0:T(8,128)S(1)}, u32[]{:S(2)}, u32[]{:S(2)}) collective-permute-start(f32[8,128]{1,0:T(8,128)S(1)} %get-tuple-element.19), channel_id=1, source_target_pairs={{0,3},{1,14},{2,1},{3,4},{4,7},{5,2},{6,5},{7,8},{8,11},{9,6},{10,... | collective-permute-start | bytes 12296 | tf_op jit(solution)/shard_map/ppermute | solution.py:265

commit v6 on v0

v6 whole, which is shorter than its diff:
```python
import functools

import jax
import jax.numpy as jnp
from jax import lax
from jax.experimental import pallas as pl
from jax.experimental.pallas import tpu as pltpu
from jax.sharding import Mesh
from jax.sharding import PartitionSpec as P

F32 = jnp.float32
AXES = ("y", "x", "zh", "zl", "c")
WIDE = ("y", "x")
DEEP = ("zh", "zl", "c")
PARTS = 8
LIMIT = 48 * 1024 * 1024
EDGE = 53500000


def mult(left, right, contract=((1,), (0,))):
    return lax.dot_general(
        left, right, (contract, ((), ())),
        preferred_element_type=F32, precision=lax.Precision.HIGHEST,
    )


def whole(*shape):
    return jax.ShapeDtypeStruct(shape, F32)


def call(body, out_shape, *args, scalars=0):
    spaces = [pltpu.SMEM] * scalars + [pltpu.VMEM] * (len(args) - scalars)
    return pl.pallas_call(
        body,
        out_shape=out_shape,
        in_specs=[pl.BlockSpec(memory_space=space) for space in spaces],
        compiler_params=pltpu.CompilerParams(vmem_limit_bytes=LIMIT),
    )(*args)


def split_body(which, counts_ref, loading_ref, offset_ref, keep, other, held, row, sems):
    rows, comps = keep.shape
    outs = (other, keep)
    copies = [
        pltpu.make_async_copy(
            counts_ref.at[pl.ds(pl.multiple_of(which[k] * rows, rows), rows), :], held.at[k], sems.at[k]
        )
        for k in range(2)
    ]
    copies.append(pltpu.make_async_copy(loading_ref, other.at[pl.ds(rows, comps), :], sems.at[2]))
    copies.append(pltpu.make_async_copy(offset_ref, row, sems.at[3]))
    for copy in copies:
        copy.start()
    for k in range(2):
        copies[k].wait()
        outs[k][0:rows, :] = jnp.log(held[k])
    copies[2].wait()
    copies[3].wait()
    other[rows + comps : rows + comps + 8, :] = jnp.broadcast_to(row[...], (8, comps))


def split(which, counts, loading, offset):
    rows, width = counts.shape[0] // 2, counts.shape[1]
    return pl.pallas_call(
        split_body,
        out_shape=(whole(rows, width), whole(rows + loading.shape[0] + 8, width)),
        in_specs=[pl.BlockSpec(memory_space=pltpu.SMEM)] + [pl.BlockSpec(memory_space=pltpu.HBM)] * 3,
        scratch_shapes=[
            pltpu.VMEM((2, rows, width), F32),
            pltpu.VMEM((1, width), F32),
            pltpu.SemaphoreType.DMA((4,)),
        ],
        compiler_params=pltpu.CompilerParams(vmem_limit_bytes=EDGE),
    )(which, counts, loading, offset)


def encode_body(mine, other, loading_ref, offset_ref, out_ref):
    total, comps = mine.shape
    rows, share = total // PARTS, comps // PARTS
    load = jnp.concatenate([loading_ref[...], other[total : total + comps, :]], axis=0)
    bar = jnp.sum(load, axis=0, keepdims=True) / load.shape[0]
    bare = load - bar
    off = jnp.concatenate(
        [jnp.broadcast_to(offset_ref[...], (8, comps)), other[total + comps : total + comps + 8, :]], axis=1
    )
    shift = mult(off, load)[0:1, :]
    gram = mult(load, load, ((0,), (0,)))
    blank = jnp.zeros((4, comps), F32)
    for j in range(PARTS):
        a, b = mine[j * rows : (j + 1) * rows, :], other[j * rows : (j + 1) * rows, :]
        out_ref[j, 0:rows, :] = mult(jnp.concatenate([a, b], axis=1), bare)
        both = a + b
        sums = [
            jnp.sum(both[h * comps : (h + 1) * comps, :].T, axis=0, keepdims=True) for h in range(2)
        ]
        out_ref[j, rows : rows + 8, :] = jnp.concatenate(sums + [bar, shift, blank], axis=0)
        out_ref[j, rows + 8 : rows + 8 + share, :] = gram[j * share : (j + 1) * share, :]


def finish_body(channels, in_ref, out_ref):
    height, comps = in_ref.shape[1:]
    share = comps // PARTS
    rows = height - 8 - share
    group = channels // PARTS
    bars = jnp.concatenate([in_ref[j, rows + 2 : rows + 3, :] for j in range(PARTS)], axis=0)
    shift = sum(in_ref[j, rows + 3 : rows + 4, :] for j in range(PARTS))
    geos = []
    for h in range(2):
        sums = jnp.concatenate([in_ref[j, rows + h : rows + h + 1, :] for j in range(PARTS)], axis=0)
        geo = jnp.sum(sums, axis=0, keepdims=True) / channels
        at = h * comps
        total = mult(sums - group * geo, bars, ((0,), (0,))) - shift
        for j in range(PARTS):
            total += in_ref[j, at : at + comps, :]
        out_ref[at : at + comps, :] = total
        geos.append(geo)
    out_ref[rows : rows + 8, :] = jnp.concatenate(geos + [jnp.zeros((6, comps), F32)], axis=0)
    out_ref[rows + 8 : rows + 8 + share, :] = sum(in_ref[j, rows + 8 : rows + 8 + share, :] for j in range(PARTS))


def block_terms(first, in_ref, logs, offs):
    blocks, height, comps = in_ref.shape
    rows = height - 8 - comps // PARTS
    wide, sums = 0.0, 0.0
    for j in range(blocks):
        s = in_ref[j, 0:rows, :]
        geo = jnp.concatenate(
            [
                jnp.broadcast_to(in_ref[j, rows + h : rows + h + 1, :], (comps, comps)).T
                for h in range(2)
            ],
            axis=0,
        )
        here = pl.ds(pl.multiple_of((2 * j + first) * rows, rows), rows)
        both = jnp.concatenate([a[here, :] - geo - off for a, off in zip(logs, offs)] + [s], axis=1)
        sums += jnp.sum(both, axis=0, keepdims=True)
        wide += mult(s.T, both)
    return wide, sums


def some_grad_body(side, in_ref, mine, other, offset_ref, out_ref):
    total, comps = mine.shape
    offs = (offset_ref[...], other[total + comps : total + comps + 1, :])
    wide, sums = block_terms(side[0], in_ref, (mine, other), offs)
    out_ref[0:comps, :] = wide
    out_ref[comps : comps + 8, :] = jnp.broadcast_to(sums, (8, sums.shape[1]))


def grad_body(side, near_ref, in_ref, some_ref, mine, other, loading_ref, offset_ref, *outs):
    total, comps = mine.shape
    height = in_ref.shape[1]
    share = comps // PARTS
    rows = height - 8 - share
    offs = (offset_ref[...], other[total + comps : total + comps + 1, :])
    wide, sums = block_terms(1 - side[0], near_ref, (mine, other), offs)
    wide, sums = wide + some_ref[0:comps, :], sums + some_ref[comps : comps + 1, :]
    here = [a[j, rows + 8 : rows + 8 + share, :] for j in range(PARTS // 2) for a in (in_ref, near_ref)]
    there = [a[j, rows + 8 : rows + 8 + share, :] for j in range(PARTS // 2) for a in (near_ref, in_ref)]
    gram = jnp.where(side[0] == 0, jnp.concatenate(here, axis=0), jnp.concatenate(there, axis=0))
    row = lax.broadcasted_iota(jnp.int32, (comps, comps), 0)
    col = lax.broadcasted_iota(jnp.int32, (comps, comps), 1)
    hat = gram - jnp.where(row == col, 2.0, 0.0).astype(F32)
    loads = (loading_ref[...], other[total : total + comps, :])
    square = wide[:, 2 * comps : 3 * comps]
    s_hat = mult(jnp.broadcast_to(sums[:, 2 * comps : 3 * comps], (8, comps)), hat)
    for k, out in enumerate(outs):
        part = slice(k * comps, (k + 1) * comps)
        out[0:comps, :] = mult(wide[:, part], hat, ((0,), (0,))) + mult(loads[k], square)
        out[comps : comps + 8, :] = -(mult(s_hat, loads[k], ((1,), (1,))) + sums[:, part])


def deal_body(a_ref, b_ref, out_ref):
    pieces, _, comps = out_ref.shape
    share = comps // pieces
    total = a_ref[...] + b_ref[...]
    for p in range(pieces):
        out_ref[p, 0:share, :] = total[p * share : (p + 1) * share, :]
        out_ref[p, share:8, :] = total[comps : comps + 8 - share, :]


def gather_body(pixels, in_ref, out_ref):
    total = jnp.sum(in_ref[...], axis=0) / pixels
    for j in range(out_ref.shape[0]):
        out_ref[j] = total


def last_body(in_ref, load_ref, off_ref):
    pieces = in_ref.shape[0]
    share = load_ref.shape[0] // pieces
    for p in range(pieces):
        load_ref[p * share : (p + 1) * share, :] = in_ref[p, 0:share, :]
    off_ref[...] = in_ref[0, share : share + 1, :]


def on_device(counts, offset, loading):
    pixels = counts.shape[0] * lax.axis_size(WIDE)
    comps = loading.shape[1]
    channels = counts.shape[1] * PARTS * 2
    height = counts.shape[0] // 2 // PARTS + 8 + comps // PARTS
    core = lax.axis_index("c").astype(jnp.int32)
    side = lax.axis_index("zl").astype(jnp.int32).reshape(1)
    offset = offset.reshape(1, comps)

    swap = [(0, 1), (1, 0)]
    near_pairs = []
    for z in range(PARTS):
        for c in range(2):
            partner = (((z - c) % PARTS ^ 1) + c) % PARTS
            near_pairs.append((2 * z + c, 2 * partner + c))

    mine, other_out = split(jnp.stack([1 - core, core]), counts, loading, offset)
    other = lax.ppermute(other_out, "c", swap)
    partial = call(encode_body, whole(PARTS, height, comps), mine, other, loading, offset)
    gathered = lax.all_to_all(partial, ("zh", "zl"), 0, 0)
    own = call(functools.partial(finish_body, channels), whole(height, comps), gathered)
    scores = lax.all_gather(own, "zh", axis=0)
    near = lax.ppermute(scores, DEEP, near_pairs)
    some = call(
        some_grad_body, whole(comps + 8, 3 * comps), side, scores, mine, other, offset, scalars=1
    )
    shape = whole(comps + 8, comps)
    grad_mine, grad_other = call(
        grad_body, (shape, shape), side, near, scores, some, mine, other, loading, offset, scalars=1
    )
    arrived = lax.ppermute(grad_other, "c", swap)
    plane = lax.axis_size(WIDE)
    pieces = call(deal_body, whole(plane, 8, comps), grad_mine, arrived)
    pieces = lax.all_to_all(pieces, WIDE, 0, 0)
    pieces = call(functools.partial(gather_body, pixels), whole(plane, 8, comps), pieces)
    pieces = lax.all_to_all(pieces, WIDE, 0, 0)
    grad, grad_offset = call(last_body, (whole(comps, comps), whole(1, comps)), pieces)
    return grad, grad_offset.reshape(comps)


def solution(mesh):
    wide, deep = mesh.devices.shape
    split_mesh = Mesh(mesh.devices.reshape(wide // 4, 4, deep // 4, 2, 2), AXES)
    return jax.shard_map(
        on_device,
        mesh=split_mesh,
        in_specs=(P(WIDE, DEEP), P(DEEP), P(DEEP, None)),
        out_specs=(P(DEEP, None), P(DEEP)),
        check_vma=False,
    )
```

time: 552 us -> 121 us (0.22)
  waiting for transfers between devices: 383 us -> 11.3 us
  blocking collectives: 123 us -> 91.2 us
  matrix products: 26.1 us -> 0 us
  between operations: 13.8 us -> 0.72 us
  Pallas kernels: 0 us -> 8.56 us
  starting transfers between devices: 0.3 us -> 6.72 us
    psum x3 -> x0, waiting for transfers between devices: 383 us -> none  [the longest x1 150 us: on_device(): load_sum, offset_sum = lax.psum((load_term, offset_term), 'pix')]
    psum x2 -> x0, blocking collectives: 123 us -> none  [the longest x1 68.5 us: on_device(): load_sum, offset_sum = lax.psum((load_term, offset_term), 'pix')]
    all_to_all x0 -> x3, blocking collectives: none -> 74.9 us  [the longest x1 41.3 us: on_device(): gathered = lax.all_to_all(partial, ('zh', 'zl'), 0, 0)]
    dot_general x6 -> x0, matrix products: 26.1 us -> none  [mult(): jnp.dot(left, right, preferred_element_type=jnp.float32, precision=lax.Pr...]
    all_gather x0 -> x1, blocking collectives: none -> 16.4 us  [on_device(): scores = lax.all_gather(own, 'zh', axis=0)]
    ppermute x0 -> x3, waiting for transfers between devices: none -> 11.3 us  [the longest x1 7.37 us: on_device(): near = lax.ppermute(scores, DEEP, near_pairs)]
    pallas_call x0 -> x8, Pallas kernels: none -> 8.56 us  [the longest x7 6.29 us: call(): pl.pallas_call(body, out_shape=out_shape, in_specs=[pl.BlockSpec(memory_s...]
    ppermute x0 -> x3, starting transfers between devices: none -> 6.72 us  [the longest x1 2.88 us: on_device(): near = lax.ppermute(scores, DEEP, near_pairs)]
  transfers between devices with their start and end apart: 3 -> 3, of which waited for: 3 -> 3; matrix products, arithmetic and copies ran while one was open for 1% -> 0% of each run, Pallas kernels for 0% -> 1%
where the time goes in v6:
time: 121 us; the launch traced here: 120 us
  blocking collectives  91.2 us (75%)
  waiting for transfers between devices  11.3 us (9%)
  Pallas kernels  8.56 us (7%)
  starting transfers between devices  6.72 us (6%)
  local copies, waits for them, and re-layouts  1.5 us (1%)
    all_to_all x1, blocking collectives, on_device(): gathered = lax.all_to_all(partial, ('zh', 'zl'), 0, 0)  41.3 us
    all_to_all x2, blocking collectives, on_device(): pieces = lax.all_to_all(pieces, WIDE, 0, 0)  33.6 us
    all_gather x1, blocking collectives, on_device(): scores = lax.all_gather(own, 'zh', axis=0)  16.4 us
    ppermute x1, waiting for transfers between devices, on_device(): near = lax.ppermute(scores, DEEP, near_pairs)  7.37 us
    pallas_call x7, Pallas kernels, call(): pl.pallas_call(body, out_shape=out_shape, in_specs=[pl.BlockSpec(memory_s...  6.29 us
    ppermute x1, starting transfers between devices, on_device(): near = lax.ppermute(scores, DEEP, near_pairs)  2.88 us
    ppermute x1, waiting for transfers between devices, on_device(): other = lax.ppermute(other_out, 'c', swap)  2.73 us
  transfers between devices with their start and end apart: 3, of which 3 were waited for; matrix products, arithmetic and copies ran while one was open for 0% of the time, Pallas kernels for 1%

profile of v6, /device:TPU:8, one launch (start us, length us, event | category | flops | bytes accessed | tf_op | source)
XLA Modules:
  0.0 120.1 jit_solution(2700886436258095571)
XLA Ops:
  0.6 0.1 pad_add_fusion.which
  0.7 0.0 copy-start
  0.7 0.8 copy-done
  1.5 0.0 copy-start.2
  1.6 0.7 copy-done.2
  2.2 2.3 %shard_map.50 = (f32[2048,128]{1,0:T(8,128)S(1)}, f32[2184,128]{1,0:T(8,128)S(1)}) custom-call(s32[2]{0:T(128)S(1)} %pad_add_fusion.which, f32[4096,128]{1,0:T(8,128)} %counts_ref.1, f32[128,128]{1,0:T(8,128)S(1)} %copy-done, f32[1,128]{1,0:T(1,128)S(1)} %bitcast.9), custom_call_target="tpu_custom_call" | custom-call | tf_op jit(solution)/shard_map/pallas_call | solution.py:64
  4.5 1.9 %collective-permute-start = (f32[2184,128]{1,0:T(8,128)S(1)}, f32[2184,128]{1,0:T(8,128)S(1)}, u32[]{:S(2)}, u32[]{:S(2)}) collective-permute-start(f32[2184,128]{1,0:T(8,128)S(1)} %get-tuple-element.9), channel_id=1, source_target_pairs={{0,1},{1,0},{2,3},{3,2},{4,5},{5,4},{6,7},{7,6},{8,9},{9,8},{10,11... | collective-permute-start | bytes 3354632 | tf_op jit(solution)/shard_map/ppermute | solution.py:212
  6.4 2.7 %collective-permute-done.other = f32[2184,128]{1,0:T(8,128)S(1)} collective-permute-done((f32[2184,128]{1,0:T(8,128)S(1)}, f32[2184,128]{1,0:T(8,128)S(1)}, u32[]{:S(2)}, u32[]{:S(2)}) %collective-permute-start) | collective-permute-done | bytes 1118240 | tf_op jit(solution)/shard_map/ppermute | solution.py:212
  9.1 2.1 %shard_map.51 = f32[8,280,128]{2,1,0:T(8,128)S(1)} custom-call(f32[2048,128]{1,0:T(8,128)S(1)} %get-tuple-element.8.mine, f32[2184,128]{1,0:T(8,128)S(1)} %collective-permute-done.other, f32[128,128]{1,0:T(8,128)S(1)} %copy-done, f32[1,128]{1,0:T(1,128)S(1)} %bitcast.10), custom_call_target="tpu_custom_call" | custom-call | tf_op jit(solution)/shard_map/pallas_call | solution.py:33
  11.2 41.3 %all_to_all.15.in_ref = f32[8,280,128]{2,1,0:T(8,128)S(1)} all-to-all(f32[8,280,128]{2,1,0:T(8,128)S(1)} %shard_map.51), channel_id=1, replica_groups=mesh['y'=8,'x'=4,'zh'=4,'zl'=2,'c'=2] {'zh','zl'}, dimensions={0} | all-to-all | bytes 2293760 | tf_op jit(solution)/shard_map/all_to_all | solution.py:214
  52.5 0.4 shard_map.52
  52.9 16.4 %all-gather = f32[1120,128]{1,0:T(8,128)S(1)} all-gather(f32[280,128]{1,0:T(8,128)S(1)} %shard_map.52), channel_id=2, replica_groups=mesh['y'=8,'x'=4,'zh'=4,'zl'=2,'c'=2] {'zh'}, dimensions={0}, use_global_device_ids=true | all-gather | bytes 716800 | tf_op jit(solution)/shard_map/all_gather | solution.py:216
  69.2 2.9 %collective-permute-start.1 = (f32[4,280,128]{2,1,0:T(8,128)S(1)}, f32[4,280,128]{2,1,0:T(8,128)S(1)}, u32[]{:S(2)}, u32[]{:S(2)}) collective-permute-start(f32[4,280,128]{2,1,0:T(8,128)S(1)} %bitcast.6), channel_id=1, source_target_pairs={{0,2},{1,15},{2,0},{3,5},{4,6},{5,3},{6,4},{7,9},{8,10},{9,7},{10,... | collective-permute-start | bytes 1720328 | tf_op jit(solution)/shard_map/ppermute | solution.py:217
  72.1 0.0 copy-done.3
  72.1 0.0 copy-start.1
  72.1 1.3 %shard_map.53.some_ref = f32[136,384]{1,0:T(8,128)S(1)} custom-call(s32[1]{0:T(128)} %bitcast.side, f32[4,280,128]{2,1,0:T(8,128)S(1)} %bitcast.7, f32[2048,128]{1,0:T(8,128)S(1)} %get-tuple-element.8.mine, f32[2184,128]{1,0:T(8,128)S(1)} %collective-permute-done.other, f32[1,128]{1,0:T(1,128)S(1)} %bitcast.11), custom_call_target="tpu_custom_call" | custom-call | tf_op jit(solution)/shard_map/pallas_call | solution.py:33
  73.4 7.4 %collective-permute-done.1.near_ref = f32[4,280,128]{2,1,0:T(8,128)S(1)} collective-permute-done((f32[4,280,128]{2,1,0:T(8,128)S(1)}, f32[4,280,128]{2,1,0:T(8,128)S(1)}, u32[]{:S(2)}, u32[]{:S(2)}) %collective-permute-start.1) | collective-permute-done | bytes 573472 | tf_op jit(solution)/shard_map/ppermute | solution.py:217
  80.8 0.0 copy-done.1
  80.8 1.8 %shard_map.54 = (f32[136,128]{1,0:T(8,128)S(1)}, f32[136,128]{1,0:T(8,128)S(1)}) custom-call(s32[1]{0:T(128)} %bitcast.side, f32[4,280,128]{2,1,0:T(8,128)S(1)} %collective-permute-done.1.near_ref, f32[4,280,128]{2,1,0:T(8,128)S(1)} %bitcast.8, f32[136,384]{1,0:T(8,128)S(1)} %shard_map.53.some_ref, f32[2048,128]{1,0:T(8,128)S(1)} %get-tuple-element.8.mine, ...), custom_call_target="tpu_custom_call" | custom-call | tf_op jit(solution)/shard_map/pallas_call | solution.py:33
  82.6 1.9 %collective-permute-start.2 = (f32[136,128]{1,0:T(8,128)S(1)}, f32[136,128]{1,0:T(8,128)S(1)}, u32[]{:S(2)}, u32[]{:S(2)}) collective-permute-start(f32[136,128]{1,0:T(8,128)S(1)} %get-tuple-element.11), channel_id=1, source_target_pairs={{0,1},{1,0},{2,3},{3,2},{4,5},{5,4},{6,7},{7,6},{8,9},{9,8},{10,11... | collective-permute-start | bytes 208904 | tf_op jit(solution)/shard_map/ppermute | solution.py:225
  84.6 1.2 %collective-permute-done.2.b_ref = f32[136,128]{1,0:T(8,128)S(1)} collective-permute-done((f32[136,128]{1,0:T(8,128)S(1)}, f32[136,128]{1,0:T(8,128)S(1)}, u32[]{:S(2)}, u32[]{:S(2)}) %collective-permute-start.2) | collective-permute-done | bytes 69664 | tf_op jit(solution)/shard_map/ppermute | solution.py:225
  85.8 19.9 %all_to_all.16.in_ref = f32[32,8,128]{2,1,0:T(8,128)S(1)} all-to-all(f32[32,8,128]{2,1,0:T(8,128)S(1)} %shard_map.55), channel_id=1, replica_groups=mesh['y'=8,'x'=4,'zh'=4,'zl'=2,'c'=2] {'y','x'}, dimensions={0} | all-to-all | bytes 262144 | tf_op jit(solution)/shard_map/all_to_all | solution.py:228
  105.7 13.7 %all_to_all.17.in_ref = f32[32,8,128]{2,1,0:T(8,128)S(1)} all-to-all(f32[32,8,128]{2,1,0:T(8,128)S(1)} %shard_map.56), channel_id=1, replica_groups=mesh['y'=8,'x'=4,'zh'=4,'zl'=2,'c'=2] {'y','x'}, dimensions={0} | all-to-all | bytes 262144 | tf_op jit(solution)/shard_map/all_to_all | solution.py:230
  119.5 0.6 shard_map.57
  (3 shorter events, 0.1 us)
Async XLA Ops:
  0.7 0.8 copy-start
  1.5 0.7 copy-start.2
  4.5 4.7 %collective-permute-start = (f32[2184,128]{1,0:T(8,128)S(1)}, f32[2184,128]{1,0:T(8,128)S(1)}, u32[]{:S(2)}, u32[]{:S(2)}) collective-permute-start(f32[2184,128]{1,0:T(8,128)S(1)} %get-tuple-element.9), channel_id=1, source_target_pairs={{0,1},{1,0},{2,3},{3,2},{4,5},{5,4},{6,7},{7,6},{8,9},{9,8},{10,11... | collective-permute-start | bytes 3354632 | tf_op jit(solution)/shard_map/ppermute | solution.py:212
  52.5 19.6 %copy-start.3 = (f32[128]{0:T(128)S(1)}, f32[128]{0:T(128)}, u32[]{:S(2)}) copy-start(f32[128]{0:T(128)} %param.4) | copy-start | bytes 1540
  69.2 11.6 %collective-permute-start.1 = (f32[4,280,128]{2,1,0:T(8,128)S(1)}, f32[4,280,128]{2,1,0:T(8,128)S(1)}, u32[]{:S(2)}, u32[]{:S(2)}) collective-permute-start(f32[4,280,128]{2,1,0:T(8,128)S(1)} %bitcast.6), channel_id=1, source_target_pairs={{0,2},{1,15},{2,0},{3,5},{4,6},{5,3},{6,4},{7,9},{8,10},{9,7},{10,... | collective-permute-start | bytes 1720328 | tf_op jit(solution)/shard_map/ppermute | solution.py:217
  72.1 8.7 %copy-start.1 = (f32[128,128]{1,0:T(8,128)S(1)}, f32[128,128]{1,0:T(8,128)}, u32[]{:S(2)}) copy-start(f32[128,128]{1,0:T(8,128)} %loading_ref.5) | copy-start | bytes 196612
  82.6 3.2 %collective-permute-start.2 = (f32[136,128]{1,0:T(8,128)S(1)}, f32[136,128]{1,0:T(8,128)S(1)}, u32[]{:S(2)}, u32[]{:S(2)}) collective-permute-start(f32[136,128]{1,0:T(8,128)S(1)} %get-tuple-element.11), channel_id=1, source_target_pairs={{0,1},{1,0},{2,3},{3,2},{4,5},{5,4},{6,7},{7,6},{8,9},{9,8},{10,11... | collective-permute-start | bytes 208904 | tf_op jit(solution)/shard_map/ppermute | solution.py:225

commit v7 on v6

--- a/solution.py
+++ b/solution.py
@@ -14,7 +14,6 @@
 DEEP = ("zh", "zl", "c")
 PARTS = 8
 LIMIT = 48 * 1024 * 1024
-EDGE = 53500000
 
 
 def mult(left, right, contract=((1,), (0,))):
@@ -38,75 +37,116 @@
     )(*args)
 
 
-def split_body(which, counts_ref, loading_ref, offset_ref, keep, other, held, row, sems):
-    rows, comps = keep.shape
-    outs = (other, keep)
+def send_body(which, counts_ref, loading_ref, offset_ref, out_ref, held, row, sems):
+    rows, comps = held.shape
+    half = rows // 2
     copies = [
         pltpu.make_async_copy(
-            counts_ref.at[pl.ds(pl.multiple_of(which[k] * rows, rows), rows), :], held.at[k], sems.at[k]
+            counts_ref.at[pl.ds(pl.multiple_of(which[0] * rows + k * half, half), half), :],
+            held.at[pl.ds(k * half, half), :],
+            sems.at[k],
         )
         for k in range(2)
     ]
-    copies.append(pltpu.make_async_copy(loading_ref, other.at[pl.ds(rows, comps), :], sems.at[2]))
+    copies.append(pltpu.make_async_copy(loading_ref, out_ref.at[pl.ds(rows, comps), :], sems.at[2]))
     copies.append(pltpu.make_async_copy(offset_ref, row, sems.at[3]))
     for copy in copies:
         copy.start()
     for k in range(2):
         copies[k].wait()
-        outs[k][0:rows, :] = jnp.log(held[k])
+        out_ref[k * half : (k + 1) * half, :] = jnp.log(held[k * half : (k + 1) * half, :])
     copies[2].wait()
     copies[3].wait()
-    other[rows + comps : rows + comps + 8, :] = jnp.broadcast_to(row[...], (8, comps))
-
-
-def split(which, counts, loading, offset):
+    out_ref[rows + comps : rows + comps + 8, :] = jnp.broadcast_to(row[...], (8, comps))
+
+
+def keep_body(which, counts_ref, out_ref, held, sem):
+    rows = held.shape[0]
+    copy = pltpu.make_async_copy(
+        counts_ref.at[pl.ds(pl.multiple_of(which[0] * rows, rows), rows), :], held, sem
+    )
+    copy.start()
+    copy.wait()
+    out_ref[...] = jnp.log(held[...])
+
+
+def cut(body, height, scratch, which, counts, *more):
     rows, width = counts.shape[0] // 2, counts.shape[1]
     return pl.pallas_call(
-        split_body,
-        out_shape=(whole(rows, width), whole(rows + loading.shape[0] + 8, width)),
-        in_specs=[pl.BlockSpec(memory_space=pltpu.SMEM)] + [pl.BlockSpec(memory_space=pltpu.HBM)] * 3,
-        scratch_shapes=[
-            pltpu.VMEM((2, rows, width), F32),
-            pltpu.VMEM((1, width), F32),
-            pltpu.SemaphoreType.DMA((4,)),
-        ],
-        compiler_params=pltpu.CompilerParams(vmem_limit_bytes=EDGE),
-    )(which, counts, loading, offset)
-
-
-def encode_body(mine, other, loading_ref, offset_ref, out_ref):
+        body,
+        out_shape=whole(height, width),
+        in_specs=[pl.BlockSpec(memory_space=pltpu.SMEM)]
+        + [pl.BlockSpec(memory_space=pltpu.HBM)] * (1 + len(more)),
+        scratch_shapes=[pltpu.VMEM((rows, width), F32)] + scratch,
+        compiler_params=pltpu.CompilerParams(vmem_limit_bytes=LIMIT),
+    )(which.reshape(1), *(pltpu.with_memory_space_constraint(a, pltpu.HBM) for a in (counts,) + more))
+
+
+def source_terms(load, off):
+    bar = jnp.sum(load, axis=0, keepdims=True) / load.shape[0]
+    return bar, load - bar, mult(off, load)[0:1, :], mult(load, load, ((0,), (0,)))
+
+
+def log_sums(logs):
+    comps = logs.shape[1]
+    return [
+        jnp.sum(logs[h * comps : (h + 1) * comps, :].T, axis=0, keepdims=True)
+        for h in range(logs.shape[0] // comps)
+    ]
+
+
+def encode_body(mine, loading_ref, offset_ref, out_ref):
     total, comps = mine.shape
     rows, share = total // PARTS, comps // PARTS
-    load = jnp.concatenate([loading_ref[...], other[total : total + comps, :]], axis=0)
-    bar = jnp.sum(load, axis=0, keepdims=True) / load.shape[0]
-    bare = load - bar
-    off = jnp.concatenate(
-        [jnp.broadcast_to(offset_ref[...], (8, comps)), other[total + comps : total + comps + 8, :]], axis=1
-    )
-    shift = mult(off, load)[0:1, :]
-    gram = mult(load, load, ((0,), (0,)))
-    blank = jnp.zeros((4, comps), F32)
+    bar, bare, shift, gram = source_terms(
+        loading_ref[...], jnp.broadcast_to(offset_ref[...], (8, comps))
+    )
+    blank = jnp.zeros((1, comps), F32)
     for j in range(PARTS):
-        a, b = mine[j * rows : (j + 1) * rows, :], other[j * rows : (j + 1) * rows, :]
-        out_ref[j, 0:rows, :] = mult(jnp.concatenate([a, b], axis=1), bare)
-        both = a + b
-        sums = [
-            jnp.sum(both[h * comps : (h + 1) * comps, :].T, axis=0, keepdims=True) for h in range(2)
-        ]
-        out_ref[j, rows : rows + 8, :] = jnp.concatenate(sums + [bar, shift, blank], axis=0)
+        logs = mine[j * rows : (j + 1) * rows, :]
+        out_ref[j, 0:rows, :] = mult(logs, bare)
+        out_ref[j, rows : rows + 8, :] = jnp.concatenate(
+            log_sums(logs) + [blank, blank, bar, blank, shift, blank], axis=0
+        )
         out_ref[j, rows + 8 : rows + 8 + share, :] = gram[j * share : (j + 1) * share, :]
+
+
+def encode_last_body(in_ref, other, out_ref):
+    height, comps = in_ref.shape[1:]
+    share = comps // PARTS
+    rows = height - 8 - share
+    total = PARTS * rows
+    bar, bare, shift, gram = source_terms(
+        other[total : total + comps, :], other[total + comps : total + comps + 8, :]
+    )
+    blank = jnp.zeros((1, comps), F32)
+    for j in range(PARTS):
+        logs = other[j * rows : (j + 1) * rows, :]
+        out_ref[j, 0:rows, :] = in_ref[j, 0:rows, :] + mult(logs, bare)
+        out_ref[j, rows : rows + 8, :] = in_ref[j, rows : rows + 8, :] + jnp.concatenate(
+            [blank, blank] + log_sums(logs) + [blank, bar, shift, blank], axis=0
+        )
+        at = rows + 8
+        out_ref[j, at : at + share, :] = in_ref[j, at : at + share, :] + gram[j * share : (j + 1) * share, :]
 
 
 def finish_body(channels, in_ref, out_ref):
     height, comps = in_ref.shape[1:]
     share = comps // PARTS
     rows = height - 8 - share
-    group = channels // PARTS
-    bars = jnp.concatenate([in_ref[j, rows + 2 : rows + 3, :] for j in range(PARTS)], axis=0)
-    shift = sum(in_ref[j, rows + 3 : rows + 4, :] for j in range(PARTS))
+    group = channels // (2 * PARTS)
+    bars = jnp.concatenate([in_ref[j, rows + 4 : rows + 6, :] for j in range(PARTS)], axis=0)
+    shift = sum(in_ref[j, rows + 6 : rows + 7, :] for j in range(PARTS))
     geos = []
     for h in range(2):
-        sums = jnp.concatenate([in_ref[j, rows + h : rows + h + 1, :] for j in range(PARTS)], axis=0)
+        sums = jnp.concatenate(
+            [
+                in_ref[j, rows + h + k : rows + h + k + 1, :]
+                for j in range(PARTS)
+                for k in (0, 2)
+            ],
+            axis=0,
+        )
         geo = jnp.sum(sums, axis=0, keepdims=True) / channels
         at = h * comps
         total = mult(sums - group * geo, bars, ((0,), (0,))) - shift
@@ -146,7 +186,7 @@
     out_ref[comps : comps + 8, :] = jnp.broadcast_to(sums, (8, sums.shape[1]))
 
 
-def grad_body(side, near_ref, in_ref, some_ref, mine, other, loading_ref, offset_ref, *outs):
+def grad_body(side, near_ref, in_ref, some_ref, mine, other, offset_ref, out_ref, rest_ref):
     total, comps = mine.shape
     height = in_ref.shape[1]
     share = comps // PARTS
@@ -160,13 +200,27 @@
     row = lax.broadcasted_iota(jnp.int32, (comps, comps), 0)
     col = lax.broadcasted_iota(jnp.int32, (comps, comps), 1)
     hat = gram - jnp.where(row == col, 2.0, 0.0).astype(F32)
-    loads = (loading_ref[...], other[total : total + comps, :])
     square = wide[:, 2 * comps : 3 * comps]
-    s_hat = mult(jnp.broadcast_to(sums[:, 2 * comps : 3 * comps], (8, comps)), hat)
-    for k, out in enumerate(outs):
-        part = slice(k * comps, (k + 1) * comps)
-        out[0:comps, :] = mult(wide[:, part], hat, ((0,), (0,))) + mult(loads[k], square)
-        out[comps : comps + 8, :] = -(mult(s_hat, loads[k], ((1,), (1,))) + sums[:, part])
+    s_sum, c_mine, c_other = (sums[:, k * comps : (k + 1) * comps] for k in (2, 0, 1))
+    source_grad(wide[:, comps : 2 * comps], hat, square, s_sum, c_other, other[total : total + comps, :], out_ref)
+    rest_ref[0] = wide[:, 0:comps]
+    rest_ref[1] = hat
+    rest_ref[2] = square
+    rest_ref[3] = jnp.broadcast_to(s_sum, (comps, comps))
+    rest_ref[4] = jnp.broadcast_to(c_mine, (comps, comps))
+
+
+def source_grad(w_turned, hat, square, s_sum, c_sum, load, out_ref):
+    comps = load.shape[1]
+    s_hat = mult(jnp.broadcast_to(s_sum, (8, comps)), hat)
+    out_ref[0:comps, :] = mult(w_turned, hat, ((0,), (0,))) + mult(load, square)
+    out_ref[comps : comps + 8, :] = -(mult(s_hat, load, ((1,), (1,))) + c_sum)
+
+
+def mine_grad_body(rest_ref, loading_ref, out_ref):
+    source_grad(
+        rest_ref[0], rest_ref[1], rest_ref[2], rest_ref[3, 0:1, :], rest_ref[4, 0:1, :], loading_ref[...], out_ref
+    )
 
 
 def deal_body(a_ref, b_ref, out_ref):
@@ -208,9 +262,14 @@
             partner = (((z - c) % PARTS ^ 1) + c) % PARTS
             near_pairs.append((2 * z + c, 2 * partner + c))
 
-    mine, other_out = split(jnp.stack([1 - core, core]), counts, loading, offset)
-    other = lax.ppermute(other_out, "c", swap)
-    partial = call(encode_body, whole(PARTS, height, comps), mine, other, loading, offset)
+    half = counts.shape[0] // 2
+    scratch = [pltpu.VMEM((1, comps), F32), pltpu.SemaphoreType.DMA((4,))]
+    sent = cut(send_body, half + comps + 8, scratch, 1 - core, counts, loading, offset)
+    other = lax.ppermute(sent, "c", swap)
+    mine = cut(keep_body, half, [pltpu.SemaphoreType.DMA], core, counts)
+    block = whole(PARTS, height, comps)
+    partial = call(encode_body, block, mine, loading, offset)
+    partial = call(encode_last_body, block, partial, other)
     gathered = lax.all_to_all(partial, ("zh", "zl"), 0, 0)
     own = call(functools.partial(finish_body, channels), whole(height, comps), gathered)
     scores = lax.all_gather(own, "zh", axis=0)
@@ -219,10 +278,11 @@
         some_grad_body, whole(comps + 8, 3 * comps), side, scores, mine, other, offset, scalars=1
     )
     shape = whole(comps + 8, comps)
-    grad_mine, grad_other = call(
-        grad_body, (shape, shape), side, near, scores, some, mine, other, loading, offset, scalars=1
+    grad_other, rest = call(
+        grad_body, (shape, whole(5, comps, comps)), side, near, scores, some, mine, other, offset, scalars=1
     )
     arrived = lax.ppermute(grad_other, "c", swap)
+    grad_mine = call(mine_grad_body, shape, rest, loading)
     plane = lax.axis_size(WIDE)
     pieces = call(deal_body, whole(plane, 8, comps), grad_mine, arrived)
     pieces = lax.all_to_all(pieces, WIDE, 0, 0)

time: 121 us -> 118 us (0.975)
  waiting for transfers between devices: 11.3 us -> 9.07 us
  blocking collectives: 91.2 us -> 92.9 us
  local copies, waits for them, and re-layouts: 1.5 us -> 0.01 us
    ppermute x1, waiting for transfers between devices: 2.73 us -> 0.14 us  [on_device(): other = lax.ppermute(sent, 'c', swap)]
    unnamed x8 -> x4, local copies, waits for them, and re-layouts: 1.5 us -> 0.01 us
    all_gather x1, blocking collectives: 16.4 us -> 17.8 us  [on_device(): scores = lax.all_gather(own, 'zh', axis=0)]
    pallas_call x1 -> x2, Pallas kernels: 2.26 us -> 2.73 us  [cut(): pl.pallas_call(body, out_shape=whole(height, width), in_specs=[pl.BlockSp...]
    pallas_call x7 -> x9, Pallas kernels: 6.29 us -> 6.7 us  [call(): pl.pallas_call(body, out_shape=out_shape, in_specs=[pl.BlockSpec(memory_s...]
  transfers between devices with their start and end apart: 3 -> 3, of which waited for: 3 -> 3; matrix products, arithmetic and copies ran while one was open for 0% -> 0% of each run, Pallas kernels for 1% -> 4%
where the time goes in v7:
time: 118 us
  blocking collectives  92.9 us (79%)
  Pallas kernels  9.42 us (8%)
  waiting for transfers between devices  9.07 us (8%)
  starting transfers between devices  5.97 us (5%)
    all_to_all x1, blocking collectives, on_device(): gathered = lax.all_to_all(partial, ('zh', 'zl'), 0, 0)  41.5 us
    all_to_all x2, blocking collectives, on_device(): pieces = lax.all_to_all(pieces, WIDE, 0, 0)  33.6 us
    all_gather x1, blocking collectives, on_device(): scores = lax.all_gather(own, 'zh', axis=0)  17.8 us
    ppermute x1, waiting for transfers between devices, on_device(): near = lax.ppermute(scores, DEEP, near_pairs)  8.17 us
    pallas_call x9, Pallas kernels, call(): pl.pallas_call(body, out_shape=out_shape, in_specs=[pl.BlockSpec(memory_s...  6.7 us
    pallas_call x2, Pallas kernels, cut(): pl.pallas_call(body, out_shape=whole(height, width), in_specs=[pl.BlockSp...  2.73 us
  transfers between devices with their start and end apart: 3, of which 3 were waited for; matrix products, arithmetic and copies ran while one was open for 0% of the time, Pallas kernels for 4%

profile of v7, /device:TPU:8, one launch (start us, length us, event | category | flops | bytes accessed | tf_op | source)
XLA Modules:
  0.0 118.2 jit_solution(11465236044369831556)
XLA Ops:
  0.6 1.3 %shard_map.52 = f32[2184,128]{1,0:T(8,128)S(1)} custom-call(s32[1]{0:T(128)} %bitcast.3.which, f32[4096,128]{1,0:T(8,128)} %counts_ref.3, f32[128,128]{1,0:T(8,128)} %loading_ref.5, f32[1,128]{1,0:T(1,128)} %bitcast.9), custom_call_target="tpu_custom_call" | custom-call | tf_op jit(solution)/shard_map/pallas_call | solution.py:75
  2.0 1.9 %collective-permute-start = (f32[2184,128]{1,0:T(8,128)S(1)}, f32[2184,128]{1,0:T(8,128)S(1)}, u32[]{:S(2)}, u32[]{:S(2)}) collective-permute-start(f32[2184,128]{1,0:T(8,128)S(1)} %shard_map.52), channel_id=1, source_target_pairs={{0,1},{1,0},{2,3},{3,2},{4,5},{5,4},{6,7},{7,6},{8,9},{9,8},{10,11... | collective-permute-start | bytes 3354632 | tf_op jit(solution)/shard_map/ppermute | solution.py:268
  3.9 0.0 copy-start
  3.9 0.0 copy-start.1
  3.9 1.4 %shard_map.50.mine = f32[2048,128]{1,0:T(8,128)S(1)} custom-call(s32[1]{0:T(128)} %bitcast.1.which, f32[4096,128]{1,0:T(8,128)} %counts_ref.3), custom_call_target="tpu_custom_call" | custom-call | tf_op jit(solution)/shard_map/pallas_call | solution.py:75
  5.3 0.0 copy-done
  5.3 0.0 copy-done.1
  5.3 1.1 shard_map.51.in_ref
  6.5 0.1 collective-permute-done.other
  6.6 1.1 shard_map.53
  7.8 41.5 %all_to_all.15.in_ref = f32[8,280,128]{2,1,0:T(8,128)S(1)} all-to-all(f32[8,280,128]{2,1,0:T(8,128)S(1)} %shard_map.53), channel_id=1, replica_groups=mesh['y'=8,'x'=4,'zh'=4,'zl'=2,'c'=2] {'zh','zl'}, dimensions={0} | all-to-all | bytes 2293760 | tf_op jit(solution)/shard_map/all_to_all | solution.py:273
  49.2 0.3 shard_map.54
  49.6 17.8 %all-gather = f32[1120,128]{1,0:T(8,128)S(1)} all-gather(f32[280,128]{1,0:T(8,128)S(1)} %shard_map.54), channel_id=2, replica_groups=mesh['y'=8,'x'=4,'zh'=4,'zl'=2,'c'=2] {'zh'}, dimensions={0}, use_global_device_ids=true | all-gather | bytes 716800 | tf_op jit(solution)/shard_map/all_gather | solution.py:275
  67.4 2.1 %collective-permute-start.1 = (f32[4,280,128]{2,1,0:T(8,128)S(1)}, f32[4,280,128]{2,1,0:T(8,128)S(1)}, u32[]{:S(2)}, u32[]{:S(2)}) collective-permute-start(f32[4,280,128]{2,1,0:T(8,128)S(1)} %bitcast.6), channel_id=1, source_target_pairs={{0,2},{1,15},{2,0},{3,5},{4,6},{5,3},{6,4},{7,9},{8,10},{9,7},{10,... | collective-permute-start | bytes 1720328 | tf_op jit(solution)/shard_map/ppermute | solution.py:276
  69.6 1.3 %shard_map.55.some_ref = f32[136,384]{1,0:T(8,128)S(1)} custom-call(s32[1]{0:T(128)} %bitcast.side, f32[4,280,128]{2,1,0:T(8,128)S(1)} %bitcast.7, f32[2048,128]{1,0:T(8,128)S(1)} %shard_map.50.mine, f32[2184,128]{1,0:T(8,128)S(1)} %collective-permute-done.other, f32[1,128]{1,0:T(1,128)S(1)} %bitcast.11), custom_call_target="tpu_custom_call" | custom-call | tf_op jit(solution)/shard_map/pallas_call | solution.py:32
  70.9 8.2 %collective-permute-done.1.near_ref = f32[4,280,128]{2,1,0:T(8,128)S(1)} collective-permute-done((f32[4,280,128]{2,1,0:T(8,128)S(1)}, f32[4,280,128]{2,1,0:T(8,128)S(1)}, u32[]{:S(2)}, u32[]{:S(2)}) %collective-permute-start.1) | collective-permute-done | bytes 573472 | tf_op jit(solution)/shard_map/ppermute | solution.py:276
  79.0 1.6 %shard_map.56 = (f32[136,128]{1,0:T(8,128)S(1)}, f32[5,128,128]{2,1,0:T(8,128)S(1)}) custom-call(s32[1]{0:T(128)} %bitcast.side, f32[4,280,128]{2,1,0:T(8,128)S(1)} %collective-permute-done.1.near_ref, f32[4,280,128]{2,1,0:T(8,128)S(1)} %bitcast.8, f32[136,384]{1,0:T(8,128)S(1)} %shard_map.55.some_ref, f32[2048,128]{1,0:T(8,128)S(1)} %shard_map.50.mine, ...), custom_call_target="tpu_custom_call" | custom-call | tf_op jit(solution)/shard_map/pallas_call | solution.py:32
  80.7 1.9 %collective-permute-start.2 = (f32[136,128]{1,0:T(8,128)S(1)}, f32[136,128]{1,0:T(8,128)S(1)}, u32[]{:S(2)}, u32[]{:S(2)}) collective-permute-start(f32[136,128]{1,0:T(8,128)S(1)} %get-tuple-element.7), channel_id=1, source_target_pairs={{0,1},{1,0},{2,3},{3,2},{4,5},{5,4},{6,7},{7,6},{8,9},{9,8},{10,11... | collective-permute-start | bytes 208904 | tf_op jit(solution)/shard_map/ppermute | solution.py:284
  82.6 0.5 shard_map.57.a_ref
  83.1 0.8 collective-permute-done.2.b_ref
  83.9 19.9 %all_to_all.16.in_ref = f32[32,8,128]{2,1,0:T(8,128)S(1)} all-to-all(f32[32,8,128]{2,1,0:T(8,128)S(1)} %shard_map.58), channel_id=1, replica_groups=mesh['y'=8,'x'=4,'zh'=4,'zl'=2,'c'=2] {'y','x'}, dimensions={0} | all-to-all | bytes 262144 | tf_op jit(solution)/shard_map/all_to_all | solution.py:288
  103.8 13.7 %all_to_all.17.in_ref = f32[32,8,128]{2,1,0:T(8,128)S(1)} all-to-all(f32[32,8,128]{2,1,0:T(8,128)S(1)} %shard_map.59), channel_id=1, replica_groups=mesh['y'=8,'x'=4,'zh'=4,'zl'=2,'c'=2] {'y','x'}, dimensions={0} | all-to-all | bytes 262144 | tf_op jit(solution)/shard_map/all_to_all | solution.py:290
  117.5 0.6 shard_map.60
  (2 shorter events, 0.1 us)
Async XLA Ops:
  2.0 4.7 %collective-permute-start = (f32[2184,128]{1,0:T(8,128)S(1)}, f32[2184,128]{1,0:T(8,128)S(1)}, u32[]{:S(2)}, u32[]{:S(2)}) collective-permute-start(f32[2184,128]{1,0:T(8,128)S(1)} %shard_map.52), channel_id=1, source_target_pairs={{0,1},{1,0},{2,3},{3,2},{4,5},{5,4},{6,7},{7,6},{8,9},{9,8},{10,11... | collective-permute-start | bytes 3354632 | tf_op jit(solution)/shard_map/ppermute | solution.py:268
  3.9 1.4 %copy-start = (f32[128,128]{1,0:T(8,128)S(1)}, f32[128,128]{1,0:T(8,128)}, u32[]{:S(2)}) copy-start(f32[128,128]{1,0:T(8,128)} %loading_ref.5) | copy-start | bytes 196612
  3.9 1.4 %copy-start.1 = (f32[128]{0:T(128)S(1)}, f32[128]{0:T(128)}, u32[]{:S(2)}) copy-start(f32[128]{0:T(128)} %param.4) | copy-start | bytes 1540
  67.4 11.6 %collective-permute-start.1 = (f32[4,280,128]{2,1,0:T(8,128)S(1)}, f32[4,280,128]{2,1,0:T(8,128)S(1)}, u32[]{:S(2)}, u32[]{:S(2)}) collective-permute-start(f32[4,280,128]{2,1,0:T(8,128)S(1)} %bitcast.6), channel_id=1, source_target_pairs={{0,2},{1,15},{2,0},{3,5},{4,6},{5,3},{6,4},{7,9},{8,10},{9,7},{10,... | collective-permute-start | bytes 1720328 | tf_op jit(solution)/shard_map/ppermute | solution.py:276
  80.7 3.2 %collective-permute-start.2 = (f32[136,128]{1,0:T(8,128)S(1)}, f32[136,128]{1,0:T(8,128)S(1)}, u32[]{:S(2)}, u32[]{:S(2)}) collective-permute-start(f32[136,128]{1,0:T(8,128)S(1)} %get-tuple-element.7), channel_id=1, source_target_pairs={{0,1},{1,0},{2,3},{3,2},{4,5},{5,4},{6,7},{7,6},{8,9},{9,8},{10,11... | collective-permute-start | bytes 208904 | tf_op jit(solution)/shard_map/ppermute | solution.py:284

commit v8 on v7

--- a/solution.py
+++ b/solution.py
@@ -252,7 +252,7 @@
     channels = counts.shape[1] * PARTS * 2
     height = counts.shape[0] // 2 // PARTS + 8 + comps // PARTS
     core = lax.axis_index("c").astype(jnp.int32)
-    side = lax.axis_index("zl").astype(jnp.int32).reshape(1)
+    side = (lax.axis_index("zl") ^ lax.axis_index("c")).astype(jnp.int32).reshape(1)
     offset = offset.reshape(1, comps)
 
     swap = [(0, 1), (1, 0)]
@@ -261,6 +261,15 @@
         for c in range(2):
             partner = (((z - c) % PARTS ^ 1) + c) % PARTS
             near_pairs.append((2 * z + c, 2 * partner + c))
+
+    rings = [[2 * z for z in range(PARTS)], [2 * z + 1 for z in reversed(range(PARTS))]]
+    rings4 = [ring[k::2] for ring in rings for k in range(2)]
+    plane = lax.axis_size(WIDE)
+    planes = [
+        [2 * (PARTS * p + z) + c for p in (reversed(range(plane)) if c else range(plane))]
+        for z in range(PARTS)
+        for c in range(2)
+    ]
 
     half = counts.shape[0] // 2
     scratch = [pltpu.VMEM((1, comps), F32), pltpu.SemaphoreType.DMA((4,))]
@@ -270,9 +279,9 @@
     block = whole(PARTS, height, comps)
     partial = call(encode_body, block, mine, loading, offset)
     partial = call(encode_last_body, block, partial, other)
-    gathered = lax.all_to_all(partial, ("zh", "zl"), 0, 0)
+    gathered = lax.all_to_all(partial, DEEP, 0, 0, axis_index_groups=rings)
     own = call(functools.partial(finish_body, channels), whole(height, comps), gathered)
-    scores = lax.all_gather(own, "zh", axis=0)
+    scores = lax.all_gather(own, DEEP, axis=0, axis_index_groups=rings4)
     near = lax.ppermute(scores, DEEP, near_pairs)
     some = call(
         some_grad_body, whole(comps + 8, 3 * comps), side, scores, mine, other, offset, scalars=1
@@ -283,11 +292,10 @@
     )
     arrived = lax.ppermute(grad_other, "c", swap)
     grad_mine = call(mine_grad_body, shape, rest, loading)
-    plane = lax.axis_size(WIDE)
     pieces = call(deal_body, whole(plane, 8, comps), grad_mine, arrived)
-    pieces = lax.all_to_all(pieces, WIDE, 0, 0)
+    pieces = lax.all_to_all(pieces, AXES, 0, 0, axis_index_groups=planes)
     pieces = call(functools.partial(gather_body, pixels), whole(plane, 8, comps), pieces)
-    pieces = lax.all_to_all(pieces, WIDE, 0, 0)
+    pieces = lax.all_to_all(pieces, AXES, 0, 0, axis_index_groups=planes)
     grad, grad_offset = call(last_body, (whole(comps, comps), whole(1, comps)), pieces)
     return grad, grad_offset.reshape(comps)
 

time: 118 us -> 116 us (0.983)
  the two profiles are of different devices: /device:TPU:8 before, /device:TPU:128 now
where the time goes in v8:
time: 116 us; the launch traced here: 115 us
  blocking collectives  90 us (78%)
  Pallas kernels  9.42 us (8%)
  waiting for transfers between devices  9.29 us (8%)
  starting transfers between devices  5.75 us (5%)
    all_to_all x1, blocking collectives, on_device(): gathered = lax.all_to_all(partial, DEEP, 0, 0, axis_index_groups=rings)  36.8 us
    all_to_all x2, blocking collectives, on_device(): pieces = lax.all_to_all(pieces, AXES, 0, 0, axis_index_groups=planes)  34.2 us
    all_gather x1, blocking collectives, on_device(): scores = lax.all_gather(own, DEEP, axis=0, axis_index_groups=rings4)  19 us
    ppermute x1, waiting for transfers between devices, on_device(): near = lax.ppermute(scores, DEEP, near_pairs)  8.38 us
    pallas_call x9, Pallas kernels, call(): pl.pallas_call(body, out_shape=out_shape, in_specs=[pl.BlockSpec(memory_s...  6.69 us
    pallas_call x2, Pallas kernels, cut(): pl.pallas_call(body, out_shape=whole(height, width), in_specs=[pl.BlockSp...  2.72 us
  transfers between devices with their start and end apart: 3, of which 3 were waited for; matrix products, arithmetic and copies ran while one was open for 0% of the time, Pallas kernels for 4%

profile of v8, /device:TPU:128, one launch (start us, length us, event | category | flops | bytes accessed | tf_op | source)
XLA Modules:
  0.0 115.2 jit_solution(12768858789148792546)
XLA Ops:
  0.6 1.3 %shard_map.52 = f32[2184,128]{1,0:T(8,128)S(1)} custom-call(s32[1]{0:T(128)} %bitcast.3.which, f32[4096,128]{1,0:T(8,128)} %counts_ref.3, f32[128,128]{1,0:T(8,128)} %loading_ref.5, f32[1,128]{1,0:T(1,128)} %bitcast.9), custom_call_target="tpu_custom_call" | custom-call | tf_op jit(solution)/shard_map/pallas_call | solution.py:75
  2.0 1.9 %collective-permute-start = (f32[2184,128]{1,0:T(8,128)S(1)}, f32[2184,128]{1,0:T(8,128)S(1)}, u32[]{:S(2)}, u32[]{:S(2)}) collective-permute-start(f32[2184,128]{1,0:T(8,128)S(1)} %shard_map.52), channel_id=1, source_target_pairs={{0,1},{1,0},{2,3},{3,2},{4,5},{5,4},{6,7},{7,6},{8,9},{9,8},{10,11... | collective-permute-start | bytes 3354632 | tf_op jit(solution)/shard_map/ppermute | solution.py:277
  3.9 0.0 copy-start
  3.9 0.0 copy-start.1
  3.9 1.4 %shard_map.50.mine = f32[2048,128]{1,0:T(8,128)S(1)} custom-call(s32[1]{0:T(128)} %bitcast.1.which, f32[4096,128]{1,0:T(8,128)} %counts_ref.3), custom_call_target="tpu_custom_call" | custom-call | tf_op jit(solution)/shard_map/pallas_call | solution.py:75
  5.3 0.0 copy-done
  5.3 0.0 copy-done.1
  5.3 1.1 shard_map.51.in_ref
  6.5 0.1 collective-permute-done.other
  6.6 1.1 shard_map.53
  7.8 36.8 %all_to_all.15.in_ref = f32[8,280,128]{2,1,0:T(8,128)S(1)} all-to-all(f32[8,280,128]{2,1,0:T(8,128)S(1)} %shard_map.53), channel_id=1, replica_groups={{0,2,4,6,8,10,12,14},{15,13,11,9,7,5,3,1},{16,18,20,22,24,26,28,30},{31..., dimensions={0} | all-to-all | bytes 2293760 | tf_op jit(solution)/shard_map/all_to_all | solution.py:282
  44.5 0.3 shard_map.54
  44.9 19.0 %all-gather = f32[1120,128]{1,0:T(8,128)S(1)} all-gather(f32[280,128]{1,0:T(8,128)S(1)} %shard_map.54), channel_id=2, replica_groups={{0,4,8,12},{2,6,10,14},{15,11,7,3},{13,9,5,1},{16,20,24,28},{18,22,26,3..., dimensions={0}, use_global_device_ids=true | all-gather | bytes 716800 | tf_op jit(solution)/shard_map/all_gather | solution.py:284
  63.9 1.9 %collective-permute-start.1 = (f32[4,280,128]{2,1,0:T(8,128)S(1)}, f32[4,280,128]{2,1,0:T(8,128)S(1)}, u32[]{:S(2)}, u32[]{:S(2)}) collective-permute-start(f32[4,280,128]{2,1,0:T(8,128)S(1)} %bitcast.6), channel_id=1, source_target_pairs={{0,2},{1,15},{2,0},{3,5},{4,6},{5,3},{6,4},{7,9},{8,10},{9,7},{10,... | collective-permute-start | bytes 1720328 | tf_op jit(solution)/shard_map/ppermute | solution.py:285
  65.8 1.3 %shard_map.55.some_ref = f32[136,384]{1,0:T(8,128)S(1)} custom-call(s32[1]{0:T(128)} %bitcast.side, f32[4,280,128]{2,1,0:T(8,128)S(1)} %bitcast.7, f32[2048,128]{1,0:T(8,128)S(1)} %shard_map.50.mine, f32[2184,128]{1,0:T(8,128)S(1)} %collective-permute-done.other, f32[1,128]{1,0:T(1,128)S(1)} %bitcast.11), custom_call_target="tpu_custom_call" | custom-call | tf_op jit(solution)/shard_map/pallas_call | solution.py:32
  67.1 8.4 %collective-permute-done.1.near_ref = f32[4,280,128]{2,1,0:T(8,128)S(1)} collective-permute-done((f32[4,280,128]{2,1,0:T(8,128)S(1)}, f32[4,280,128]{2,1,0:T(8,128)S(1)}, u32[]{:S(2)}, u32[]{:S(2)}) %collective-permute-start.1) | collective-permute-done | bytes 573472 | tf_op jit(solution)/shard_map/ppermute | solution.py:285
  75.5 1.6 %shard_map.56 = (f32[136,128]{1,0:T(8,128)S(1)}, f32[5,128,128]{2,1,0:T(8,128)S(1)}) custom-call(s32[1]{0:T(128)} %bitcast.side, f32[4,280,128]{2,1,0:T(8,128)S(1)} %collective-permute-done.1.near_ref, f32[4,280,128]{2,1,0:T(8,128)S(1)} %bitcast.8, f32[136,384]{1,0:T(8,128)S(1)} %shard_map.55.some_ref, f32[2048,128]{1,0:T(8,128)S(1)} %shard_map.50.mine, ...), custom_call_target="tpu_custom_call" | custom-call | tf_op jit(solution)/shard_map/pallas_call | solution.py:32
  77.1 1.9 %collective-permute-start.2 = (f32[136,128]{1,0:T(8,128)S(1)}, f32[136,128]{1,0:T(8,128)S(1)}, u32[]{:S(2)}, u32[]{:S(2)}) collective-permute-start(f32[136,128]{1,0:T(8,128)S(1)} %get-tuple-element.7), channel_id=1, source_target_pairs={{0,1},{1,0},{2,3},{3,2},{4,5},{5,4},{6,7},{7,6},{8,9},{9,8},{10,11... | collective-permute-start | bytes 208904 | tf_op jit(solution)/shard_map/ppermute | solution.py:293
  79.1 0.5 shard_map.57.a_ref
  79.5 0.8 collective-permute-done.2.b_ref
  80.3 20.2 %all_to_all.16.in_ref = f32[32,8,128]{2,1,0:T(8,128)S(1)} all-to-all(f32[32,8,128]{2,1,0:T(8,128)S(1)} %shard_map.58), channel_id=1, replica_groups={{0,16,32,48,64,80,96,112,128,144,160,176,192,208,224,240,256,272,288,30..., dimensions={0} | all-to-all | bytes 262144 | tf_op jit(solution)/shard_map/all_to_all | solution.py:296
  100.6 14.0 %all_to_all.17.in_ref = f32[32,8,128]{2,1,0:T(8,128)S(1)} all-to-all(f32[32,8,128]{2,1,0:T(8,128)S(1)} %shard_map.59), channel_id=1, replica_groups={{0,16,32,48,64,80,96,112,128,144,160,176,192,208,224,240,256,272,288,30..., dimensions={0} | all-to-all | bytes 262144 | tf_op jit(solution)/shard_map/all_to_all | solution.py:298
  114.6 0.6 shard_map.60
  (2 shorter events, 0.1 us)
Async XLA Ops:
  2.0 4.7 %collective-permute-start = (f32[2184,128]{1,0:T(8,128)S(1)}, f32[2184,128]{1,0:T(8,128)S(1)}, u32[]{:S(2)}, u32[]{:S(2)}) collective-permute-start(f32[2184,128]{1,0:T(8,128)S(1)} %shard_map.52), channel_id=1, source_target_pairs={{0,1},{1,0},{2,3},{3,2},{4,5},{5,4},{6,7},{7,6},{8,9},{9,8},{10,11... | collective-permute-start | bytes 3354632 | tf_op jit(solution)/shard_map/ppermute | solution.py:277
  3.9 1.4 %copy-start = (f32[128,128]{1,0:T(8,128)S(1)}, f32[128,128]{1,0:T(8,128)}, u32[]{:S(2)}) copy-start(f32[128,128]{1,0:T(8,128)} %loading_ref.5) | copy-start | bytes 196612
  3.9 1.4 %copy-start.1 = (f32[128]{0:T(128)S(1)}, f32[128]{0:T(128)}, u32[]{:S(2)}) copy-start(f32[128]{0:T(128)} %param.4) | copy-start | bytes 1540
  63.9 11.6 %collective-permute-start.1 = (f32[4,280,128]{2,1,0:T(8,128)S(1)}, f32[4,280,128]{2,1,0:T(8,128)S(1)}, u32[]{:S(2)}, u32[]{:S(2)}) collective-permute-start(f32[4,280,128]{2,1,0:T(8,128)S(1)} %bitcast.6), channel_id=1, source_target_pairs={{0,2},{1,15},{2,0},{3,5},{4,6},{5,3},{6,4},{7,9},{8,10},{9,7},{10,... | collective-permute-start | bytes 1720328 | tf_op jit(solution)/shard_map/ppermute | solution.py:285
  77.1 3.2 %collective-permute-start.2 = (f32[136,128]{1,0:T(8,128)S(1)}, f32[136,128]{1,0:T(8,128)S(1)}, u32[]{:S(2)}, u32[]{:S(2)}) collective-permute-start(f32[136,128]{1,0:T(8,128)S(1)} %get-tuple-element.7), channel_id=1, source_target_pairs={{0,1},{1,0},{2,3},{3,2},{4,5},{5,4},{6,7},{7,6},{8,9},{9,8},{10,11... | collective-permute-start | bytes 208904 | tf_op jit(solution)/shard_map/ppermute | solution.py:293

commit v9 on v8

--- a/solution.py
+++ b/solution.py
@@ -252,7 +252,7 @@
     channels = counts.shape[1] * PARTS * 2
     height = counts.shape[0] // 2 // PARTS + 8 + comps // PARTS
     core = lax.axis_index("c").astype(jnp.int32)
-    side = (lax.axis_index("zl") ^ lax.axis_index("c")).astype(jnp.int32).reshape(1)
+    side = lax.axis_index("zl").astype(jnp.int32).reshape(1)
     offset = offset.reshape(1, comps)
 
     swap = [(0, 1), (1, 0)]
@@ -262,8 +262,6 @@
             partner = (((z - c) % PARTS ^ 1) + c) % PARTS
             near_pairs.append((2 * z + c, 2 * partner + c))
 
-    rings = [[2 * z for z in range(PARTS)], [2 * z + 1 for z in reversed(range(PARTS))]]
-    rings4 = [ring[k::2] for ring in rings for k in range(2)]
     plane = lax.axis_size(WIDE)
     planes = [
         [2 * (PARTS * p + z) + c for p in (reversed(range(plane)) if c else range(plane))]
@@ -279,9 +277,9 @@
     block = whole(PARTS, height, comps)
     partial = call(encode_body, block, mine, loading, offset)
     partial = call(encode_last_body, block, partial, other)
-    gathered = lax.all_to_all(partial, DEEP, 0, 0, axis_index_groups=rings)
+    gathered = lax.all_to_all(partial, ("zh", "zl"), 0, 0)
     own = call(functools.partial(finish_body, channels), whole(height, comps), gathered)
-    scores = lax.all_gather(own, DEEP, axis=0, axis_index_groups=rings4)
+    scores = lax.all_gather(own, "zh", axis=0)
     near = lax.ppermute(scores, DEEP, near_pairs)
     some = call(
         some_grad_body, whole(comps + 8, 3 * comps), side, scores, mine, other, offset, scalars=1

time: 116 us -> 118 us (1.017)
  the two profiles are of different devices: /device:TPU:128 before, /device:TPU:8 now
where the time goes in v9:
time: 118 us
  blocking collectives  92.8 us (79%)
  Pallas kernels  9.42 us (8%)
  waiting for transfers between devices  9.07 us (8%)
  starting transfers between devices  5.97 us (5%)
    all_to_all x1, blocking collectives, on_device(): gathered = lax.all_to_all(partial, ('zh', 'zl'), 0, 0)  41.5 us
    all_to_all x2, blocking collectives, on_device(): pieces = lax.all_to_all(pieces, AXES, 0, 0, axis_index_groups=planes)  33.5 us
    all_gather x1, blocking collectives, on_device(): scores = lax.all_gather(own, 'zh', axis=0)  17.8 us
    ppermute x1, waiting for transfers between devices, on_device(): near = lax.ppermute(scores, DEEP, near_pairs)  8.17 us
    pallas_call x9, Pallas kernels, call(): pl.pallas_call(body, out_shape=out_shape, in_specs=[pl.BlockSpec(memory_s...  6.7 us
    pallas_call x2, Pallas kernels, cut(): pl.pallas_call(body, out_shape=whole(height, width), in_specs=[pl.BlockSp...  2.73 us
  transfers between devices with their start and end apart: 3, of which 3 were waited for; matrix products, arithmetic and copies ran while one was open for 0% of the time, Pallas kernels for 4%

profile of v9, /device:TPU:8, one launch (start us, length us, event | category | flops | bytes accessed | tf_op | source)
XLA Modules:
  0.0 118.0 jit_solution(501380109496441874)
XLA Ops:
  0.6 1.3 %shard_map.52 = f32[2184,128]{1,0:T(8,128)S(1)} custom-call(s32[1]{0:T(128)} %bitcast.3.which, f32[4096,128]{1,0:T(8,128)} %counts_ref.3, f32[128,128]{1,0:T(8,128)} %loading_ref.5, f32[1,128]{1,0:T(1,128)} %bitcast.9), custom_call_target="tpu_custom_call" | custom-call | tf_op jit(solution)/shard_map/pallas_call | solution.py:75
  2.0 1.9 %collective-permute-start = (f32[2184,128]{1,0:T(8,128)S(1)}, f32[2184,128]{1,0:T(8,128)S(1)}, u32[]{:S(2)}, u32[]{:S(2)}) collective-permute-start(f32[2184,128]{1,0:T(8,128)S(1)} %shard_map.52), channel_id=1, source_target_pairs={{0,1},{1,0},{2,3},{3,2},{4,5},{5,4},{6,7},{7,6},{8,9},{9,8},{10,11... | collective-permute-start | bytes 3354632 | tf_op jit(solution)/shard_map/ppermute | solution.py:275
  3.9 0.0 copy-start
  3.9 0.0 copy-start.1
  3.9 1.4 %shard_map.50.mine = f32[2048,128]{1,0:T(8,128)S(1)} custom-call(s32[1]{0:T(128)} %bitcast.1.which, f32[4096,128]{1,0:T(8,128)} %counts_ref.3), custom_call_target="tpu_custom_call" | custom-call | tf_op jit(solution)/shard_map/pallas_call | solution.py:75
  5.3 0.0 copy-done
  5.3 0.0 copy-done.1
  5.3 1.1 shard_map.51.in_ref
  6.5 0.1 collective-permute-done.other
  6.6 1.1 shard_map.53
  7.8 41.5 %all_to_all.15.in_ref = f32[8,280,128]{2,1,0:T(8,128)S(1)} all-to-all(f32[8,280,128]{2,1,0:T(8,128)S(1)} %shard_map.53), channel_id=1, replica_groups=mesh['y'=8,'x'=4,'zh'=4,'zl'=2,'c'=2] {'zh','zl'}, dimensions={0} | all-to-all | bytes 2293760 | tf_op jit(solution)/shard_map/all_to_all | solution.py:280
  49.2 0.3 shard_map.54
  49.6 17.8 %all-gather = f32[1120,128]{1,0:T(8,128)S(1)} all-gather(f32[280,128]{1,0:T(8,128)S(1)} %shard_map.54), channel_id=2, replica_groups=mesh['y'=8,'x'=4,'zh'=4,'zl'=2,'c'=2] {'zh'}, dimensions={0}, use_global_device_ids=true | all-gather | bytes 716800 | tf_op jit(solution)/shard_map/all_gather | solution.py:282
  67.4 2.1 %collective-permute-start.1 = (f32[4,280,128]{2,1,0:T(8,128)S(1)}, f32[4,280,128]{2,1,0:T(8,128)S(1)}, u32[]{:S(2)}, u32[]{:S(2)}) collective-permute-start(f32[4,280,128]{2,1,0:T(8,128)S(1)} %bitcast.6), channel_id=1, source_target_pairs={{0,2},{1,15},{2,0},{3,5},{4,6},{5,3},{6,4},{7,9},{8,10},{9,7},{10,... | collective-permute-start | bytes 1720328 | tf_op jit(solution)/shard_map/ppermute | solution.py:283
  69.6 1.3 %shard_map.55.some_ref = f32[136,384]{1,0:T(8,128)S(1)} custom-call(s32[1]{0:T(128)} %bitcast.side, f32[4,280,128]{2,1,0:T(8,128)S(1)} %bitcast.7, f32[2048,128]{1,0:T(8,128)S(1)} %shard_map.50.mine, f32[2184,128]{1,0:T(8,128)S(1)} %collective-permute-done.other, f32[1,128]{1,0:T(1,128)S(1)} %bitcast.11), custom_call_target="tpu_custom_call" | custom-call | tf_op jit(solution)/shard_map/pallas_call | solution.py:32
  70.9 8.2 %collective-permute-done.1.near_ref = f32[4,280,128]{2,1,0:T(8,128)S(1)} collective-permute-done((f32[4,280,128]{2,1,0:T(8,128)S(1)}, f32[4,280,128]{2,1,0:T(8,128)S(1)}, u32[]{:S(2)}, u32[]{:S(2)}) %collective-permute-start.1) | collective-permute-done | bytes 573472 | tf_op jit(solution)/shard_map/ppermute | solution.py:283
  79.0 1.6 %shard_map.56 = (f32[136,128]{1,0:T(8,128)S(1)}, f32[5,128,128]{2,1,0:T(8,128)S(1)}) custom-call(s32[1]{0:T(128)} %bitcast.side, f32[4,280,128]{2,1,0:T(8,128)S(1)} %collective-permute-done.1.near_ref, f32[4,280,128]{2,1,0:T(8,128)S(1)} %bitcast.8, f32[136,384]{1,0:T(8,128)S(1)} %shard_map.55.some_ref, f32[2048,128]{1,0:T(8,128)S(1)} %shard_map.50.mine, ...), custom_call_target="tpu_custom_call" | custom-call | tf_op jit(solution)/shard_map/pallas_call | solution.py:32
  80.7 1.9 %collective-permute-start.2 = (f32[136,128]{1,0:T(8,128)S(1)}, f32[136,128]{1,0:T(8,128)S(1)}, u32[]{:S(2)}, u32[]{:S(2)}) collective-permute-start(f32[136,128]{1,0:T(8,128)S(1)} %get-tuple-element.7), channel_id=1, source_target_pairs={{0,1},{1,0},{2,3},{3,2},{4,5},{5,4},{6,7},{7,6},{8,9},{9,8},{10,11... | collective-permute-start | bytes 208904 | tf_op jit(solution)/shard_map/ppermute | solution.py:291
  82.6 0.5 shard_map.57.a_ref
  83.1 0.8 collective-permute-done.2.b_ref
  83.9 19.5 %all_to_all.16.in_ref = f32[32,8,128]{2,1,0:T(8,128)S(1)} all-to-all(f32[32,8,128]{2,1,0:T(8,128)S(1)} %shard_map.58), channel_id=1, replica_groups={{0,16,32,48,64,80,96,112,128,144,160,176,192,208,224,240,256,272,288,30..., dimensions={0} | all-to-all | bytes 262144 | tf_op jit(solution)/shard_map/all_to_all | solution.py:294
  103.4 14.0 %all_to_all.17.in_ref = f32[32,8,128]{2,1,0:T(8,128)S(1)} all-to-all(f32[32,8,128]{2,1,0:T(8,128)S(1)} %shard_map.59), channel_id=1, replica_groups={{0,16,32,48,64,80,96,112,128,144,160,176,192,208,224,240,256,272,288,30..., dimensions={0} | all-to-all | bytes 262144 | tf_op jit(solution)/shard_map/all_to_all | solution.py:296
  117.4 0.6 shard_map.60
  (2 shorter events, 0.1 us)
Async XLA Ops:
  2.0 4.7 %collective-permute-start = (f32[2184,128]{1,0:T(8,128)S(1)}, f32[2184,128]{1,0:T(8,128)S(1)}, u32[]{:S(2)}, u32[]{:S(2)}) collective-permute-start(f32[2184,128]{1,0:T(8,128)S(1)} %shard_map.52), channel_id=1, source_target_pairs={{0,1},{1,0},{2,3},{3,2},{4,5},{5,4},{6,7},{7,6},{8,9},{9,8},{10,11... | collective-permute-start | bytes 3354632 | tf_op jit(solution)/shard_map/ppermute | solution.py:275
  3.9 1.4 %copy-start = (f32[128,128]{1,0:T(8,128)S(1)}, f32[128,128]{1,0:T(8,128)}, u32[]{:S(2)}) copy-start(f32[128,128]{1,0:T(8,128)} %loading_ref.5) | copy-start | bytes 196612
  3.9 1.4 %copy-start.1 = (f32[128]{0:T(128)S(1)}, f32[128]{0:T(128)}, u32[]{:S(2)}) copy-start(f32[128]{0:T(128)} %param.4) | copy-start | bytes 1540
  67.4 11.6 %collective-permute-start.1 = (f32[4,280,128]{2,1,0:T(8,128)S(1)}, f32[4,280,128]{2,1,0:T(8,128)S(1)}, u32[]{:S(2)}, u32[]{:S(2)}) collective-permute-start(f32[4,280,128]{2,1,0:T(8,128)S(1)} %bitcast.6), channel_id=1, source_target_pairs={{0,2},{1,15},{2,0},{3,5},{4,6},{5,3},{6,4},{7,9},{8,10},{9,7},{10,... | collective-permute-start | bytes 1720328 | tf_op jit(solution)/shard_map/ppermute | solution.py:283
  80.7 3.2 %collective-permute-start.2 = (f32[136,128]{1,0:T(8,128)S(1)}, f32[136,128]{1,0:T(8,128)S(1)}, u32[]{:S(2)}, u32[]{:S(2)}) collective-permute-start(f32[136,128]{1,0:T(8,128)S(1)} %get-tuple-element.7), channel_id=1, source_target_pairs={{0,1},{1,0},{2,3},{3,2},{4,5},{5,4},{6,7},{7,6},{8,9},{9,8},{10,11... | collective-permute-start | bytes 208904 | tf_op jit(solution)/shard_map/ppermute | solution.py:291

commit v10 on v8

--- a/solution.py
+++ b/solution.py
@@ -82,9 +82,32 @@
     )(which.reshape(1), *(pltpu.with_memory_space_constraint(a, pltpu.HBM) for a in (counts,) + more))
 
 
+def fold(gram):
+    half = gram.shape[0] // 2
+    row = lax.broadcasted_iota(jnp.int32, (half, 2 * half), 0)
+    col = lax.broadcasted_iota(jnp.int32, (half, 2 * half), 1)
+    low = pltpu.roll(gram[half:, :], half, 1)
+    folded = jnp.where((col < half) & (col > row), low, gram[:half, :])
+    return folded, jnp.sum(jnp.where(col == row, low, 0.0), axis=0, keepdims=True)
+
+
+def unfold(folded, diagonal):
+    half = folded.shape[0]
+    row = lax.broadcasted_iota(jnp.int32, (half, 2 * half), 0)
+    col = lax.broadcasted_iota(jnp.int32, (half, 2 * half), 1)
+    turned = jnp.concatenate([folded, jnp.zeros_like(folded)], axis=0).T
+    high = jnp.where((col < half) & (col > row), turned[:half, :], folded)
+    right = jnp.where(
+        col - half > row,
+        pltpu.roll(folded, half, 1),
+        pltpu.roll(jnp.where(col == row, diagonal, turned[:half, :]), half, 1),
+    )
+    return jnp.concatenate([high, jnp.where(col < half, turned[half:, :], right)], axis=0)
+
+
 def source_terms(load, off):
     bar = jnp.sum(load, axis=0, keepdims=True) / load.shape[0]
-    return bar, load - bar, mult(off, load)[0:1, :], mult(load, load, ((0,), (0,)))
+    return bar, load - bar, mult(off, load)[0:1, :], fold(mult(load, load, ((0,), (0,))))
 
 
 def log_sums(logs):
@@ -97,8 +120,8 @@
 
 def encode_body(mine, loading_ref, offset_ref, out_ref):
     total, comps = mine.shape
-    rows, share = total // PARTS, comps // PARTS
-    bar, bare, shift, gram = source_terms(
+    rows, share = total // PARTS, comps // 2 // PARTS
+    bar, bare, shift, (gram, diagonal) = source_terms(
         loading_ref[...], jnp.broadcast_to(offset_ref[...], (8, comps))
     )
     blank = jnp.zeros((1, comps), F32)
@@ -106,17 +129,17 @@
         logs = mine[j * rows : (j + 1) * rows, :]
         out_ref[j, 0:rows, :] = mult(logs, bare)
         out_ref[j, rows : rows + 8, :] = jnp.concatenate(
-            log_sums(logs) + [blank, blank, bar, blank, shift, blank], axis=0
+            log_sums(logs) + [blank, blank, bar, blank, shift, diagonal], axis=0
         )
         out_ref[j, rows + 8 : rows + 8 + share, :] = gram[j * share : (j + 1) * share, :]
 
 
 def encode_last_body(in_ref, other, out_ref):
     height, comps = in_ref.shape[1:]
-    share = comps // PARTS
+    share = comps // 2 // PARTS
     rows = height - 8 - share
     total = PARTS * rows
-    bar, bare, shift, gram = source_terms(
+    bar, bare, shift, (gram, diagonal) = source_terms(
         other[total : total + comps, :], other[total + comps : total + comps + 8, :]
     )
     blank = jnp.zeros((1, comps), F32)
@@ -124,7 +147,7 @@
         logs = other[j * rows : (j + 1) * rows, :]
         out_ref[j, 0:rows, :] = in_ref[j, 0:rows, :] + mult(logs, bare)
         out_ref[j, rows : rows + 8, :] = in_ref[j, rows : rows + 8, :] + jnp.concatenate(
-            [blank, blank] + log_sums(logs) + [blank, bar, shift, blank], axis=0
+            [blank, blank] + log_sums(logs) + [blank, bar, shift, diagonal], axis=0
         )
         at = rows + 8
         out_ref[j, at : at + share, :] = in_ref[j, at : at + share, :] + gram[j * share : (j + 1) * share, :]
@@ -132,7 +155,7 @@
 
 def finish_body(channels, in_ref, out_ref):
     height, comps = in_ref.shape[1:]
-    share = comps // PARTS
+    share = comps // 2 // PARTS
     rows = height - 8 - share
     group = channels // (2 * PARTS)
     bars = jnp.concatenate([in_ref[j, rows + 4 : rows + 6, :] for j in range(PARTS)], axis=0)
@@ -154,13 +177,14 @@
             total += in_ref[j, at : at + comps, :]
         out_ref[at : at + comps, :] = total
         geos.append(geo)
-    out_ref[rows : rows + 8, :] = jnp.concatenate(geos + [jnp.zeros((6, comps), F32)], axis=0)
+    diagonal = sum(in_ref[j, rows + 7 : rows + 8, :] for j in range(PARTS))
+    out_ref[rows : rows + 8, :] = jnp.concatenate(geos + [diagonal, jnp.zeros((5, comps), F32)], axis=0)
     out_ref[rows + 8 : rows + 8 + share, :] = sum(in_ref[j, rows + 8 : rows + 8 + share, :] for j in range(PARTS))
 
 
 def block_terms(first, in_ref, logs, offs):
     blocks, height, comps = in_ref.shape
-    rows = height - 8 - comps // PARTS
+    rows = height - 8 - comps // 2 // PARTS
     wide, sums = 0.0, 0.0
     for j in range(blocks):
         s = in_ref[j, 0:rows, :]
@@ -189,7 +213,7 @@
 def grad_body(side, near_ref, in_ref, some_ref, mine, other, offset_ref, out_ref, rest_ref):
     total, comps = mine.shape
     height = in_ref.shape[1]
-    share = comps // PARTS
+    share = comps // 2 // PARTS
     rows = height - 8 - share
     offs = (offset_ref[...], other[total + comps : total + comps + 1, :])
     wide, sums = block_terms(1 - side[0], near_ref, (mine, other), offs)
@@ -197,6 +221,7 @@
     here = [a[j, rows + 8 : rows + 8 + share, :] for j in range(PARTS // 2) for a in (in_ref, near_ref)]
     there = [a[j, rows + 8 : rows + 8 + share, :] for j in range(PARTS // 2) for a in (near_ref, in_ref)]
     gram = jnp.where(side[0] == 0, jnp.concatenate(here, axis=0), jnp.concatenate(there, axis=0))
+    gram = unfold(gram, in_ref[0, rows + 2 : rows + 3, :])
     row = lax.broadcasted_iota(jnp.int32, (comps, comps), 0)
     col = lax.broadcasted_iota(jnp.int32, (comps, comps), 1)
     hat = gram - jnp.where(row == col, 2.0, 0.0).astype(F32)
@@ -250,7 +275,7 @@
     pixels = counts.shape[0] * lax.axis_size(WIDE)
     comps = loading.shape[1]
     channels = counts.shape[1] * PARTS * 2
-    height = counts.shape[0] // 2 // PARTS + 8 + comps // PARTS
+    height = counts.shape[0] // 2 // PARTS + 8 + comps // 2 // PARTS
     core = lax.axis_index("c").astype(jnp.int32)
     side = (lax.axis_index("zl") ^ lax.axis_index("c")).astype(jnp.int32).reshape(1)
     offset = offset.reshape(1, comps)

time: 116 us -> 114 us (0.983)
  no operation moved by 1% of the time
where the time goes in v10:
time: 114 us
  blocking collectives  89.1 us (78%)
  Pallas kernels  9.42 us (8%)
  waiting for transfers between devices  9.11 us (8%)
  starting transfers between devices  5.75 us (5%)
    all_to_all x1, blocking collectives, on_device(): gathered = lax.all_to_all(partial, DEEP, 0, 0, axis_index_groups=rings)  36.1 us
    all_to_all x2, blocking collectives, on_device(): pieces = lax.all_to_all(pieces, AXES, 0, 0, axis_index_groups=planes)  34.2 us
    all_gather x1, blocking collectives, on_device(): scores = lax.all_gather(own, DEEP, axis=0, axis_index_groups=rings4)  18.8 us
    ppermute x1, waiting for transfers between devices, on_device(): near = lax.ppermute(scores, DEEP, near_pairs)  8.2 us
    pallas_call x9, Pallas kernels, call(): pl.pallas_call(body, out_shape=out_shape, in_specs=[pl.BlockSpec(memory_s...  6.7 us
    pallas_call x2, Pallas kernels, cut(): pl.pallas_call(body, out_shape=whole(height, width), in_specs=[pl.BlockSp...  2.72 us
  transfers between devices with their start and end apart: 3, of which 3 were waited for; matrix products, arithmetic and copies ran while one was open for 0% of the time, Pallas kernels for 4%

profile of v10, /device:TPU:128, one launch (start us, length us, event | category | flops | bytes accessed | tf_op | source)
XLA Modules:
  0.0 114.1 jit_solution(17615101977367026763)
XLA Ops:
  0.6 1.3 %shard_map.52 = f32[2184,128]{1,0:T(8,128)S(1)} custom-call(s32[1]{0:T(128)} %bitcast.3.which, f32[4096,128]{1,0:T(8,128)} %counts_ref.3, f32[128,128]{1,0:T(8,128)} %loading_ref.5, f32[1,128]{1,0:T(1,128)} %bitcast.9), custom_call_target="tpu_custom_call" | custom-call | tf_op jit(solution)/shard_map/pallas_call | solution.py:75
  2.0 1.9 %collective-permute-start = (f32[2184,128]{1,0:T(8,128)S(1)}, f32[2184,128]{1,0:T(8,128)S(1)}, u32[]{:S(2)}, u32[]{:S(2)}) collective-permute-start(f32[2184,128]{1,0:T(8,128)S(1)} %shard_map.52), channel_id=1, source_target_pairs={{0,1},{1,0},{2,3},{3,2},{4,5},{5,4},{6,7},{7,6},{8,9},{9,8},{10,11... | collective-permute-start | bytes 3354632 | tf_op jit(solution)/shard_map/ppermute | solution.py:302
  3.9 0.0 copy-start
  3.9 0.0 copy-start.1
  3.9 1.4 %shard_map.50.mine = f32[2048,128]{1,0:T(8,128)S(1)} custom-call(s32[1]{0:T(128)} %bitcast.1.which, f32[4096,128]{1,0:T(8,128)} %counts_ref.3), custom_call_target="tpu_custom_call" | custom-call | tf_op jit(solution)/shard_map/pallas_call | solution.py:75
  5.3 0.0 copy-done
  5.3 0.0 copy-done.1
  5.3 1.1 shard_map.51.in_ref
  6.5 0.1 collective-permute-done.other
  6.6 1.1 shard_map.53
  7.8 36.1 %all_to_all.15.in_ref = f32[8,272,128]{2,1,0:T(8,128)S(1)} all-to-all(f32[8,272,128]{2,1,0:T(8,128)S(1)} %shard_map.53), channel_id=1, replica_groups={{0,2,4,6,8,10,12,14},{15,13,11,9,7,5,3,1},{16,18,20,22,24,26,28,30},{31..., dimensions={0} | all-to-all | bytes 2228224 | tf_op jit(solution)/shard_map/all_to_all | solution.py:307
  43.8 0.3 shard_map.54
  44.2 18.8 %all-gather = f32[1088,128]{1,0:T(8,128)S(1)} all-gather(f32[272,128]{1,0:T(8,128)S(1)} %shard_map.54), channel_id=2, replica_groups={{0,4,8,12},{2,6,10,14},{15,11,7,3},{13,9,5,1},{16,20,24,28},{18,22,26,3..., dimensions={0}, use_global_device_ids=true | all-gather | bytes 696320 | tf_op jit(solution)/shard_map/all_gather | solution.py:309
  63.0 1.9 %collective-permute-start.1 = (f32[4,272,128]{2,1,0:T(8,128)S(1)}, f32[4,272,128]{2,1,0:T(8,128)S(1)}, u32[]{:S(2)}, u32[]{:S(2)}) collective-permute-start(f32[4,272,128]{2,1,0:T(8,128)S(1)} %bitcast.6), channel_id=1, source_target_pairs={{0,2},{1,15},{2,0},{3,5},{4,6},{5,3},{6,4},{7,9},{8,10},{9,7},{10,... | collective-permute-start | bytes 1671176 | tf_op jit(solution)/shard_map/ppermute | solution.py:310
  64.9 1.3 %shard_map.55.some_ref = f32[136,384]{1,0:T(8,128)S(1)} custom-call(s32[1]{0:T(128)} %bitcast.side, f32[4,272,128]{2,1,0:T(8,128)S(1)} %bitcast.7, f32[2048,128]{1,0:T(8,128)S(1)} %shard_map.50.mine, f32[2184,128]{1,0:T(8,128)S(1)} %collective-permute-done.other, f32[1,128]{1,0:T(1,128)S(1)} %bitcast.11), custom_call_target="tpu_custom_call" | custom-call | tf_op jit(solution)/shard_map/pallas_call | solution.py:32
  66.2 8.2 %collective-permute-done.1.near_ref = f32[4,272,128]{2,1,0:T(8,128)S(1)} collective-permute-done((f32[4,272,128]{2,1,0:T(8,128)S(1)}, f32[4,272,128]{2,1,0:T(8,128)S(1)}, u32[]{:S(2)}, u32[]{:S(2)}) %collective-permute-start.1) | collective-permute-done | bytes 557088 | tf_op jit(solution)/shard_map/ppermute | solution.py:310
  74.4 1.6 %shard_map.56 = (f32[136,128]{1,0:T(8,128)S(1)}, f32[5,128,128]{2,1,0:T(8,128)S(1)}) custom-call(s32[1]{0:T(128)} %bitcast.side, f32[4,272,128]{2,1,0:T(8,128)S(1)} %collective-permute-done.1.near_ref, f32[4,272,128]{2,1,0:T(8,128)S(1)} %bitcast.8, f32[136,384]{1,0:T(8,128)S(1)} %shard_map.55.some_ref, f32[2048,128]{1,0:T(8,128)S(1)} %shard_map.50.mine, ...), custom_call_target="tpu_custom_call" | custom-call | tf_op jit(solution)/shard_map/pallas_call | solution.py:32
  76.0 1.9 %collective-permute-start.2 = (f32[136,128]{1,0:T(8,128)S(1)}, f32[136,128]{1,0:T(8,128)S(1)}, u32[]{:S(2)}, u32[]{:S(2)}) collective-permute-start(f32[136,128]{1,0:T(8,128)S(1)} %get-tuple-element.7), channel_id=1, source_target_pairs={{0,1},{1,0},{2,3},{3,2},{4,5},{5,4},{6,7},{7,6},{8,9},{9,8},{10,11... | collective-permute-start | bytes 208904 | tf_op jit(solution)/shard_map/ppermute | solution.py:318
  77.9 0.5 shard_map.57.a_ref
  78.4 0.8 collective-permute-done.2.b_ref
  79.2 20.2 %all_to_all.16.in_ref = f32[32,8,128]{2,1,0:T(8,128)S(1)} all-to-all(f32[32,8,128]{2,1,0:T(8,128)S(1)} %shard_map.58), channel_id=1, replica_groups={{0,16,32,48,64,80,96,112,128,144,160,176,192,208,224,240,256,272,288,30..., dimensions={0} | all-to-all | bytes 262144 | tf_op jit(solution)/shard_map/all_to_all | solution.py:321
  99.5 14.0 %all_to_all.17.in_ref = f32[32,8,128]{2,1,0:T(8,128)S(1)} all-to-all(f32[32,8,128]{2,1,0:T(8,128)S(1)} %shard_map.59), channel_id=1, replica_groups={{0,16,32,48,64,80,96,112,128,144,160,176,192,208,224,240,256,272,288,30..., dimensions={0} | all-to-all | bytes 262144 | tf_op jit(solution)/shard_map/all_to_all | solution.py:323
  113.5 0.6 shard_map.60
  (2 shorter events, 0.1 us)
Async XLA Ops:
  2.0 4.7 %collective-permute-start = (f32[2184,128]{1,0:T(8,128)S(1)}, f32[2184,128]{1,0:T(8,128)S(1)}, u32[]{:S(2)}, u32[]{:S(2)}) collective-permute-start(f32[2184,128]{1,0:T(8,128)S(1)} %shard_map.52), channel_id=1, source_target_pairs={{0,1},{1,0},{2,3},{3,2},{4,5},{5,4},{6,7},{7,6},{8,9},{9,8},{10,11... | collective-permute-start | bytes 3354632 | tf_op jit(solution)/shard_map/ppermute | solution.py:302
  3.9 1.4 %copy-start = (f32[128,128]{1,0:T(8,128)S(1)}, f32[128,128]{1,0:T(8,128)}, u32[]{:S(2)}) copy-start(f32[128,128]{1,0:T(8,128)} %loading_ref.5) | copy-start | bytes 196612
  3.9 1.4 %copy-start.1 = (f32[128]{0:T(128)S(1)}, f32[128]{0:T(128)}, u32[]{:S(2)}) copy-start(f32[128]{0:T(128)} %param.4) | copy-start | bytes 1540
  63.0 11.4 %collective-permute-start.1 = (f32[4,272,128]{2,1,0:T(8,128)S(1)}, f32[4,272,128]{2,1,0:T(8,128)S(1)}, u32[]{:S(2)}, u32[]{:S(2)}) collective-permute-start(f32[4,272,128]{2,1,0:T(8,128)S(1)} %bitcast.6), channel_id=1, source_target_pairs={{0,2},{1,15},{2,0},{3,5},{4,6},{5,3},{6,4},{7,9},{8,10},{9,7},{10,... | collective-permute-start | bytes 1671176 | tf_op jit(solution)/shard_map/ppermute | solution.py:310
  76.0 3.2 %collective-permute-start.2 = (f32[136,128]{1,0:T(8,128)S(1)}, f32[136,128]{1,0:T(8,128)S(1)}, u32[]{:S(2)}, u32[]{:S(2)}) collective-permute-start(f32[136,128]{1,0:T(8,128)S(1)} %get-tuple-element.7), channel_id=1, source_target_pairs={{0,1},{1,0},{2,3},{3,2},{4,5},{5,4},{6,7},{7,6},{8,9},{9,8},{10,11... | collective-permute-start | bytes 208904 | tf_op jit(solution)/shard_map/ppermute | solution.py:318

commit v11 on v10

--- a/solution.py
+++ b/solution.py
@@ -277,7 +277,7 @@
     channels = counts.shape[1] * PARTS * 2
     height = counts.shape[0] // 2 // PARTS + 8 + comps // 2 // PARTS
     core = lax.axis_index("c").astype(jnp.int32)
-    side = (lax.axis_index("zl") ^ lax.axis_index("c")).astype(jnp.int32).reshape(1)
+    side = lax.axis_index("zl").astype(jnp.int32).reshape(1)
     offset = offset.reshape(1, comps)
 
     swap = [(0, 1), (1, 0)]
@@ -287,13 +287,13 @@
             partner = (((z - c) % PARTS ^ 1) + c) % PARTS
             near_pairs.append((2 * z + c, 2 * partner + c))
 
-    rings = [[2 * z for z in range(PARTS)], [2 * z + 1 for z in reversed(range(PARTS))]]
+    rings = [[2 * (step * k % PARTS) + c for k in range(PARTS)] for c, step in ((0, 3), (1, PARTS - 3))]
     rings4 = [ring[k::2] for ring in rings for k in range(2)]
     plane = lax.axis_size(WIDE)
     planes = [
-        [2 * (PARTS * p + z) + c for p in (reversed(range(plane)) if c else range(plane))]
+        [2 * (PARTS * (step * k % plane) + z) + c for k in range(plane)]
         for z in range(PARTS)
-        for c in range(2)
+        for c, step in ((0, 11), (1, plane - 11))
     ]
 
     half = counts.shape[0] // 2

time: 114 us -> 116 us (1.018)
  the two profiles are of different devices: /device:TPU:128 before, /device:TPU:2 now
where the time goes in v11:
time: 116 us
  blocking collectives  90.9 us (78%)
  Pallas kernels  9.42 us (8%)
  waiting for transfers between devices  8.65 us (7%)
  starting transfers between devices  6.21 us (5%)
    all_to_all x1, blocking collectives, on_device(): gathered = lax.all_to_all(partial, DEEP, 0, 0, axis_index_groups=rings)  40.6 us
    all_to_all x2, blocking collectives, on_device(): pieces = lax.all_to_all(pieces, AXES, 0, 0, axis_index_groups=planes)  33.6 us
    all_gather x1, blocking collectives, on_device(): scores = lax.all_gather(own, DEEP, axis=0, axis_index_groups=rings4)  16.8 us
    ppermute x1, waiting for transfers between devices, on_device(): near = lax.ppermute(scores, DEEP, near_pairs)  7.74 us
    pallas_call x9, Pallas kernels, call(): pl.pallas_call(body, out_shape=out_shape, in_specs=[pl.BlockSpec(memory_s...  6.7 us
    pallas_call x2, Pallas kernels, cut(): pl.pallas_call(body, out_shape=whole(height, width), in_specs=[pl.BlockSp...  2.73 us
    ppermute x1, starting transfers between devices, on_device(): near = lax.ppermute(scores, DEEP, near_pairs)  2.37 us
  transfers between devices with their start and end apart: 3, of which 3 were waited for; matrix products, arithmetic and copies ran while one was open for 0% of the time, Pallas kernels for 4%

profile of v11, /device:TPU:2, one launch (start us, length us, event | category | flops | bytes accessed | tf_op | source)
XLA Modules:
  0.0 116.0 jit_solution(9429446568186797619)
XLA Ops:
  0.6 1.3 %shard_map.52 = f32[2184,128]{1,0:T(8,128)S(1)} custom-call(s32[1]{0:T(128)} %bitcast.3.which, f32[4096,128]{1,0:T(8,128)} %counts_ref.3, f32[128,128]{1,0:T(8,128)} %loading_ref.5, f32[1,128]{1,0:T(1,128)} %bitcast.9), custom_call_target="tpu_custom_call" | custom-call | tf_op jit(solution)/shard_map/pallas_call | solution.py:75
  2.0 1.9 %collective-permute-start = (f32[2184,128]{1,0:T(8,128)S(1)}, f32[2184,128]{1,0:T(8,128)S(1)}, u32[]{:S(2)}, u32[]{:S(2)}) collective-permute-start(f32[2184,128]{1,0:T(8,128)S(1)} %shard_map.52), channel_id=1, source_target_pairs={{0,1},{1,0},{2,3},{3,2},{4,5},{5,4},{6,7},{7,6},{8,9},{9,8},{10,11... | collective-permute-start | bytes 3354632 | tf_op jit(solution)/shard_map/ppermute | solution.py:302
  3.9 0.0 copy-start
  3.9 0.0 copy-start.1
  3.9 1.4 %shard_map.50.mine = f32[2048,128]{1,0:T(8,128)S(1)} custom-call(s32[1]{0:T(128)} %bitcast.1.which, f32[4096,128]{1,0:T(8,128)} %counts_ref.3), custom_call_target="tpu_custom_call" | custom-call | tf_op jit(solution)/shard_map/pallas_call | solution.py:75
  5.3 0.0 copy-done
  5.3 0.0 copy-done.1
  5.3 1.1 shard_map.51.in_ref
  6.5 0.1 collective-permute-done.other
  6.6 1.1 shard_map.53
  7.8 40.6 %all_to_all.15.in_ref = f32[8,272,128]{2,1,0:T(8,128)S(1)} all-to-all(f32[8,272,128]{2,1,0:T(8,128)S(1)} %shard_map.53), channel_id=1, replica_groups={{0,6,12,2,8,14,4,10},{1,11,5,15,9,3,13,7},{16,22,28,18,24,30,20,26},{17..., dimensions={0} | all-to-all | bytes 2228224 | tf_op jit(solution)/shard_map/all_to_all | solution.py:307
  48.4 0.3 shard_map.54
  48.7 16.8 %all-gather = f32[1088,128]{1,0:T(8,128)S(1)} all-gather(f32[272,128]{1,0:T(8,128)S(1)} %shard_map.54), channel_id=2, replica_groups={{0,12,8,4},{6,2,14,10},{1,5,9,13},{11,15,3,7},{16,28,24,20},{22,18,30,2..., dimensions={0}, use_global_device_ids=true | all-gather | bytes 696320 | tf_op jit(solution)/shard_map/all_gather | solution.py:309
  65.5 2.4 %collective-permute-start.1 = (f32[4,272,128]{2,1,0:T(8,128)S(1)}, f32[4,272,128]{2,1,0:T(8,128)S(1)}, u32[]{:S(2)}, u32[]{:S(2)}) collective-permute-start(f32[4,272,128]{2,1,0:T(8,128)S(1)} %bitcast.6), channel_id=1, source_target_pairs={{0,2},{1,15},{2,0},{3,5},{4,6},{5,3},{6,4},{7,9},{8,10},{9,7},{10,... | collective-permute-start | bytes 1671176 | tf_op jit(solution)/shard_map/ppermute | solution.py:310
  67.9 1.3 %shard_map.55.some_ref = f32[136,384]{1,0:T(8,128)S(1)} custom-call(s32[1]{0:T(128)} %bitcast.side, f32[4,272,128]{2,1,0:T(8,128)S(1)} %bitcast.7, f32[2048,128]{1,0:T(8,128)S(1)} %shard_map.50.mine, f32[2184,128]{1,0:T(8,128)S(1)} %collective-permute-done.other, f32[1,128]{1,0:T(1,128)S(1)} %bitcast.11), custom_call_target="tpu_custom_call" | custom-call | tf_op jit(solution)/shard_map/pallas_call | solution.py:32
  69.2 7.7 %collective-permute-done.1.near_ref = f32[4,272,128]{2,1,0:T(8,128)S(1)} collective-permute-done((f32[4,272,128]{2,1,0:T(8,128)S(1)}, f32[4,272,128]{2,1,0:T(8,128)S(1)}, u32[]{:S(2)}, u32[]{:S(2)}) %collective-permute-start.1) | collective-permute-done | bytes 557088 | tf_op jit(solution)/shard_map/ppermute | solution.py:310
  76.9 1.6 %shard_map.56 = (f32[136,128]{1,0:T(8,128)S(1)}, f32[5,128,128]{2,1,0:T(8,128)S(1)}) custom-call(s32[1]{0:T(128)} %bitcast.side, f32[4,272,128]{2,1,0:T(8,128)S(1)} %collective-permute-done.1.near_ref, f32[4,272,128]{2,1,0:T(8,128)S(1)} %bitcast.8, f32[136,384]{1,0:T(8,128)S(1)} %shard_map.55.some_ref, f32[2048,128]{1,0:T(8,128)S(1)} %shard_map.50.mine, ...), custom_call_target="tpu_custom_call" | custom-call | tf_op jit(solution)/shard_map/pallas_call | solution.py:32
  78.5 1.9 %collective-permute-start.2 = (f32[136,128]{1,0:T(8,128)S(1)}, f32[136,128]{1,0:T(8,128)S(1)}, u32[]{:S(2)}, u32[]{:S(2)}) collective-permute-start(f32[136,128]{1,0:T(8,128)S(1)} %get-tuple-element.7), channel_id=1, source_target_pairs={{0,1},{1,0},{2,3},{3,2},{4,5},{5,4},{6,7},{7,6},{8,9},{9,8},{10,11... | collective-permute-start | bytes 208904 | tf_op jit(solution)/shard_map/ppermute | solution.py:318
  80.5 0.5 shard_map.57.a_ref
  80.9 0.8 collective-permute-done.2.b_ref
  81.7 19.5 %all_to_all.16.in_ref = f32[32,8,128]{2,1,0:T(8,128)S(1)} all-to-all(f32[32,8,128]{2,1,0:T(8,128)S(1)} %shard_map.58), channel_id=1, replica_groups={{0,176,352,16,192,368,32,208,384,48,224,400,64,240,416,80,256,432,96,27..., dimensions={0} | all-to-all | bytes 262144 | tf_op jit(solution)/shard_map/all_to_all | solution.py:321
  101.3 14.1 %all_to_all.17.in_ref = f32[32,8,128]{2,1,0:T(8,128)S(1)} all-to-all(f32[32,8,128]{2,1,0:T(8,128)S(1)} %shard_map.59), channel_id=1, replica_groups={{0,176,352,16,192,368,32,208,384,48,224,400,64,240,416,80,256,432,96,27..., dimensions={0} | all-to-all | bytes 262144 | tf_op jit(solution)/shard_map/all_to_all | solution.py:323
  115.3 0.6 shard_map.60
  (2 shorter events, 0.1 us)
Async XLA Ops:
  2.0 4.7 %collective-permute-start = (f32[2184,128]{1,0:T(8,128)S(1)}, f32[2184,128]{1,0:T(8,128)S(1)}, u32[]{:S(2)}, u32[]{:S(2)}) collective-permute-start(f32[2184,128]{1,0:T(8,128)S(1)} %shard_map.52), channel_id=1, source_target_pairs={{0,1},{1,0},{2,3},{3,2},{4,5},{5,4},{6,7},{7,6},{8,9},{9,8},{10,11... | collective-permute-start | bytes 3354632 | tf_op jit(solution)/shard_map/ppermute | solution.py:302
  3.9 1.4 %copy-start = (f32[128,128]{1,0:T(8,128)S(1)}, f32[128,128]{1,0:T(8,128)}, u32[]{:S(2)}) copy-start(f32[128,128]{1,0:T(8,128)} %loading_ref.5) | copy-start | bytes 196612
  3.9 1.4 %copy-start.1 = (f32[128]{0:T(128)S(1)}, f32[128]{0:T(128)}, u32[]{:S(2)}) copy-start(f32[128]{0:T(128)} %param.4) | copy-start | bytes 1540
  65.5 11.4 %collective-permute-start.1 = (f32[4,272,128]{2,1,0:T(8,128)S(1)}, f32[4,272,128]{2,1,0:T(8,128)S(1)}, u32[]{:S(2)}, u32[]{:S(2)}) collective-permute-start(f32[4,272,128]{2,1,0:T(8,128)S(1)} %bitcast.6), channel_id=1, source_target_pairs={{0,2},{1,15},{2,0},{3,5},{4,6},{5,3},{6,4},{7,9},{8,10},{9,7},{10,... | collective-permute-start | bytes 1671176 | tf_op jit(solution)/shard_map/ppermute | solution.py:310
  78.5 3.2 %collective-permute-start.2 = (f32[136,128]{1,0:T(8,128)S(1)}, f32[136,128]{1,0:T(8,128)S(1)}, u32[]{:S(2)}, u32[]{:S(2)}) collective-permute-start(f32[136,128]{1,0:T(8,128)S(1)} %get-tuple-element.7), channel_id=1, source_target_pairs={{0,1},{1,0},{2,3},{3,2},{4,5},{5,4},{6,7},{7,6},{8,9},{9,8},{10,11... | collective-permute-start | bytes 208904 | tf_op jit(solution)/shard_map/ppermute | solution.py:318

commit v12 on v10

--- a/solution.py
+++ b/solution.py
@@ -182,7 +182,7 @@
     out_ref[rows + 8 : rows + 8 + share, :] = sum(in_ref[j, rows + 8 : rows + 8 + share, :] for j in range(PARTS))
 
 
-def block_terms(first, in_ref, logs, offs):
+def block_terms(first, base, in_ref, logs, offs):
     blocks, height, comps = in_ref.shape
     rows = height - 8 - comps // 2 // PARTS
     wide, sums = 0.0, 0.0
@@ -195,31 +195,37 @@
             ],
             axis=0,
         )
-        here = pl.ds(pl.multiple_of((2 * j + first) * rows, rows), rows)
+        here = pl.ds(pl.multiple_of((2 * (base + j) + first) * rows, rows), rows)
         both = jnp.concatenate([a[here, :] - geo - off for a, off in zip(logs, offs)] + [s], axis=1)
         sums += jnp.sum(both, axis=0, keepdims=True)
         wide += mult(s.T, both)
     return wide, sums
 
 
-def some_grad_body(side, in_ref, mine, other, offset_ref, out_ref):
+def some_grad_body(other_side, side, in_ref, mine, other, offset_ref, *refs):
     total, comps = mine.shape
+    out_ref = refs[-1]
     offs = (offset_ref[...], other[total + comps : total + comps + 1, :])
-    wide, sums = block_terms(side[0], in_ref, (mine, other), offs)
+    first = 1 - side[0] if other_side else side[0]
+    wide, sums = block_terms(first, 0, in_ref, (mine, other), offs)
+    for before in refs[:-1]:
+        wide, sums = wide + before[0:comps, :], sums + before[comps : comps + 1, :]
     out_ref[0:comps, :] = wide
     out_ref[comps : comps + 8, :] = jnp.broadcast_to(sums, (8, sums.shape[1]))
 
 
-def grad_body(side, near_ref, in_ref, some_ref, mine, other, offset_ref, out_ref, rest_ref):
+def grad_body(side, late_ref, early_ref, in_ref, some_ref, mine, other, offset_ref, out_ref, rest_ref):
     total, comps = mine.shape
     height = in_ref.shape[1]
     share = comps // 2 // PARTS
     rows = height - 8 - share
     offs = (offset_ref[...], other[total + comps : total + comps + 1, :])
-    wide, sums = block_terms(1 - side[0], near_ref, (mine, other), offs)
+    wide, sums = block_terms(1 - side[0], early_ref.shape[0], late_ref, (mine, other), offs)
     wide, sums = wide + some_ref[0:comps, :], sums + some_ref[comps : comps + 1, :]
-    here = [a[j, rows + 8 : rows + 8 + share, :] for j in range(PARTS // 2) for a in (in_ref, near_ref)]
-    there = [a[j, rows + 8 : rows + 8 + share, :] for j in range(PARTS // 2) for a in (near_ref, in_ref)]
+    ours = [in_ref[j, rows + 8 : rows + 8 + share, :] for j in range(PARTS // 2)]
+    theirs = [a[j, rows + 8 : rows + 8 + share, :] for a in (early_ref, late_ref) for j in range(PARTS // 4)]
+    here = [a for pair in zip(ours, theirs) for a in pair]
+    there = [a for pair in zip(theirs, ours) for a in pair]
     gram = jnp.where(side[0] == 0, jnp.concatenate(here, axis=0), jnp.concatenate(there, axis=0))
     gram = unfold(gram, in_ref[0, rows + 2 : rows + 3, :])
     row = lax.broadcasted_iota(jnp.int32, (comps, comps), 0)
@@ -307,13 +313,15 @@
     gathered = lax.all_to_all(partial, DEEP, 0, 0, axis_index_groups=rings)
     own = call(functools.partial(finish_body, channels), whole(height, comps), gathered)
     scores = lax.all_gather(own, DEEP, axis=0, axis_index_groups=rings4)
-    near = lax.ppermute(scores, DEEP, near_pairs)
-    some = call(
-        some_grad_body, whole(comps + 8, 3 * comps), side, scores, mine, other, offset, scalars=1
-    )
+    early = lax.ppermute(scores[: PARTS // 4], DEEP, near_pairs)
+    late = lax.ppermute(scores[PARTS // 4 :], DEEP, near_pairs)
+    total = whole(comps + 8, 3 * comps)
+    logs = (mine, other, offset)
+    some = call(functools.partial(some_grad_body, False), total, side, scores, *logs, scalars=1)
+    some = call(functools.partial(some_grad_body, True), total, side, early, *logs, some, scalars=1)
     shape = whole(comps + 8, comps)
     grad_other, rest = call(
-        grad_body, (shape, whole(5, comps, comps)), side, near, scores, some, mine, other, offset, scalars=1
+        grad_body, (shape, whole(5, comps, comps)), side, late, early, scores, some, *logs, scalars=1
     )
     arrived = lax.ppermute(grad_other, "c", swap)
     grad_mine = call(mine_grad_body, shape, rest, loading)

time: 114 us -> 115 us (level)
  waiting for transfers between devices: 9.11 us -> 4.66 us
  starting transfers between devices: 5.75 us -> 9.67 us
    ppermute x1 -> x2, waiting for transfers between devices: 8.2 us -> 3.75 us  [the longest x1 2.26 us: on_device(): late = lax.ppermute(scores[PARTS // 4:], DEEP, near_pairs)]
    ppermute x1 -> x2, starting transfers between devices: 1.91 us -> 5.83 us  [the longest x1 3.92 us: on_device(): late = lax.ppermute(scores[PARTS // 4:], DEEP, near_pairs)]
    pallas_call x9 -> x10, Pallas kernels: 6.7 us -> 6.85 us  [call(): pl.pallas_call(body, out_shape=out_shape, in_specs=[pl.BlockSpec(memory_s...]
  transfers between devices with their start and end apart: 3 -> 4, of which waited for: 3 -> 4; matrix products, arithmetic and copies ran while one was open for 0% -> 0% of each run, Pallas kernels for 4% -> 4%
where the time goes in v12:
time: 115 us
  blocking collectives  89.1 us (77%)
  starting transfers between devices  9.67 us (8%)
  Pallas kernels  9.57 us (8%)
  waiting for transfers between devices  4.66 us (4%)
    all_to_all x1, blocking collectives, on_device(): gathered = lax.all_to_all(partial, DEEP, 0, 0, axis_index_groups=rings)  36.1 us
    all_to_all x2, blocking collectives, on_device(): pieces = lax.all_to_all(pieces, AXES, 0, 0, axis_index_groups=planes)  34.2 us
    all_gather x1, blocking collectives, on_device(): scores = lax.all_gather(own, DEEP, axis=0, axis_index_groups=rings4)  18.8 us
    pallas_call x10, Pallas kernels, call(): pl.pallas_call(body, out_shape=out_shape, in_specs=[pl.BlockSpec(memory_s...  6.85 us
    ppermute x1, starting transfers between devices, on_device(): late = lax.ppermute(scores[PARTS // 4:], DEEP, near_pairs)  3.92 us
    pallas_call x2, Pallas kernels, cut(): pl.pallas_call(body, out_shape=whole(height, width), in_specs=[pl.BlockSp...  2.72 us
  transfers between devices with their start and end apart: 4, of which 4 were waited for; matrix products, arithmetic and copies ran while one was open for 0% of the time, Pallas kernels for 4%

profile of v12, /device:TPU:128, one launch (start us, length us, event | category | flops | bytes accessed | tf_op | source)
XLA Modules:
  0.0 114.6 jit_solution(6013439679980080193)
XLA Ops:
  0.6 1.3 %shard_map.52 = f32[2184,128]{1,0:T(8,128)S(1)} custom-call(s32[1]{0:T(128)} %bitcast.3.which, f32[4096,128]{1,0:T(8,128)} %counts_ref.3, f32[128,128]{1,0:T(8,128)} %loading_ref.5, f32[1,128]{1,0:T(1,128)} %bitcast.10), custom_call_target="tpu_custom_call" | custom-call | tf_op jit(solution)/shard_map/pallas_call | solution.py:75
  2.0 1.9 %collective-permute-start = (f32[2184,128]{1,0:T(8,128)S(1)}, f32[2184,128]{1,0:T(8,128)S(1)}, u32[]{:S(2)}, u32[]{:S(2)}) collective-permute-start(f32[2184,128]{1,0:T(8,128)S(1)} %shard_map.52), channel_id=1, source_target_pairs={{0,1},{1,0},{2,3},{3,2},{4,5},{5,4},{6,7},{7,6},{8,9},{9,8},{10,11... | collective-permute-start | bytes 3354632 | tf_op jit(solution)/shard_map/ppermute | solution.py:308
  3.9 0.0 copy-start
  3.9 1.4 %shard_map.50.mine = f32[2048,128]{1,0:T(8,128)S(1)} custom-call(s32[1]{0:T(128)} %bitcast.1.which, f32[4096,128]{1,0:T(8,128)} %counts_ref.3), custom_call_target="tpu_custom_call" | custom-call | tf_op jit(solution)/shard_map/pallas_call | solution.py:75
  5.3 1.1 shard_map.51.in_ref
  6.5 0.1 collective-permute-done.other
  6.6 1.1 shard_map.53
  7.8 36.1 %all_to_all.15.in_ref = f32[8,272,128]{2,1,0:T(8,128)S(1)} all-to-all(f32[8,272,128]{2,1,0:T(8,128)S(1)} %shard_map.53), channel_id=1, replica_groups={{0,2,4,6,8,10,12,14},{15,13,11,9,7,5,3,1},{16,18,20,22,24,26,28,30},{31..., dimensions={0} | all-to-all | bytes 2228224 | tf_op jit(solution)/shard_map/all_to_all | solution.py:313
  43.8 0.3 shard_map.54
  44.2 18.8 %all-gather = f32[1088,128]{1,0:T(8,128)S(1)} all-gather(f32[272,128]{1,0:T(8,128)S(1)} %shard_map.54), channel_id=2, replica_groups={{0,4,8,12},{2,6,10,14},{15,11,7,3},{13,9,5,1},{16,20,24,28},{18,22,26,3..., dimensions={0}, use_global_device_ids=true | all-gather | bytes 696320 | tf_op jit(solution)/shard_map/all_gather | solution.py:315
  63.0 0.8 fusion
  63.8 1.9 %collective-permute-start.2 = (f32[2,272,128]{2,1,0:T(8,128)}, f32[2,272,128]{2,1,0:T(8,128)S(1)}, u32[]{:S(2)}, u32[]{:S(2)}) collective-permute-start(f32[2,272,128]{2,1,0:T(8,128)} %bitcast.5), channel_id=1, source_target_pairs={{0,2},{1,15},{2,0},{3,5},{4,6},{5,3},{6,4},{7,9},{8,10},{9,7},{10,... | collective-permute-start | bytes 835592 | tf_op jit(solution)/shard_map/ppermute | solution.py:316
  65.7 3.9 %collective-permute-start.1 = (f32[2,272,128]{2,1,0:T(8,128)}, f32[2,272,128]{2,1,0:T(8,128)S(1)}, u32[]{:S(2)}, u32[]{:S(2)}) collective-permute-start(f32[2,272,128]{2,1,0:T(8,128)} %bitcast.4), channel_id=1, source_target_pairs={{0,2},{1,15},{2,0},{3,5},{4,6},{5,3},{6,4},{7,9},{8,10},{9,7},{10,... | collective-permute-start | bytes 835592 | tf_op jit(solution)/shard_map/ppermute | solution.py:317
  69.7 1.3 %shard_map.55.refs_0_ = f32[136,384]{1,0:T(8,128)S(1)} custom-call(s32[1]{0:T(128)} %bitcast.side, f32[4,272,128]{2,1,0:T(8,128)S(1)} %bitcast.8, f32[2048,128]{1,0:T(8,128)S(1)} %shard_map.50.mine, f32[2184,128]{1,0:T(8,128)S(1)} %collective-permute-done.other, f32[1,128]{1,0:T(1,128)S(1)} %bitcast.12), custom_call_target="tpu_custom_call" | custom-call | tf_op jit(solution)/shard_map/pallas_call | solution.py:32
  71.0 1.5 %collective-permute-done.2.in_ref.early_ref = f32[2,272,128]{2,1,0:T(8,128)S(1)} collective-permute-done((f32[2,272,128]{2,1,0:T(8,128)}, f32[2,272,128]{2,1,0:T(8,128)S(1)}, u32[]{:S(2)}, u32[]{:S(2)}) %collective-permute-start.2) | collective-permute-done | bytes 278560 | tf_op jit(solution)/shard_map/ppermute | solution.py:316
  72.4 0.7 shard_map.56.some_ref
  73.2 2.3 %collective-permute-done.1.late_ref = f32[2,272,128]{2,1,0:T(8,128)S(1)} collective-permute-done((f32[2,272,128]{2,1,0:T(8,128)}, f32[2,272,128]{2,1,0:T(8,128)S(1)}, u32[]{:S(2)}, u32[]{:S(2)}) %collective-permute-start.1) | collective-permute-done | bytes 278560 | tf_op jit(solution)/shard_map/ppermute | solution.py:317
  75.4 1.1 shard_map.57
  76.5 1.9 %collective-permute-start.3 = (f32[136,128]{1,0:T(8,128)S(1)}, f32[136,128]{1,0:T(8,128)S(1)}, u32[]{:S(2)}, u32[]{:S(2)}) collective-permute-start(f32[136,128]{1,0:T(8,128)S(1)} %get-tuple-element.7), channel_id=1, source_target_pairs={{0,1},{1,0},{2,3},{3,2},{4,5},{5,4},{6,7},{7,6},{8,9},{9,8},{10,11... | collective-permute-start | bytes 208904 | tf_op jit(solution)/shard_map/ppermute | solution.py:326
  78.4 0.5 shard_map.58.a_ref
  78.9 0.8 collective-permute-done.3.b_ref
  79.7 20.2 %all_to_all.16.in_ref = f32[32,8,128]{2,1,0:T(8,128)S(1)} all-to-all(f32[32,8,128]{2,1,0:T(8,128)S(1)} %shard_map.59), channel_id=1, replica_groups={{0,16,32,48,64,80,96,112,128,144,160,176,192,208,224,240,256,272,288,30..., dimensions={0} | all-to-all | bytes 262144 | tf_op jit(solution)/shard_map/all_to_all | solution.py:329
  100.0 14.0 %all_to_all.17.in_ref = f32[32,8,128]{2,1,0:T(8,128)S(1)} all-to-all(f32[32,8,128]{2,1,0:T(8,128)S(1)} %shard_map.60), channel_id=1, replica_groups={{0,16,32,48,64,80,96,112,128,144,160,176,192,208,224,240,256,272,288,30..., dimensions={0} | all-to-all | bytes 262144 | tf_op jit(solution)/shard_map/all_to_all | solution.py:331
  113.9 0.6 shard_map.61
  (5 shorter events, 0.1 us)
Async XLA Ops:
  2.0 4.7 %collective-permute-start = (f32[2184,128]{1,0:T(8,128)S(1)}, f32[2184,128]{1,0:T(8,128)S(1)}, u32[]{:S(2)}, u32[]{:S(2)}) collective-permute-start(f32[2184,128]{1,0:T(8,128)S(1)} %shard_map.52), channel_id=1, source_target_pairs={{0,1},{1,0},{2,3},{3,2},{4,5},{5,4},{6,7},{7,6},{8,9},{9,8},{10,11... | collective-permute-start | bytes 3354632 | tf_op jit(solution)/shard_map/ppermute | solution.py:308
  3.9 1.4 %copy-start = (f32[128,128]{1,0:T(8,128)S(1)}, f32[128,128]{1,0:T(8,128)}, u32[]{:S(2)}) copy-start(f32[128,128]{1,0:T(8,128)} %loading_ref.5) | copy-start | bytes 196612
  3.9 1.4 %copy-start.1 = (f32[128]{0:T(128)S(1)}, f32[128]{0:T(128)}, u32[]{:S(2)}) copy-start(f32[128]{0:T(128)} %param.4) | copy-start | bytes 1540
  63.8 8.6 %collective-permute-start.2 = (f32[2,272,128]{2,1,0:T(8,128)}, f32[2,272,128]{2,1,0:T(8,128)S(1)}, u32[]{:S(2)}, u32[]{:S(2)}) collective-permute-start(f32[2,272,128]{2,1,0:T(8,128)} %bitcast.5), channel_id=1, source_target_pairs={{0,2},{1,15},{2,0},{3,5},{4,6},{5,3},{6,4},{7,9},{8,10},{9,7},{10,... | collective-permute-start | bytes 835592 | tf_op jit(solution)/shard_map/ppermute | solution.py:316
  65.7 9.7 %collective-permute-start.1 = (f32[2,272,128]{2,1,0:T(8,128)}, f32[2,272,128]{2,1,0:T(8,128)S(1)}, u32[]{:S(2)}, u32[]{:S(2)}) collective-permute-start(f32[2,272,128]{2,1,0:T(8,128)} %bitcast.4), channel_id=1, source_target_pairs={{0,2},{1,15},{2,0},{3,5},{4,6},{5,3},{6,4},{7,9},{8,10},{9,7},{10,... | collective-permute-start | bytes 835592 | tf_op jit(solution)/shard_map/ppermute | solution.py:317
  76.5 3.2 %collective-permute-start.3 = (f32[136,128]{1,0:T(8,128)S(1)}, f32[136,128]{1,0:T(8,128)S(1)}, u32[]{:S(2)}, u32[]{:S(2)}) collective-permute-start(f32[136,128]{1,0:T(8,128)S(1)} %get-tuple-element.7), channel_id=1, source_target_pairs={{0,1},{1,0},{2,3},{3,2},{4,5},{5,4},{6,7},{7,6},{8,9},{9,8},{10,11... | collective-permute-start | bytes 208904 | tf_op jit(solution)/shard_map/ppermute | solution.py:326

commit v13 on v10

--- a/solution.py
+++ b/solution.py
@@ -182,7 +182,7 @@
     out_ref[rows + 8 : rows + 8 + share, :] = sum(in_ref[j, rows + 8 : rows + 8 + share, :] for j in range(PARTS))
 
 
-def block_terms(first, in_ref, logs, offs):
+def block_terms(first, flip, in_ref, logs, offs):
     blocks, height, comps = in_ref.shape
     rows = height - 8 - comps // 2 // PARTS
     wide, sums = 0.0, 0.0
@@ -195,7 +195,7 @@
             ],
             axis=0,
         )
-        here = pl.ds(pl.multiple_of((2 * j + first) * rows, rows), rows)
+        here = pl.ds(pl.multiple_of((2 * (j ^ flip) + first) * rows, rows), rows)
         both = jnp.concatenate([a[here, :] - geo - off for a, off in zip(logs, offs)] + [s], axis=1)
         sums += jnp.sum(both, axis=0, keepdims=True)
         wide += mult(s.T, both)
@@ -205,7 +205,7 @@
 def some_grad_body(side, in_ref, mine, other, offset_ref, out_ref):
     total, comps = mine.shape
     offs = (offset_ref[...], other[total + comps : total + comps + 1, :])
-    wide, sums = block_terms(side[0], in_ref, (mine, other), offs)
+    wide, sums = block_terms(side[0], side[1], in_ref, (mine, other), offs)
     out_ref[0:comps, :] = wide
     out_ref[comps : comps + 8, :] = jnp.broadcast_to(sums, (8, sums.shape[1]))
 
@@ -216,11 +216,16 @@
     share = comps // 2 // PARTS
     rows = height - 8 - share
     offs = (offset_ref[...], other[total + comps : total + comps + 1, :])
-    wide, sums = block_terms(1 - side[0], near_ref, (mine, other), offs)
+    wide, sums = block_terms(1 - side[0], side[1], near_ref, (mine, other), offs)
     wide, sums = wide + some_ref[0:comps, :], sums + some_ref[comps : comps + 1, :]
-    here = [a[j, rows + 8 : rows + 8 + share, :] for j in range(PARTS // 2) for a in (in_ref, near_ref)]
-    there = [a[j, rows + 8 : rows + 8 + share, :] for j in range(PARTS // 2) for a in (near_ref, in_ref)]
-    gram = jnp.where(side[0] == 0, jnp.concatenate(here, axis=0), jnp.concatenate(there, axis=0))
+    def whole_gram(order):
+        shares = [[a[j, rows + 8 : rows + 8 + share, :] for a in (in_ref, near_ref)] for j in order]
+        here = jnp.concatenate([a for pair in shares for a in pair], axis=0)
+        there = jnp.concatenate([a for pair in shares for a in pair[::-1]], axis=0)
+        return jnp.where(side[0] == 0, here, there)
+
+    order = list(range(PARTS // 2))
+    gram = jnp.where(side[1] == 0, whole_gram(order), whole_gram(order[::-1]))
     gram = unfold(gram, in_ref[0, rows + 2 : rows + 3, :])
     row = lax.broadcasted_iota(jnp.int32, (comps, comps), 0)
     col = lax.broadcasted_iota(jnp.int32, (comps, comps), 1)
@@ -277,7 +282,7 @@
     channels = counts.shape[1] * PARTS * 2
     height = counts.shape[0] // 2 // PARTS + 8 + comps // 2 // PARTS
     core = lax.axis_index("c").astype(jnp.int32)
-    side = (lax.axis_index("zl") ^ lax.axis_index("c")).astype(jnp.int32).reshape(1)
+    side = jnp.stack([lax.axis_index("zl").astype(jnp.int32), (PARTS // 2 - 1) * core])
     offset = offset.reshape(1, comps)
 
     swap = [(0, 1), (1, 0)]
@@ -287,8 +292,7 @@
             partner = (((z - c) % PARTS ^ 1) + c) % PARTS
             near_pairs.append((2 * z + c, 2 * partner + c))
 
-    rings = [[2 * z for z in range(PARTS)], [2 * z + 1 for z in reversed(range(PARTS))]]
-    rings4 = [ring[k::2] for ring in rings for k in range(2)]
+    quads = [[2 * z + c for z in range(k, PARTS, 2)][:: 1 - 2 * c] for c in range(2) for k in range(2)]
     plane = lax.axis_size(WIDE)
     planes = [
         [2 * (PARTS * p + z) + c for p in (reversed(range(plane)) if c else range(plane))]
@@ -304,9 +308,9 @@
     block = whole(PARTS, height, comps)
     partial = call(encode_body, block, mine, loading, offset)
     partial = call(encode_last_body, block, partial, other)
-    gathered = lax.all_to_all(partial, DEEP, 0, 0, axis_index_groups=rings)
+    gathered = lax.all_to_all(partial, ("zh", "zl"), 0, 0)
     own = call(functools.partial(finish_body, channels), whole(height, comps), gathered)
-    scores = lax.all_gather(own, DEEP, axis=0, axis_index_groups=rings4)
+    scores = lax.all_gather(own, DEEP, axis=0, axis_index_groups=quads)
     near = lax.ppermute(scores, DEEP, near_pairs)
     some = call(
         some_grad_body, whole(comps + 8, 3 * comps), side, scores, mine, other, offset, scalars=1

time: 114 us -> 118 us (1.035)
  the two profiles are of different devices: /device:TPU:128 before, /device:TPU:8 now
where the time goes in v13:
time: 118 us
  blocking collectives  92 us (78%)
  Pallas kernels  10.5 us (9%)
  waiting for transfers between devices  8.02 us (7%)
  starting transfers between devices  6.22 us (5%)
    all_to_all x1, blocking collectives, on_device(): gathered = lax.all_to_all(partial, ('zh', 'zl'), 0, 0)  40.8 us
    all_to_all x2, blocking collectives, on_device(): pieces = lax.all_to_all(pieces, AXES, 0, 0, axis_index_groups=planes)  33.5 us
    all_gather x1, blocking collectives, on_device(): scores = lax.all_gather(own, DEEP, axis=0, axis_index_groups=quads)  17.7 us
    pallas_call x9, Pallas kernels, call(): pl.pallas_call(body, out_shape=out_shape, in_specs=[pl.BlockSpec(memory_s...  7.78 us
    ppermute x1, waiting for transfers between devices, on_device(): near = lax.ppermute(scores, DEEP, near_pairs)  7.11 us
    pallas_call x2, Pallas kernels, cut(): pl.pallas_call(body, out_shape=whole(height, width), in_specs=[pl.BlockSp...  2.72 us
    ppermute x1, starting transfers between devices, on_device(): near = lax.ppermute(scores, DEEP, near_pairs)  2.38 us
  transfers between devices with their start and end apart: 3, of which 3 were waited for; matrix products, arithmetic and copies ran while one was open for 0% of the time, Pallas kernels for 4%

profile of v13, /device:TPU:8, one launch (start us, length us, event | category | flops | bytes accessed | tf_op | source)
XLA Modules:
  0.0 117.6 jit_solution(9423227679953929467)
XLA Ops:
  0.6 1.3 %shard_map.52 = f32[2184,128]{1,0:T(8,128)S(1)} custom-call(s32[1]{0:T(128)} %bitcast.4.which, f32[4096,128]{1,0:T(8,128)} %counts_ref.3, f32[128,128]{1,0:T(8,128)} %loading_ref.5, f32[1,128]{1,0:T(1,128)} %bitcast.10), custom_call_target="tpu_custom_call" | custom-call | tf_op jit(solution)/shard_map/pallas_call | solution.py:75
  2.0 1.9 %collective-permute-start = (f32[2184,128]{1,0:T(8,128)S(1)}, f32[2184,128]{1,0:T(8,128)S(1)}, u32[]{:S(2)}, u32[]{:S(2)}) collective-permute-start(f32[2184,128]{1,0:T(8,128)S(1)} %shard_map.52), channel_id=1, source_target_pairs={{0,1},{1,0},{2,3},{3,2},{4,5},{5,4},{6,7},{7,6},{8,9},{9,8},{10,11... | collective-permute-start | bytes 3354632 | tf_op jit(solution)/shard_map/ppermute | solution.py:306
  3.9 0.0 copy-start
  3.9 0.0 copy-start.1
  3.9 1.4 %shard_map.50.mine = f32[2048,128]{1,0:T(8,128)S(1)} custom-call(s32[1]{0:T(128)} %bitcast.2.which, f32[4096,128]{1,0:T(8,128)} %counts_ref.3), custom_call_target="tpu_custom_call" | custom-call | tf_op jit(solution)/shard_map/pallas_call | solution.py:75
  5.3 0.0 copy-done
  5.3 0.0 copy-done.1
  5.3 1.1 shard_map.51.in_ref
  6.5 0.1 collective-permute-done.other
  6.6 1.1 shard_map.53
  7.8 40.8 %all_to_all.15.in_ref = f32[8,272,128]{2,1,0:T(8,128)S(1)} all-to-all(f32[8,272,128]{2,1,0:T(8,128)S(1)} %shard_map.53), channel_id=1, replica_groups=mesh['y'=8,'x'=4,'zh'=4,'zl'=2,'c'=2] {'zh','zl'}, dimensions={0} | all-to-all | bytes 2228224 | tf_op jit(solution)/shard_map/all_to_all | solution.py:311
  48.5 0.3 shard_map.54
  48.9 17.7 %all-gather = f32[1088,128]{1,0:T(8,128)S(1)} all-gather(f32[272,128]{1,0:T(8,128)S(1)} %shard_map.54), channel_id=2, replica_groups={{0,4,8,12},{2,6,10,14},{13,9,5,1},{15,11,7,3},{16,20,24,28},{18,22,26,3..., dimensions={0}, use_global_device_ids=true | all-gather | bytes 696320 | tf_op jit(solution)/shard_map/all_gather | solution.py:313
  66.6 2.4 %collective-permute-start.1 = (f32[4,272,128]{2,1,0:T(8,128)S(1)}, f32[4,272,128]{2,1,0:T(8,128)S(1)}, u32[]{:S(2)}, u32[]{:S(2)}) collective-permute-start(f32[4,272,128]{2,1,0:T(8,128)S(1)} %bitcast.7), channel_id=1, source_target_pairs={{0,2},{1,15},{2,0},{3,5},{4,6},{5,3},{6,4},{7,9},{8,10},{9,7},{10,... | collective-permute-start | bytes 1671176 | tf_op jit(solution)/shard_map/ppermute | solution.py:314
  69.0 0.1 pad_add_fusion.side
  69.1 1.8 %shard_map.55.some_ref = f32[136,384]{1,0:T(8,128)S(1)} custom-call(s32[2]{0:T(128)S(1)} %pad_add_fusion.side, f32[4,272,128]{2,1,0:T(8,128)S(1)} %bitcast.8, f32[2048,128]{1,0:T(8,128)S(1)} %shard_map.50.mine, f32[2184,128]{1,0:T(8,128)S(1)} %collective-permute-done.other, f32[1,128]{1,0:T(1,128)S(1)} %bitcast.12), custom_call_target="tpu_custom_call" | custom-call | tf_op jit(solution)/shard_map/pallas_call | solution.py:32
  70.9 7.1 %collective-permute-done.1.near_ref = f32[4,272,128]{2,1,0:T(8,128)S(1)} collective-permute-done((f32[4,272,128]{2,1,0:T(8,128)S(1)}, f32[4,272,128]{2,1,0:T(8,128)S(1)}, u32[]{:S(2)}, u32[]{:S(2)}) %collective-permute-start.1) | collective-permute-done | bytes 557088 | tf_op jit(solution)/shard_map/ppermute | solution.py:314
  78.0 2.2 %shard_map.56 = (f32[136,128]{1,0:T(8,128)S(1)}, f32[5,128,128]{2,1,0:T(8,128)S(1)}) custom-call(s32[2]{0:T(128)S(1)} %pad_add_fusion.side, f32[4,272,128]{2,1,0:T(8,128)S(1)} %collective-permute-done.1.near_ref, f32[4,272,128]{2,1,0:T(8,128)S(1)} %bitcast.9, f32[136,384]{1,0:T(8,128)S(1)} %shard_map.55.some_ref, f32[2048,128]{1,0:T(8,128)S(1)} %shard_map.50.mine, ...), custom_call_target="tpu_custom_call" | custom-call | tf_op jit(solution)/shard_map/pallas_call | solution.py:32
  80.2 1.9 %collective-permute-start.2 = (f32[136,128]{1,0:T(8,128)S(1)}, f32[136,128]{1,0:T(8,128)S(1)}, u32[]{:S(2)}, u32[]{:S(2)}) collective-permute-start(f32[136,128]{1,0:T(8,128)S(1)} %get-tuple-element.7), channel_id=1, source_target_pairs={{0,1},{1,0},{2,3},{3,2},{4,5},{5,4},{6,7},{7,6},{8,9},{9,8},{10,11... | collective-permute-start | bytes 208904 | tf_op jit(solution)/shard_map/ppermute | solution.py:322
  82.1 0.5 shard_map.57.a_ref
  82.6 0.8 collective-permute-done.2.b_ref
  83.4 19.5 %all_to_all.16.in_ref = f32[32,8,128]{2,1,0:T(8,128)S(1)} all-to-all(f32[32,8,128]{2,1,0:T(8,128)S(1)} %shard_map.58), channel_id=1, replica_groups={{0,16,32,48,64,80,96,112,128,144,160,176,192,208,224,240,256,272,288,30..., dimensions={0} | all-to-all | bytes 262144 | tf_op jit(solution)/shard_map/all_to_all | solution.py:325
  103.0 14.0 %all_to_all.17.in_ref = f32[32,8,128]{2,1,0:T(8,128)S(1)} all-to-all(f32[32,8,128]{2,1,0:T(8,128)S(1)} %shard_map.59), channel_id=1, replica_groups={{0,16,32,48,64,80,96,112,128,144,160,176,192,208,224,240,256,272,288,30..., dimensions={0} | all-to-all | bytes 262144 | tf_op jit(solution)/shard_map/all_to_all | solution.py:327
  116.9 0.6 shard_map.60
  (2 shorter events, 0.1 us)
Async XLA Ops:
  2.0 4.7 %collective-permute-start = (f32[2184,128]{1,0:T(8,128)S(1)}, f32[2184,128]{1,0:T(8,128)S(1)}, u32[]{:S(2)}, u32[]{:S(2)}) collective-permute-start(f32[2184,128]{1,0:T(8,128)S(1)} %shard_map.52), channel_id=1, source_target_pairs={{0,1},{1,0},{2,3},{3,2},{4,5},{5,4},{6,7},{7,6},{8,9},{9,8},{10,11... | collective-permute-start | bytes 3354632 | tf_op jit(solution)/shard_map/ppermute | solution.py:306
  3.9 1.4 %copy-start = (f32[128,128]{1,0:T(8,128)S(1)}, f32[128,128]{1,0:T(8,128)}, u32[]{:S(2)}) copy-start(f32[128,128]{1,0:T(8,128)} %loading_ref.5) | copy-start | bytes 196612
  3.9 1.4 %copy-start.1 = (f32[128]{0:T(128)S(1)}, f32[128]{0:T(128)}, u32[]{:S(2)}) copy-start(f32[128]{0:T(128)} %param.4) | copy-start | bytes 1540
  66.6 11.4 %collective-permute-start.1 = (f32[4,272,128]{2,1,0:T(8,128)S(1)}, f32[4,272,128]{2,1,0:T(8,128)S(1)}, u32[]{:S(2)}, u32[]{:S(2)}) collective-permute-start(f32[4,272,128]{2,1,0:T(8,128)S(1)} %bitcast.7), channel_id=1, source_target_pairs={{0,2},{1,15},{2,0},{3,5},{4,6},{5,3},{6,4},{7,9},{8,10},{9,7},{10,... | collective-permute-start | bytes 1671176 | tf_op jit(solution)/shard_map/ppermute | solution.py:314
  80.2 3.2 %collective-permute-start.2 = (f32[136,128]{1,0:T(8,128)S(1)}, f32[136,128]{1,0:T(8,128)S(1)}, u32[]{:S(2)}, u32[]{:S(2)}) collective-permute-start(f32[136,128]{1,0:T(8,128)S(1)} %get-tuple-element.7), channel_id=1, source_target_pairs={{0,1},{1,0},{2,3},{3,2},{4,5},{5,4},{6,7},{7,6},{8,9},{9,8},{10,11... | collective-permute-start | bytes 208904 | tf_op jit(solution)/shard_map/ppermute | solution.py:322

commit v14 on v11

--- a/solution.py
+++ b/solution.py
@@ -291,9 +291,9 @@
     rings4 = [ring[k::2] for ring in rings for k in range(2)]
     plane = lax.axis_size(WIDE)
     planes = [
-        [2 * (PARTS * (step * k % plane) + z) + c for k in range(plane)]
+        [2 * (PARTS * p + z) + c for p in (reversed(range(plane)) if c else range(plane))]
         for z in range(PARTS)
-        for c, step in ((0, 11), (1, plane - 11))
+        for c in range(2)
     ]
 
     half = counts.shape[0] // 2

time: 116 us -> 116 us (level)
  the two profiles are of different devices: /device:TPU:2 before, /device:TPU:8 now
where the time goes in v14:
time: 116 us
  blocking collectives  90.9 us (78%)
  Pallas kernels  9.42 us (8%)
  waiting for transfers between devices  8.65 us (7%)
  starting transfers between devices  6.21 us (5%)
    all_to_all x1, blocking collectives, on_device(): gathered = lax.all_to_all(partial, DEEP, 0, 0, axis_index_groups=rings)  40.6 us
    all_to_all x2, blocking collectives, on_device(): pieces = lax.all_to_all(pieces, AXES, 0, 0, axis_index_groups=planes)  33.5 us
    all_gather x1, blocking collectives, on_device(): scores = lax.all_gather(own, DEEP, axis=0, axis_index_groups=rings4)  16.8 us
    ppermute x1, waiting for transfers between devices, on_device(): near = lax.ppermute(scores, DEEP, near_pairs)  7.74 us
    pallas_call x9, Pallas kernels, call(): pl.pallas_call(body, out_shape=out_shape, in_specs=[pl.BlockSpec(memory_s...  6.69 us
    pallas_call x2, Pallas kernels, cut(): pl.pallas_call(body, out_shape=whole(height, width), in_specs=[pl.BlockSp...  2.73 us
    ppermute x1, starting transfers between devices, on_device(): near = lax.ppermute(scores, DEEP, near_pairs)  2.37 us
  transfers between devices with their start and end apart: 3, of which 3 were waited for; matrix products, arithmetic and copies ran while one was open for 0% of the time, Pallas kernels for 4%

profile of v14, /device:TPU:8, one launch (start us, length us, event | category | flops | bytes accessed | tf_op | source)
XLA Modules:
  0.0 115.9 jit_solution(14842006976690120705)
XLA Ops:
  0.6 1.3 %shard_map.52 = f32[2184,128]{1,0:T(8,128)S(1)} custom-call(s32[1]{0:T(128)} %bitcast.3.which, f32[4096,128]{1,0:T(8,128)} %counts_ref.3, f32[128,128]{1,0:T(8,128)} %loading_ref.5, f32[1,128]{1,0:T(1,128)} %bitcast.9), custom_call_target="tpu_custom_call" | custom-call | tf_op jit(solution)/shard_map/pallas_call | solution.py:75
  2.0 1.9 %collective-permute-start = (f32[2184,128]{1,0:T(8,128)S(1)}, f32[2184,128]{1,0:T(8,128)S(1)}, u32[]{:S(2)}, u32[]{:S(2)}) collective-permute-start(f32[2184,128]{1,0:T(8,128)S(1)} %shard_map.52), channel_id=1, source_target_pairs={{0,1},{1,0},{2,3},{3,2},{4,5},{5,4},{6,7},{7,6},{8,9},{9,8},{10,11... | collective-permute-start | bytes 3354632 | tf_op jit(solution)/shard_map/ppermute | solution.py:302
  3.9 0.0 copy-start
  3.9 0.0 copy-start.1
  3.9 1.4 %shard_map.50.mine = f32[2048,128]{1,0:T(8,128)S(1)} custom-call(s32[1]{0:T(128)} %bitcast.1.which, f32[4096,128]{1,0:T(8,128)} %counts_ref.3), custom_call_target="tpu_custom_call" | custom-call | tf_op jit(solution)/shard_map/pallas_call | solution.py:75
  5.3 0.0 copy-done
  5.3 0.0 copy-done.1
  5.3 1.1 shard_map.51.in_ref
  6.5 0.1 collective-permute-done.other
  6.6 1.1 shard_map.53
  7.8 40.6 %all_to_all.15.in_ref = f32[8,272,128]{2,1,0:T(8,128)S(1)} all-to-all(f32[8,272,128]{2,1,0:T(8,128)S(1)} %shard_map.53), channel_id=1, replica_groups={{0,6,12,2,8,14,4,10},{1,11,5,15,9,3,13,7},{16,22,28,18,24,30,20,26},{17..., dimensions={0} | all-to-all | bytes 2228224 | tf_op jit(solution)/shard_map/all_to_all | solution.py:307
  48.4 0.3 shard_map.54
  48.7 16.8 %all-gather = f32[1088,128]{1,0:T(8,128)S(1)} all-gather(f32[272,128]{1,0:T(8,128)S(1)} %shard_map.54), channel_id=2, replica_groups={{0,12,8,4},{6,2,14,10},{1,5,9,13},{11,15,3,7},{16,28,24,20},{22,18,30,2..., dimensions={0}, use_global_device_ids=true | all-gather | bytes 696320 | tf_op jit(solution)/shard_map/all_gather | solution.py:309
  65.5 2.4 %collective-permute-start.1 = (f32[4,272,128]{2,1,0:T(8,128)S(1)}, f32[4,272,128]{2,1,0:T(8,128)S(1)}, u32[]{:S(2)}, u32[]{:S(2)}) collective-permute-start(f32[4,272,128]{2,1,0:T(8,128)S(1)} %bitcast.6), channel_id=1, source_target_pairs={{0,2},{1,15},{2,0},{3,5},{4,6},{5,3},{6,4},{7,9},{8,10},{9,7},{10,... | collective-permute-start | bytes 1671176 | tf_op jit(solution)/shard_map/ppermute | solution.py:310
  67.9 1.3 %shard_map.55.some_ref = f32[136,384]{1,0:T(8,128)S(1)} custom-call(s32[1]{0:T(128)} %bitcast.side, f32[4,272,128]{2,1,0:T(8,128)S(1)} %bitcast.7, f32[2048,128]{1,0:T(8,128)S(1)} %shard_map.50.mine, f32[2184,128]{1,0:T(8,128)S(1)} %collective-permute-done.other, f32[1,128]{1,0:T(1,128)S(1)} %bitcast.11), custom_call_target="tpu_custom_call" | custom-call | tf_op jit(solution)/shard_map/pallas_call | solution.py:32
  69.2 7.7 %collective-permute-done.1.near_ref = f32[4,272,128]{2,1,0:T(8,128)S(1)} collective-permute-done((f32[4,272,128]{2,1,0:T(8,128)S(1)}, f32[4,272,128]{2,1,0:T(8,128)S(1)}, u32[]{:S(2)}, u32[]{:S(2)}) %collective-permute-start.1) | collective-permute-done | bytes 557088 | tf_op jit(solution)/shard_map/ppermute | solution.py:310
  76.9 1.6 %shard_map.56 = (f32[136,128]{1,0:T(8,128)S(1)}, f32[5,128,128]{2,1,0:T(8,128)S(1)}) custom-call(s32[1]{0:T(128)} %bitcast.side, f32[4,272,128]{2,1,0:T(8,128)S(1)} %collective-permute-done.1.near_ref, f32[4,272,128]{2,1,0:T(8,128)S(1)} %bitcast.8, f32[136,384]{1,0:T(8,128)S(1)} %shard_map.55.some_ref, f32[2048,128]{1,0:T(8,128)S(1)} %shard_map.50.mine, ...), custom_call_target="tpu_custom_call" | custom-call | tf_op jit(solution)/shard_map/pallas_call | solution.py:32
  78.5 1.9 %collective-permute-start.2 = (f32[136,128]{1,0:T(8,128)S(1)}, f32[136,128]{1,0:T(8,128)S(1)}, u32[]{:S(2)}, u32[]{:S(2)}) collective-permute-start(f32[136,128]{1,0:T(8,128)S(1)} %get-tuple-element.7), channel_id=1, source_target_pairs={{0,1},{1,0},{2,3},{3,2},{4,5},{5,4},{6,7},{7,6},{8,9},{9,8},{10,11... | collective-permute-start | bytes 208904 | tf_op jit(solution)/shard_map/ppermute | solution.py:318
  80.5 0.5 shard_map.57.a_ref
  80.9 0.8 collective-permute-done.2.b_ref
  81.7 19.5 %all_to_all.16.in_ref = f32[32,8,128]{2,1,0:T(8,128)S(1)} all-to-all(f32[32,8,128]{2,1,0:T(8,128)S(1)} %shard_map.58), channel_id=1, replica_groups={{0,16,32,48,64,80,96,112,128,144,160,176,192,208,224,240,256,272,288,30..., dimensions={0} | all-to-all | bytes 262144 | tf_op jit(solution)/shard_map/all_to_all | solution.py:321
  101.3 14.0 %all_to_all.17.in_ref = f32[32,8,128]{2,1,0:T(8,128)S(1)} all-to-all(f32[32,8,128]{2,1,0:T(8,128)S(1)} %shard_map.59), channel_id=1, replica_groups={{0,16,32,48,64,80,96,112,128,144,160,176,192,208,224,240,256,272,288,30..., dimensions={0} | all-to-all | bytes 262144 | tf_op jit(solution)/shard_map/all_to_all | solution.py:323
  115.3 0.6 shard_map.60
  (2 shorter events, 0.1 us)
Async XLA Ops:
  2.0 4.7 %collective-permute-start = (f32[2184,128]{1,0:T(8,128)S(1)}, f32[2184,128]{1,0:T(8,128)S(1)}, u32[]{:S(2)}, u32[]{:S(2)}) collective-permute-start(f32[2184,128]{1,0:T(8,128)S(1)} %shard_map.52), channel_id=1, source_target_pairs={{0,1},{1,0},{2,3},{3,2},{4,5},{5,4},{6,7},{7,6},{8,9},{9,8},{10,11... | collective-permute-start | bytes 3354632 | tf_op jit(solution)/shard_map/ppermute | solution.py:302
  3.9 1.4 %copy-start = (f32[128,128]{1,0:T(8,128)S(1)}, f32[128,128]{1,0:T(8,128)}, u32[]{:S(2)}) copy-start(f32[128,128]{1,0:T(8,128)} %loading_ref.5) | copy-start | bytes 196612
  3.9 1.4 %copy-start.1 = (f32[128]{0:T(128)S(1)}, f32[128]{0:T(128)}, u32[]{:S(2)}) copy-start(f32[128]{0:T(128)} %param.4) | copy-start | bytes 1540
  65.5 11.4 %collective-permute-start.1 = (f32[4,272,128]{2,1,0:T(8,128)S(1)}, f32[4,272,128]{2,1,0:T(8,128)S(1)}, u32[]{:S(2)}, u32[]{:S(2)}) collective-permute-start(f32[4,272,128]{2,1,0:T(8,128)S(1)} %bitcast.6), channel_id=1, source_target_pairs={{0,2},{1,15},{2,0},{3,5},{4,6},{5,3},{6,4},{7,9},{8,10},{9,7},{10,... | collective-permute-start | bytes 1671176 | tf_op jit(solution)/shard_map/ppermute | solution.py:310
  78.5 3.2 %collective-permute-start.2 = (f32[136,128]{1,0:T(8,128)S(1)}, f32[136,128]{1,0:T(8,128)S(1)}, u32[]{:S(2)}, u32[]{:S(2)}) collective-permute-start(f32[136,128]{1,0:T(8,128)S(1)} %get-tuple-element.7), channel_id=1, source_target_pairs={{0,1},{1,0},{2,3},{3,2},{4,5},{5,4},{6,7},{7,6},{8,9},{9,8},{10,11... | collective-permute-start | bytes 208904 | tf_op jit(solution)/shard_map/ppermute | solution.py:318
